TPU v7x, 128 devices: a whole 4x4x4 slice. The times are simulated.
128 devices in a mesh: section: 4 (over y), space: 32 (over z, x, core).
Axes of the slice: x: 4, y: 4, z: 4, core: 2. Of those that a mesh axis runs over, the one named last changes fastest.
Arguments:
- features: bfloat16 [4, 256, 512, 96], P('section', 'space'), may hold values from -6 to 6
- occupancy: int32 [4, 256, 512], P('section', 'space'), may hold values 0 or 1
- neighbors: int32 [6, 256], P(None, 'space'), may hold values from -1 to 255, as said below
- routes: int32 [4, 16384, 1], P('section', 'space'), may hold values from 0 to 63; in each aligned block of 512 rows (0 to 511, 512 to 1023, ..., all dimensions but the last counted through in order) at most 16 rows name the same one
- cotangent: float32 [4, 64, 8, 192], P('section', 'space'), may hold values from -6 to 6
- conv_weight: bfloat16 [2592, 192], replicated, may hold values from -0.125 to 0.125
- conv_bias: float32 [192], replicated, may hold values from -3 to 3
- key_weight: float32 [192, 192], replicated, may hold values from -0.4375 to 0.4375
- value_weight: float32 [192, 192], replicated, may hold values from -0.4375 to 0.4375
- queries: float32 [8, 192], replicated, may hold values from -6 to 6
Outputs:
- pooled: float32 [4, 64, 8, 192], P('section', 'space')
- d_features: bfloat16 [4, 256, 512, 96], P('section', 'space')
- d_conv_weight: float32 [2592, 192], replicated
- d_conv_bias: float32 [192], replicated
- d_key_weight: float32 [192, 192], replicated
- d_value_weight: float32 [192, 192], replicated
- d_queries: float32 [8, 192], replicated
Inputs may be any that keep to these rules, and one draw needn't show every extreme that they name: `neighbors`: blocks sit on a map of 8 x 4 tiles, one tile of 2 x 2 x 2 blocks (x, y, z) on each index d of space, tile (d % 8, d // 8). The block beside a block along x lies on the same index or on the next one, along y on the same index or 8 indices away, along z on the same index. Rows 0 to 2 and 3 to 5 are mutual: if the +x block of s is t then the -x block of t is s. `routes`: among one index's rows of one scene, at most 16 name one group, and some group has exactly 16.
All inputs are finite; a program needn't handle non-finite values. No bound on the sum of `occupancy` on one device may be relied on, other than what follows from the above.
Results may differ from a plain program's by a relative error of at most 0.0075.
Values may be sent and summed in bfloat16 or wider, within the bound.
No kernel may reach another device: no remote copies, remote signals or barrier semaphores. Data moves between devices by JAX's collectives and lax.ppermute only.
A program may use at most 128 MiB of HBM per device.

v0:
```python
import jax
import jax.numpy as jnp
from jax import lax
from jax.sharding import PartitionSpec as P

TILES_Y = 4


EPS = 1e-06
TEMPER = 8.0


def passed_along(shard, axis, by):
    peers = lax.axis_size(axis)
    pairs = [(i, i + by) for i in range(peers) if 0 <= i + by < peers]
    return lax.ppermute(shard, axis, pairs)


def paired_grid(blocks):
    amount = blocks.shape[0]
    channels = blocks.shape[-1]
    volume = blocks.reshape(amount, 8, 8, 8, channels)
    padded = jnp.pad(volume, ((0, 0), (1, 3), (1, 3), (1, 3), (0, 0)))
    return padded.reshape(amount, 6, 2, 6, 2, 6, 2, channels)


def tap_window(grid, offset_x, offset_y, offset_z):
    start_x = offset_x // 2
    start_y = offset_y // 2
    start_z = offset_z // 2
    return grid[
        :,
        start_x : start_x + 5,
        offset_x % 2,
        start_y : start_y + 5,
        offset_y % 2,
        start_z : start_z + 5,
        offset_z % 2,
        :,
    ]


def tap_list():
    listing = []
    for offset_x in range(3):
        for offset_y in range(3):
            for offset_z in range(3):
                listing.append((offset_x, offset_y, offset_z))
    return listing


def pull(plane, remote, source, here):
    amount = plane.shape[0]
    present = source >= 0
    owner = jnp.where(present, source // amount, -1)
    place = jnp.where(present, source % amount, 0)
    shaped = (-1,) + (1,) * (plane.ndim - 1)
    near = (present & (owner == here)).reshape(shaped)
    result = jnp.where(near, plane[place], 0.0)
    if remote is None:
        return result
    distant = (present & (owner != here)).reshape(shaped)
    return result + jnp.where(distant, remote[place], 0.0)


def head_terms(inputs, key_weight, value_weight, queries):
    highest = lax.Precision.HIGHEST
    key_rows = jnp.dot(inputs, key_weight, precision=highest)
    value_rows = jnp.dot(inputs, value_weight, precision=highest)
    key_unit = key_rows * lax.rsqrt(jnp.sum(key_rows * key_rows, axis=-1, keepdims=True) + EPS)
    query_unit = queries * lax.rsqrt(jnp.sum(queries * queries, axis=-1, keepdims=True) + EPS)
    weights = jnp.exp(TEMPER * jnp.dot(key_unit, query_unit.T, precision=highest))
    return (weights, value_rows)


def on_device(
    features,
    occupancy,
    neighbors,
    routes,
    cotangent,
    conv_weight,
    conv_bias,
    key_weight,
    value_weight,
    queries,
):
    highest = lax.Precision.HIGHEST
    here = lax.axis_index("space")
    devices = lax.axis_size("space")
    tiles_x = devices // TILES_Y
    occupied = occupancy[0][..., None] > 0
    masked = jnp.where(occupied, features[0], jnp.zeros_like(features[0]))
    channels = masked.shape[-1]
    blocks_here = masked.shape[0]
    width = conv_weight.shape[1]
    grid = paired_grid(masked)
    taps = tap_list()
    partial_value = jnp.zeros((blocks_here, 5, 5, 5, width), jnp.float32)
    for number, (offset_x, offset_y, offset_z) in enumerate(taps):
        window = tap_window(grid, offset_x, offset_y, offset_z)
        tap_weight = conv_weight[number * channels : (number + 1) * channels]
        partial_value = partial_value + jnp.einsum(
            "bxyzi,ic->bxyzc", window, tap_weight, preferred_element_type=jnp.float32
        )
    lower = neighbors[3:6]
    upper = neighbors[0:3]
    plane_x = partial_value[:, 4]
    from_x = passed_along(plane_x.astype(jnp.bfloat16), "space", 1).astype(plane_x.dtype)
    extra_in_x = pull(plane_x, from_x, lower[0], here)
    across_x = partial_value[:, 0:4].at[:, 0].add(extra_in_x)
    plane_y = across_x[:, :, 4]
    from_y = passed_along(plane_y.astype(jnp.bfloat16), "space", tiles_x).astype(plane_y.dtype)
    extra_in_y = pull(plane_y, from_y, lower[1], here)
    across_y = across_x[:, :, 0:4].at[:, :, 0].add(extra_in_y)
    plane_z = across_y[:, :, :, 4]
    across_z = across_y[:, :, :, 0:4].at[:, :, :, 0].add(pull(plane_z, None, lower[2], here))
    before = across_z.reshape(blocks_here * 64, width) + conv_bias
    hidden = lax.optimization_barrier(jax.nn.gelu(before).astype(jnp.bfloat16))
    rows_here = hidden.shape[0]
    groups = cotangent.shape[1] * devices
    destination = routes[0, :, 0]
    member_int = (destination[:, None] == jnp.arange(groups, dtype=jnp.int32)[None, :]).astype(
        jnp.int32
    )
    capacity = 2 * rows_here // groups
    rank = jnp.sum((jnp.cumsum(member_int, axis=0) - 1) * member_int, axis=1)
    position = destination * capacity + rank
    buffer = jnp.zeros((groups * capacity, width), jnp.bfloat16).at[position].set(hidden)
    filled = jnp.zeros((groups * capacity,), jnp.bfloat16).at[position].set(1.0)
    arrived, arrived_flag = (
        lax.all_to_all(
            buffer.reshape(groups, capacity, width),
            "space",
            split_axis=0,
            concat_axis=1,
            tiled=True,
        ),
        lax.all_to_all(
            filled.reshape(groups, capacity), "space", split_axis=0, concat_axis=1, tiled=True
        ),
    )
    flag_column = arrived_flag.reshape(-1, 1).astype(jnp.float32)

    def owned(inputs, key_w, value_w, query_w):
        local_groups = inputs.shape[0]
        weights, value_rows = head_terms(inputs.reshape(-1, width), key_w, value_w, query_w)
        weights = (weights * flag_column).reshape(local_groups, -1, weights.shape[-1])
        value_rows = value_rows.reshape(local_groups, -1, width)
        numerator = jnp.einsum("gmq,gmc->gqc", weights, value_rows, precision=highest)
        mass_sum = jnp.sum(weights, axis=1)
        return numerator / (1.0 + mass_sum)[:, :, None]

    pooled, owned_back = jax.vjp(
        owned, arrived.astype(jnp.float32), key_weight, value_weight, queries
    )
    d_arrived, d_key, d_value, d_query = owned_back(cotangent[0])
    returned = lax.all_to_all(d_arrived, "space", split_axis=1, concat_axis=0, tiled=True)
    d_hidden = returned.reshape(groups * capacity, width)[position]
    _, gelu_back = jax.vjp(jax.nn.gelu, before)
    d_before = gelu_back(d_hidden)[0]
    d_bias = jnp.sum(d_before, axis=0)
    back_z = d_before.reshape(blocks_here, 4, 4, 4, width)
    extra_z = pull(back_z[:, :, :, 0], None, upper[2], here)
    back_y_in = jnp.concatenate([back_z, extra_z[:, :, :, None]], axis=3)
    edge_y = back_y_in[:, :, 0]
    from_up_y = passed_along(edge_y.astype(jnp.bfloat16), "space", -tiles_x).astype(edge_y.dtype)
    extra_y = pull(edge_y, from_up_y, upper[1], here)
    back_x_in = jnp.concatenate([back_y_in, extra_y[:, :, None]], axis=2)
    edge_x = back_x_in[:, 0]
    from_up_x = passed_along(edge_x.astype(jnp.bfloat16), "space", -1).astype(edge_x.dtype)
    extra_x = pull(edge_x, from_up_x, upper[0], here)
    d_partial = jnp.concatenate([back_x_in, extra_x[:, None]], axis=1).astype(jnp.bfloat16)
    weight_rows = []
    d_grid = jnp.zeros((blocks_here, 6, 2, 6, 2, 6, 2, channels), jnp.float32)
    for number, (offset_x, offset_y, offset_z) in enumerate(taps):
        window = tap_window(grid, offset_x, offset_y, offset_z)
        tap_weight = conv_weight[number * channels : (number + 1) * channels]
        weight_rows.append(
            jnp.einsum("bxyzi,bxyzc->ic", window, d_partial, preferred_element_type=jnp.float32)
        )
        d_window = jnp.einsum(
            "bxyzc,ic->bxyzi", d_partial, tap_weight, preferred_element_type=jnp.float32
        )
        start_x = offset_x // 2
        start_y = offset_y // 2
        start_z = offset_z // 2
        d_grid = d_grid.at[
            :,
            start_x : start_x + 5,
            offset_x % 2,
            start_y : start_y + 5,
            offset_y % 2,
            start_z : start_z + 5,
            offset_z % 2,
            :,
        ].add(d_window)
    d_weight = jnp.concatenate(weight_rows, axis=0)
    d_volume = d_grid.reshape(blocks_here, 12, 12, 12, channels)[:, 1:9, 1:9, 1:9, :]
    d_masked = d_volume.reshape(blocks_here, 512, channels)
    d_features = jnp.where(occupied, d_masked, 0.0).astype(jnp.bfloat16)
    d_weight, d_bias, d_key, d_value, d_query = lax.psum(
        (d_weight, d_bias, d_key, d_value, d_query), ("section", "space")
    )
    return (pooled[None], d_features[None], d_weight, d_bias, d_key, d_value, d_query)


def solution(mesh):
    in_specs = (
        P("section", "space", None, None),
        P("section", "space", None),
        P(None, "space"),
        P("section", "space", None),
        P("section", "space", None, None),
        P(),
        P(),
        P(),
        P(),
        P(),
    )
    out_specs = (
        P("section", "space", None, None),
        P("section", "space", None, None),
        P(),
        P(),
        P(),
        P(),
        P(),
    )
    return jax.shard_map(
        on_device, mesh=mesh, in_specs=in_specs, out_specs=out_specs, check_vma=False
    )
```

profile of v0, /device:TPU:1, one launch (start us, length us, event | category | flops | bytes accessed | tf_op | source)
XLA Modules:
  0.0 435.8 jit_solution(17150741527667376381)
XLA Ops:
  22.6 5.0 %collective-permute-start = (bf16[8,5,5,192]{3,0,2,1:T(8,128)(2,1)S(1)}, bf16[8,5,5,192]{3,0,2,1:T(8,128)(2,1)S(1)}, u32[]{:S(2)}, u32[]{:S(2)}) collective-permute-start(bf16[8,5,5,192]{3,0,2,1:T(8,128)(2,1)S(1)} %fusion.252), channel_id=1, source_target_pairs={{0,1},{1,2},{2,3},{3,4},{4,5},{5,6},{6,7},{7,8},{8,9},{9,10},{10,1... | collective-permute-start | bytes 230408 | tf_op jit(solution)/shard_map/ppermute | solution.py:16
  29.3 3.8 scatter_custom_fusion.1
  33.8 7.7 %all-to-all-start.1 = ((bf16[32,2,16]{2,1,0:T(2,128)(2,1)}), bf16[32,2,16]{2,1,0:T(2,128)(2,1)S(1)}, u32[]{:S(2)}, u32[]{:S(2)}) async-start(bf16[32,2,16]{2,1,0:T(2,128)(2,1)} %all_to_all.35), calls=%async_computation.1 | async-start | bytes 32768 | tf_op jit(solution)/shard_map/all_to_all | solution.py:139
  43.4 3.3 collective-permute-start.1
  50.5 3.1 scatter_custom_fusion
  53.7 9.3 %all-to-all-start = ((bf16[64,16,192]{2,1,0:T(8,128)(2,1)}), bf16[64,16,192]{2,1,0:T(8,128)(2,1)S(1)}, u32[]{:S(2)}, u32[]{:S(2)}) async-start(bf16[64,16,192]{2,1,0:T(8,128)(2,1)} %bitcast.106), calls=%async_computation | async-start | bytes 1048576 | tf_op jit(solution)/shard_map/all_to_all | solution.py:132
  63.1 11.3 %all-to-all-done = bf16[64,16,192]{2,1,0:T(8,128)(2,1)S(1)} async-done(((bf16[64,16,192]{2,1,0:T(8,128)(2,1)}), bf16[64,16,192]{2,1,0:T(8,128)(2,1)S(1)}, u32[]{:S(2)}, u32[]{:S(2)}) %all-to-all-start) | async-done | bytes 393248 | tf_op jit(solution)/shard_map/all_to_all | solution.py:132
  83.9 2.7 reshape.2616
  86.6 3.5 copy.219
  90.1 4.7 %all-to-all-start.2 = ((f32[2,512,192]{2,0,1:T(2,128)}), f32[2,512,192]{2,0,1:T(2,128)}, u32[]{:S(2)}, u32[]{:S(2)}) async-start(f32[2,512,192]{2,0,1:T(2,128)} %copy.219), calls=%async_computation.2 | async-start | bytes 2097152 | tf_op jit(solution)/shard_map/all_to_all | solution.py:158
  97.7 14.5 %all-to-all-done.2 = f32[2,512,192]{2,0,1:T(2,128)} async-done(((f32[2,512,192]{2,0,1:T(2,128)}), f32[2,512,192]{2,0,1:T(2,128)}, u32[]{:S(2)}, u32[]{:S(2)}) %all-to-all-start.2) | async-done | bytes 786464 | tf_op jit(solution)/shard_map/all_to_all | solution.py:158
  118.8 65.2 %all-reduce.2 = (f32[192]{0:T(256)}, f32[8,192]{1,0:T(8,128)}) all-reduce(f32[192]{0:T(256)S(1)} %get-tuple-element.393, f32[8,192]{1,0:T(8,128)S(1)} %add_add_fusion.3), channel_id=1, replica_groups=mesh['section'=4,'space'=32] {'section','space'}, use_global_device_ids=true, to_apply=%region_12.13 | all-reduce | flops 1728 | bytes 13824 | tf_op jit(solution)/shard_map/psum | solution.py:202
  184.9 3.1 collective-permute-start.3
  188.7 2.3 collective-permute-done.3
  219.3 3.7 scatter-add.105
  230.8 2.2 fusion.8
  250.8 2.3 fusion.26
  259.6 2.5 fusion.34
  271.0 2.2 fusion.44
  275.4 2.3 fusion.48
  277.7 2.2 fusion.50
  279.9 3.9 copy.234
  286.2 137.7 %all-reduce.6.cloned.1.call-done = (f32[2592,192]{1,0:T(8,128)}, f32[192,192]{1,0:T(8,128)}, f32[192,192]{1,0:T(8,128)}) async-done(((f32[2592,192]{1,0:T(8,128)}, f32[192,192]{1,0:T(8,128)}, f32[192,192]{1,0:T(8,128)}), (f32[2592,192]{1,0:T(8,128)}, f32[192,192]{1,0:T(8,128)}, f32[192,192]{1,0:T(8,128)})) %all-reduce.6.cloned.1.call-update) | async-done | bytes 2285584 | tf_op jit(solution)/shard_map/psum | solution.py:202
  423.9 3.2 copy.237
  (223 shorter events, 118.4 us)
Async XLA Ops:
  7.2 67.3 %copy-start = (f32[192,192]{1,0:T(8,128)S(1)}, f32[192,192]{1,0:T(8,128)}, u32[]{:S(2)}) copy-start(f32[192,192]{1,0:T(8,128)} %param.77) | copy-start | bytes 442372
  10.5 1.9 copy-start.4
  12.4 9.8 %copy-start.2 = (bf16[8,12,12,12,96]{4,0,3,2,1:T(8,128)(2,1)}, bf16[8,12,12,12,96]{4,0,3,2,1:T(8,128)(2,1)S(1)}, u32[]{:S(2)}) copy-start(bf16[8,12,12,12,96]{4,0,3,2,1:T(8,128)(2,1)S(1)} %pad.119.clone) | copy-start | bytes 7962628
  21.4 6.2 %copy-start.14 = (s32[1,512,1]{1,2,0:T(1,128)S(1)}, s32[1,512,1]{1,2,0:T(1,128)}, u32[]{:S(2)}) copy-start(s32[1,512,1]{1,2,0:T(1,128)} %param.73) | copy-start | bytes 6148
  21.7 19.9 %copy-start.13 = (s32[1,8,512]{2,1,0:T(8,128)S(1)}, s32[1,8,512]{2,1,0:T(8,128)}, u32[]{:S(2)}) copy-start(s32[1,8,512]{2,1,0:T(8,128)} %param.71) | copy-start | bytes 49156
  21.7 19.9 %copy-start.15 = (s32[6,8]{1,0:T(8,128)S(1)}, s32[6,8]{1,0:T(8,128)}, u32[]{:S(2)}) copy-start(s32[6,8]{1,0:T(8,128)} %param.72) | copy-start | bytes 580
  22.2 19.7 %copy-start.9 = (f32[8,192]{1,0:T(8,128)S(1)}, f32[8,192]{1,0:T(8,128)}, u32[]{:S(2)}) copy-start(f32[8,192]{1,0:T(8,128)} %param.79) | copy-start | bytes 18436
  22.6 20.0 %collective-permute-start = (bf16[8,5,5,192]{3,0,2,1:T(8,128)(2,1)S(1)}, bf16[8,5,5,192]{3,0,2,1:T(8,128)(2,1)S(1)}, u32[]{:S(2)}, u32[]{:S(2)}) collective-permute-start(bf16[8,5,5,192]{3,0,2,1:T(8,128)(2,1)S(1)} %fusion.252), channel_id=1, source_target_pairs={{0,1},{1,2},{2,3},{3,4},{4,5},{5,6},{6,7},{7,8},{8,9},{9,10},{10,1... | collective-permute-start | bytes 230408 | tf_op jit(solution)/shard_map/ppermute | solution.py:16
  33.8 19.9 %all-to-all-start.1 = ((bf16[32,2,16]{2,1,0:T(2,128)(2,1)}), bf16[32,2,16]{2,1,0:T(2,128)(2,1)S(1)}, u32[]{:S(2)}, u32[]{:S(2)}) async-start(bf16[32,2,16]{2,1,0:T(2,128)(2,1)} %all_to_all.35), calls=%async_computation.1 | async-start | bytes 32768 | tf_op jit(solution)/shard_map/all_to_all | solution.py:139
  43.4 4.8 %collective-permute-start.1 = (bf16[8,4,5,192]{3,0,2,1:T(8,128)(2,1)S(1)}, bf16[8,4,5,192]{3,0,2,1:T(8,128)(2,1)S(1)}, u32[]{:S(2)}, u32[]{:S(2)}) collective-permute-start(bf16[8,4,5,192]{3,0,2,1:T(8,128)(2,1)S(1)} %fusion.251), channel_id=1, source_target_pairs={{0,8},{1,9},{2,10},{3,11},{4,12},{5,13},{6,14},{7,15},{8,16},{9,17... | collective-permute-start | bytes 184328 | tf_op jit(solution)/shard_map/ppermute | solution.py:16
  46.8 3.5 copy-start.16
  49.9 24.6 %copy-start.6 = (f32[8,4,4,4,192]{4,0,3,2,1:T(8,128)}, f32[8,4,4,4,192]{4,0,3,2,1:T(8,128)S(1)}, u32[]{:S(2)}) copy-start(f32[8,4,4,4,192]{4,0,3,2,1:T(8,128)S(1)} %fusion.114) | copy-start | bytes 1179652
  50.1 25.7 %copy-start.8 = (f32[192,192]{1,0:T(8,128)S(1)}, f32[192,192]{1,0:T(8,128)}, u32[]{:S(2)}) copy-start(f32[192,192]{1,0:T(8,128)} %param.78) | copy-start | bytes 442372
  50.5 26.0 %copy-start.12 = (f32[1,2,8,192]{3,2,1,0:T(8,128)S(1)}, f32[1,2,8,192]{3,2,1,0:T(8,128)}, u32[]{:S(2)}) copy-start(f32[1,2,8,192]{3,2,1,0:T(8,128)} %param.74) | copy-start | bytes 36868
  53.7 20.7 %all-to-all-start = ((bf16[64,16,192]{2,1,0:T(8,128)(2,1)}), bf16[64,16,192]{2,1,0:T(8,128)(2,1)S(1)}, u32[]{:S(2)}, u32[]{:S(2)}) async-start(bf16[64,16,192]{2,1,0:T(8,128)(2,1)} %bitcast.106), calls=%async_computation | async-start | bytes 1048576 | tf_op jit(solution)/shard_map/all_to_all | solution.py:132
  90.1 22.1 %all-to-all-start.2 = ((f32[2,512,192]{2,0,1:T(2,128)}), f32[2,512,192]{2,0,1:T(2,128)}, u32[]{:S(2)}, u32[]{:S(2)}) async-start(f32[2,512,192]{2,0,1:T(2,128)} %copy.219), calls=%async_computation.2 | async-start | bytes 2097152 | tf_op jit(solution)/shard_map/all_to_all | solution.py:158
  94.8 329.1 %all-reduce.6.cloned.1.call-start = ((), (), s32[]{:S(2)}) async-start(), calls=%async_computation.3 | async-start | bytes 6094848 | tf_op jit(solution)/shard_map/psum | solution.py:202
  116.7 67.3 %collective-permute-start.2 = (bf16[8,4,5,192]{3,0,2,1:T(8,128)(2,1)S(1)}, bf16[8,4,5,192]{3,0,2,1:T(8,128)(2,1)S(1)}, u32[]{:S(2)}, u32[]{:S(2)}) collective-permute-start(bf16[8,4,5,192]{3,0,2,1:T(8,128)(2,1)S(1)} %get-tuple-element.399), channel_id=1, source_target_pairs={{8,0},{9,1},{10,2},{11,3},{12,4},{13,5},{14,6},{15,7},{16,8},{17,9... | collective-permute-start | bytes 184328 | tf_op jit(solution)/shard_map/ppermute | solution.py:16
  184.8 9.1 %copy-start.5 = (bf16[2592,192]{0,1:T(8,128)(2,1)S(1)}, bf16[2592,192]{0,1:T(8,128)(2,1)}, u32[]{:S(2)}) copy-start(bf16[2592,192]{0,1:T(8,128)(2,1)} %param.75) | copy-start | bytes 2985988
  184.9 6.1 %collective-permute-start.3 = (bf16[8,5,5,192]{3,0,2,1:T(8,128)(2,1)S(1)}, bf16[8,5,5,192]{3,0,2,1:T(8,128)(2,1)S(1)}, u32[]{:S(2)}, u32[]{:S(2)}) collective-permute-start(bf16[8,5,5,192]{3,0,2,1:T(8,128)(2,1)S(1)} %fusion.253), channel_id=1, source_target_pairs={{1,0},{2,1},{3,2},{4,3},{5,4},{6,5},{7,6},{8,7},{9,8},{10,9},{11,1... | collective-permute-start | bytes 230408 | tf_op jit(solution)/shard_map/ppermute | solution.py:16
  191.6 4.4 %copy-start.3 = (bf16[8,12,12,12,96]{4,0,3,2,1:T(8,128)(2,1)S(1)}, bf16[8,12,12,12,96]{4,0,3,2,1:T(8,128)(2,1)}, u32[]{:S(2)}) copy-start(bf16[8,12,12,12,96]{4,0,3,2,1:T(8,128)(2,1)} %copy-done.2) | copy-start | bytes 7962628
  284.3 144.3 %copy-start.1 = (f32[192,192]{1,0:T(8,128)S(1)}, f32[192,192]{1,0:T(8,128)}, u32[]{:S(2)}) copy-start(f32[192,192]{1,0:T(8,128)} %param.77) | copy-start | bytes 442372
  423.9 3.2 copy-start.11
  423.9 3.9 copy-start.10
  (1 other events, 1.8 us)
Sparse Core Ops, SparseCore 0:
  271.1 152.7 all-reduce.5
where the time goes:
time: 444 us; the launch traced here: 436 us
  waiting for transfers between devices  166 us (37%)
  matrix products  106 us (24%)
  blocking collectives  65.2 us (15%)
  local copies, waits for them, and re-layouts  42.3 us (10%)
  starting transfers between devices  34.5 us (8%)
  between operations  15.6 us (4%)
  other arithmetic  5.63 us (1%)
    psum x1, waiting for transfers between devices, on_device(): lax.psum((d_weight, d_bias, d_key, d_value, d_query), ('section', 'space'))  138 us
    psum x1, blocking collectives, on_device(): lax.psum((d_weight, d_bias, d_key, d_value, d_query), ('section', 'space'))  65.2 us
    dot_general x27, matrix products, on_device(): jnp.einsum('bxyzc,ic->bxyzi', d_partial, tap_weight, preferred_element_ty...  57.2 us
    dot_general x27, matrix products, on_device(): jnp.einsum('bxyzi,bxyzc->ic', window, d_partial, preferred_element_type=j...  27.2 us
    all_to_all x1, waiting for transfers between devices, on_device(): lax.all_to_all(d_arrived, 'space', split_axis=1, concat_axis=0, tiled=True)  14.5 us
    ppermute x4, starting transfers between devices, passed_along(): return lax.ppermute(shard, axis, pairs)  12.7 us
    all_to_all x1, waiting for transfers between devices, on_device(): lax.all_to_all(buffer.reshape(groups, capacity, width), 'space', split_ax...  11.3 us
    dot_general x27, matrix products, on_device(): jnp.einsum('bxyzi,ic->bxyzc', window, tap_weight, preferred_element_type=...  9.9 us
  transfers between devices with their start and end apart: 8, of which 5 were waited for; matrix products, arithmetic and copies ran while one was open for 8% of the time, Pallas kernels for 0%

commit v1 on v0

v1 whole, which is shorter than its diff:
```python
import functools

import jax
import jax.numpy as jnp
from jax import lax
from jax.experimental import pallas as pl
from jax.experimental.pallas import tpu as pltpu
from jax.sharding import Mesh, PartitionSpec as P

EPS = 1e-06
TEMPER = 8.0
CIN, COUT = 96, 192
LANES = 128
SLOTS9 = 9 * LANES
GROUPS, NQ = 64, 8
SHARD = 24
HALF = 64 * SHARD
F32, BF16 = jnp.float32, jnp.bfloat16
SPACE = ("chip", "core")
CHIPS = ("section", "chip")
VMEM_LIMIT = 44 * 1024 * 1024


def params():
    return pltpu.CompilerParams(vmem_limit_bytes=VMEM_LIMIT)


def nn(a, b):
    return lax.dot_general(a, b, (((1,), (0,)), ((), ())), preferred_element_type=F32)


def nt(a, b):
    return lax.dot_general(a, b, (((1,), (1,)), ((), ())), preferred_element_type=F32)


def tn(a, b):
    return lax.dot_general(a, b, (((0,), (0,)), ((), ())), preferred_element_type=F32)


def split(a):
    high = a.astype(BF16)
    return high, (a - high.astype(F32)).astype(BF16)


def find_slots(near_ref, slot_ref):
    here = lax.axis_index("chip") * 2 + lax.axis_index("core")
    for place in range(8):
        slot_ref[place] = 0
    for slot in range(8):
        place = 0
        for axis in range(3):
            beside = near_ref[axis, slot]
            inner = jnp.logical_and(beside >= 0, lax.shift_right_arithmetic(beside, 3) == here)
            place = place + jnp.where(inner, 0, 1 << axis)
        slot_ref[place] = slot


def placed_occupancy(occ_ref, slot_ref):
    rows = [occ_ref[pl.ds(slot_ref[p], 1), :] for p in range(8)]
    return jnp.concatenate(rows, axis=0).astype(F32).T


def place_kernel(near_ref, feat_ref, occ_ref, v_ref, xs_ref, ys_ref, rows_ref, slot_ref):
    find_slots(near_ref, slot_ref)
    occ = placed_occupancy(occ_ref, slot_ref)
    rows_ref[...] = jnp.zeros_like(rows_ref)
    for by in range(2):
        for bx in range(2):
            pair = []
            for bz in range(2):
                place = bx + 2 * by + 4 * bz
                block = feat_ref[slot_ref[place]].astype(F32)
                block = jnp.where(occ[:, place : place + 1] > 0, block, 0.0)
                pair.append(block.reshape(64, 8, CIN))
            rows_ref[:, 0:CIN] = jnp.stack(pair, axis=1).reshape(1024, CIN)
            for pz in range(2):
                part = rows_ref[pl.ds(pz, 512, stride=2), :].reshape(8, 4, 2, 8, LANES)
                for py in range(2):
                    piece = part[:, :, py].reshape(8, 32, LANES).astype(BF16)
                    v_ref[pl.ds(8 * bx, 8), 2 * py + pz, pl.ds(32 * by, 32), :] = piece
            if by == 1:
                edge = [
                    rows_ref[pl.ds(pz, 512, stride=2), :].reshape(8, 8, 8, LANES)[:, 7]
                    for pz in range(2)
                ]
                ys_ref[pl.ds(128 * bx, 128), :] = (
                    jnp.stack(edge, axis=1).reshape(128, LANES).astype(BF16)
                )
    xs_ref[...] = v_ref[15].reshape(256, LANES)


def forward_kernel(
    near_ref, v_ref, xr_ref, yr_ref, xyr_ref, w_ref, bias_ref, key_ref, val_ref, query_ref,
    routes_ref, cot_ref,
    podd_ref, peven_ref, wp_ref, slope_ref, hid_ref, ku_ref, kn_ref, wt_ref, tt_ref, rr_ref,
    send_ref, slot_ref,
):
    find_slots(near_ref, slot_ref)
    wp_ref[...] = jnp.zeros_like(wp_ref)
    for tap in range(27):
        wp_ref[pl.ds(tap * LANES, CIN), :] = w_ref[pl.ds(tap * CIN, CIN), :]
    first = lax.broadcasted_iota(jnp.int32, (64, LANES), 0) % 8 == 0
    for x in range(-1, 16):
        if x < 0:
            planes = xr_ref[...].astype(F32).reshape(4, 64, LANES)
            edge = xyr_ref[...].astype(F32)
        else:
            planes = v_ref[x].astype(F32)
            edge = yr_ref[pl.ds(16 * x, 16), :].astype(F32)
        if x % 2 == 0:
            out_ref, row = peven_ref, 32 * x
        else:
            out_ref, row = podd_ref, 32 * (x + 1)
        for b in range(3):
            for c in range(3):
                py, pz = (b + 1) % 2, (c + 1) % 2
                piece = planes[2 * py + pz]
                if b == 0:
                    piece = jnp.concatenate([edge[8 * pz : 8 * pz + 8], piece[0:56]], axis=0)
                if c == 0:
                    piece = jnp.where(first, 0.0, pltpu.roll(piece, 1, 0))
                column = (3 * b + c) * LANES
                out_ref[pl.ds(row, 64), pl.ds(column, LANES)] = piece.astype(BF16)
    before = (
        nn(podd_ref[0:512, :], wp_ref[0:SLOTS9, :])
        + nn(peven_ref[...], wp_ref[SLOTS9 : 2 * SLOTS9, :])
        + nn(podd_ref[64:576, :], wp_ref[2 * SLOTS9 : 3 * SLOTS9, :])
        + bias_ref[...]
    )
    root = 0.7978845608028654
    square = before * before
    tanh = jnp.tanh(root * before * (1.0 + 0.044715 * square))
    hidden = (0.5 * before * (1.0 + tanh)).astype(BF16)
    slope_ref[...] = 0.5 * (1.0 + tanh) + 0.5 * before * (1.0 - tanh * tanh) * root * (
        1.0 + 3.0 * 0.044715 * square
    )
    hid_ref[...] = hidden

    kh, kl = split(key_ref[...])
    vh, vl = split(val_ref[...])
    keys = nn(hidden, kh) + nn(hidden, kl)
    values = nn(hidden, vh) + nn(hidden, vl)
    key_norm = lax.rsqrt(jnp.sum(keys * keys, axis=-1, keepdims=True) + EPS)
    ku = keys * key_norm
    ku_ref[...] = ku
    kn_ref[...] = key_norm
    queries = query_ref[...]
    qu = queries * lax.rsqrt(jnp.sum(queries * queries, axis=-1, keepdims=True) + EPS)
    uh, ul = split(ku)
    qh, ql = split(qu)
    weights = jnp.exp(TEMPER * (nt(qh, uh) + nt(ql, uh) + nt(qh, ul)))
    wt_ref[...] = weights

    routes = jnp.concatenate(
        [routes_ref[pl.ds(slot_ref[p], 1), :] for p in range(8)], axis=0
    ).astype(BF16)
    row = lax.broadcasted_iota(jnp.int32, (64, 512), 1)
    inside = ((row >> 6) & 3) * 16 + ((row >> 3) & 3) * 4 + (row & 3)
    pick = (inside == lax.broadcasted_iota(jnp.int32, (64, 512), 0)).astype(F32).astype(BF16)
    spread = nn(routes, pick)
    row = lax.broadcasted_iota(jnp.int32, (8, 512), 1)
    place = (row >> 8) + ((row >> 5) & 1) * 2 + ((row >> 2) & 1) * 4
    here = place == lax.broadcasted_iota(jnp.int32, (8, 512), 0)
    group = jnp.sum(jnp.where(here, spread, 0.0), axis=0, keepdims=True)
    group = jnp.broadcast_to(group, (8, 512))
    rr_ref[...] = group

    shares = jnp.concatenate(
        [jnp.where(group == float(g), weights, 0.0) for g in range(GROUPS)], axis=0
    ).astype(BF16)
    vb = values.astype(BF16)
    sums = nn(shares, jnp.concatenate([vb, jnp.ones((512, 64), BF16)], axis=1))
    cot = cot_ref[...]
    inner = jnp.sum(sums[:, 0:COUT] * cot.astype(F32), axis=-1, keepdims=True)
    lane = lax.broadcasted_iota(jnp.int32, (8, 64), 1)
    mass = jnp.zeros((8, 64), F32)
    dots = jnp.zeros((8, 64), F32)
    for g in range(GROUPS):
        mass = jnp.where(lane == g, sums[8 * g : 8 * g + 8, COUT:256], mass)
        dots = jnp.where(lane == g, inner[8 * g : 8 * g + 8], dots)
    table = jnp.concatenate([mass, dots], axis=0)
    send_ref[:, 0:COUT] = sums[:, 0:COUT]
    send_ref[:, COUT:256] = jnp.concatenate([table] * 32, axis=0)

    meets = nt(cot, vb)
    total = jnp.zeros((8, 512), F32)
    for g in range(GROUPS):
        total = total + jnp.where(group == float(g), meets[8 * g : 8 * g + 8], 0.0)
    tt_ref[...] = total


def backward_kernel(
    recv_ref, podd_ref, peven_ref, slope_ref, hid_ref, ku_ref, kn_ref, wt_ref, tt_ref, rr_ref,
    cot_ref, key_ref, val_ref, query_ref,
    pooled_ref, db_ref, xs_ref, ys_ref, keep_ref, give_ref, sum_ref,
):
    got = recv_ref[0:16, :]
    for source in range(1, 32):
        got = got + recv_ref[16 * source : 16 * source + 16, :]
    mass = got[0:8, COUT:256]
    dots = got[8:16, COUT:256]
    here = lax.axis_index("chip") * 2 + lax.axis_index("core")
    lane = lax.broadcasted_iota(jnp.int32, (8, 64), 1)
    own = [
        jnp.sum(jnp.where(lane == 2 * here + i, mass, 0.0), axis=-1, keepdims=True)
        for i in range(2)
    ]
    pooled_ref[...] = got[:, 0:COUT] / (1.0 + jnp.concatenate(own, axis=0))

    inverse = 1.0 / (1.0 + mass)
    d_mass = -dots * inverse * inverse
    ih, il = split(inverse)
    mh, ml = split(d_mass)
    group = rr_ref[...]
    member = (
        lax.broadcasted_iota(jnp.int32, (64, 512), 0).astype(F32)
        == jnp.broadcast_to(group[0:1], (64, 512))
    ).astype(F32).astype(BF16)
    inv_row = nn(ih, member) + nn(il, member)
    dm_row = nn(mh, member) + nn(ml, member)
    weights = wt_ref[...]
    d_cos = TEMPER * weights * (tt_ref[...] * inv_row + dm_row)
    scaled = weights * inv_row
    shares = jnp.concatenate(
        [jnp.where(group == float(g), scaled, 0.0) for g in range(GROUPS)], axis=0
    ).astype(BF16)
    d_value = tn(shares, cot_ref[...]).astype(BF16)

    queries = query_ref[...]
    qn = lax.rsqrt(jnp.sum(queries * queries, axis=-1, keepdims=True) + EPS)
    qu = queries * qn
    ku = ku_ref[...]
    dc = d_cos.astype(BF16)
    d_ku = tn(dc, qu.astype(BF16))
    d_key = kn_ref[...] * (d_ku - ku * jnp.sum(ku * d_ku, axis=-1, keepdims=True))
    d_key = d_key.astype(BF16)
    d_qu = nn(dc, ku.astype(BF16))
    d_query = qn * (d_qu - qu * jnp.sum(qu * d_qu, axis=-1, keepdims=True))

    d_hidden = nt(d_key, key_ref[...].astype(BF16)) + nt(d_value, val_ref[...].astype(BF16))
    d_before = d_hidden * slope_ref[...]
    db = d_before.astype(BF16)
    db_ref[...] = db
    xs_ref[...] = db[0:64]
    ys_ref[...] = d_before.reshape(8, 64, COUT)[:, 0:8].reshape(64, COUT).astype(BF16)

    hid = hid_ref[...]
    parts = (podd_ref[0:512, :], peven_ref[...], podd_ref[64:576, :])
    for a in range(3):
        grad = tn(parts[a], db)
        for tap in range(9):
            sum_ref[pl.ds((9 * a + tap) * CIN, CIN), :] = grad[tap * LANES : tap * LANES + CIN]
    base = 27 * CIN
    sum_ref[pl.ds(base, COUT), :] = tn(hid, d_key)
    sum_ref[pl.ds(base + COUT, COUT), :] = tn(hid, d_value)
    sum_ref[pl.ds(base + 2 * COUT, 8), :] = d_query
    bias = jnp.sum(d_before, axis=0, keepdims=True)
    sum_ref[pl.ds(base + 2 * COUT + 8, 8), :] = jnp.broadcast_to(bias, (8, COUT))
    end = base + 2 * COUT + 16
    sum_ref[pl.ds(end, 2 * HALF - end), :] = jnp.zeros((2 * HALF - end, COUT), F32)
    core = lax.axis_index("core")
    keep_ref[...] = sum_ref[pl.ds(pl.multiple_of(core * HALF, HALF), HALF), :].astype(BF16)
    give_ref[...] = sum_ref[pl.ds(pl.multiple_of((1 - core) * HALF, HALF), HALF), :].astype(BF16)


def add_kernel(a_ref, b_ref, out_ref):
    out_ref[...] = (a_ref[...].astype(F32) + b_ref[...].astype(F32)).astype(BF16)


def total_kernel(recv_ref, out_ref):
    total = jnp.sum(recv_ref[...].astype(F32), axis=0).astype(BF16)
    out_ref[...] = jnp.broadcast_to(total[None], out_ref.shape)


def final_kernel(mine_ref, other_ref, dw_ref, dk_ref, dv_ref, dq_ref, dbias_ref, all_ref):
    core = lax.axis_index("core")
    all_ref[pl.ds(pl.multiple_of(core * HALF, HALF), HALF), :] = mine_ref[...].astype(F32)
    all_ref[pl.ds(pl.multiple_of((1 - core) * HALF, HALF), HALF), :] = other_ref[...].astype(F32)
    base = 27 * CIN
    dw_ref[...] = all_ref[0:base, :]
    dk_ref[...] = all_ref[base : base + COUT, :]
    dv_ref[...] = all_ref[base + COUT : base + 2 * COUT, :]
    dq_ref[...] = all_ref[base + 2 * COUT : base + 2 * COUT + 8, :]
    dbias_ref[...] = all_ref[base + 2 * COUT + 8 : base + 2 * COUT + 9, :]


def spread_kernel(
    near_ref, db_ref, xr_ref, yr_ref, xyr_ref, wp_ref, occ_ref, out_ref,
    ext_ref, even_ref, odd_ref, rows_ref, slot_ref,
):
    find_slots(near_ref, slot_ref)
    occ = placed_occupancy(occ_ref, slot_ref)
    edge = yr_ref[...].astype(F32)
    for jx in range(8):
        ext_ref[pl.ds(72 * jx, 64), :] = db_ref[pl.ds(64 * jx, 64), :].astype(F32)
        ext_ref[pl.ds(72 * jx + 64, 8), :] = edge[8 * jx : 8 * jx + 8]
    ext_ref[pl.ds(576, 64), :] = xr_ref[...].astype(F32)
    ext_ref[pl.ds(640, 8), :] = xyr_ref[...].astype(F32)[0:8]
    low = ext_ref[0:576, :].astype(BF16)
    high = ext_ref[72:648, :].astype(BF16)
    even_ref[...] = nt(low, wp_ref[SLOTS9 : 2 * SLOTS9, :])
    odd_ref[...] = nt(low, wp_ref[2 * SLOTS9 : 3 * SLOTS9, :]) + nt(high, wp_ref[0:SLOTS9, :])
    last = lax.broadcasted_iota(jnp.int32, (32, LANES), 0) % 8 == 7

    def up(piece):
        return jnp.where(last, 0.0, pltpu.roll(piece, 31, 0))

    for by in range(2):
        for bx in range(2):
            for xl in range(8):
                x = 8 * bx + xl
                src_ref = even_ref if x % 2 == 0 else odd_ref
                start = 72 * (x // 2) + 32 * by

                def tap(b, c, later, src_ref=src_ref, start=start):
                    return src_ref[pl.ds(start + 8 * later, 32), pl.ds((3 * b + c) * LANES, LANES)]

                e00 = tap(1, 1, 0)
                e01 = tap(1, 2, 0) + up(tap(1, 0, 0))
                e10 = tap(2, 1, 0) + tap(0, 1, 1)
                e11 = tap(2, 2, 0) + tap(0, 2, 1) + up(tap(2, 0, 0) + tap(0, 0, 1))
                for pz, (ye, yo) in enumerate(((e00, e10), (e01, e11))):
                    both = jnp.stack([ye.reshape(4, 8, LANES), yo.reshape(4, 8, LANES)], axis=1)
                    rows_ref[pl.ds(128 * xl + pz, 64, stride=2), :] = both.reshape(64, LANES)
            tile = rows_ref[...].reshape(64, 2, 8, LANES)
            for bz in range(2):
                place = bx + 2 * by + 4 * bz
                block = tile[:, bz].reshape(512, LANES)[:, 0:CIN]
                block = jnp.where(occ[:, place : place + 1] > 0, block, 0.0)
                out_ref[slot_ref[place]] = block.astype(BF16)


def vm():
    return pl.BlockSpec(memory_space=pltpu.VMEM)


def sm():
    return pl.BlockSpec(memory_space=pltpu.SMEM)


def like(shape, dtype=F32):
    return jax.ShapeDtypeStruct(shape, dtype)


def call(kernel, first_scalar, outs, scratch, *args):
    in_specs = [sm() if i == 0 and first_scalar else vm() for i in range(len(args))]
    return pl.pallas_call(
        kernel,
        out_shape=outs,
        in_specs=in_specs,
        out_specs=jax.tree.map(lambda _: vm(), outs),
        scratch_shapes=scratch,
        compiler_params=params(),
        name=kernel.__name__,
    )(*args)


def shift(shard, by_x, by_y):
    pairs = []
    for index in range(32):
        tx, ty = index % 8 + by_x, index // 8 + by_y
        if 0 <= tx < 8 and 0 <= ty < 4:
            pairs.append((index, ty * 8 + tx))
    return lax.ppermute(shard, SPACE, pairs)


def on_device(
    features, occupancy, neighbors, routes, cotangent, conv_weight, conv_bias,
    key_weight, value_weight, queries,
):
    features, occupancy = features[0], occupancy[0]
    slots = pltpu.SMEM((8,), jnp.int32)
    cot = cotangent[0].astype(BF16).reshape(1, 16, COUT)
    cot_all = lax.all_to_all(jnp.broadcast_to(cot, (32, 16, COUT)), SPACE, 0, 0, tiled=True)
    cot_all = cot_all.reshape(512, COUT)

    v, xs, ys = call(
        place_kernel, True,
        [like((16, 4, 64, LANES), BF16), like((256, LANES), BF16), like((256, LANES), BF16)],
        [pltpu.VMEM((1024, LANES), F32), slots],
        neighbors, features, occupancy,
    )
    xr = shift(xs, 1, 0)
    yr = shift(ys, 0, 1)
    xyr = shift(ys[240:256], 1, 1)
    podd, peven, wp, slope, hid, ku, kn, wt, tt, rr, send = call(
        forward_kernel, True,
        [
            like((576, SLOTS9), BF16), like((512, SLOTS9), BF16), like((27 * LANES, COUT), BF16),
            like((512, COUT)), like((512, COUT), BF16), like((512, COUT)), like((512, 1)),
            like((8, 512)), like((8, 512)), like((8, 512)), like((512, 256)),
        ],
        [slots],
        neighbors, v, xr, yr, xyr, conv_weight, conv_bias.reshape(1, COUT), key_weight,
        value_weight, queries, routes.reshape(8, 64), cot_all,
    )
    recv = lax.all_to_all(send.reshape(32, 16, 256), SPACE, 0, 0, tiled=True).reshape(512, 256)
    pooled, db, bxs, bys, keep, give = call(
        backward_kernel, False,
        [
            like((16, COUT)), like((512, COUT), BF16), like((64, COUT), BF16),
            like((64, COUT), BF16), like((HALF, COUT), BF16), like((HALF, COUT), BF16),
        ],
        [pltpu.VMEM((2 * HALF, COUT), F32)],
        recv, podd, peven, slope, hid, ku, kn, wt, tt, rr, cot_all, key_weight, value_weight,
        queries,
    )
    swap = [(0, 1), (1, 0)]
    taken = lax.ppermute(give, "core", swap)
    half = call(add_kernel, False, like((HALF, COUT), BF16), [], keep, taken)
    pieces = lax.all_to_all(half.reshape(64, SHARD, COUT), CHIPS, 0, 0, tiled=True)
    bxr = shift(bxs, -1, 0)
    byr = shift(bys, 0, -1)
    bxyr = shift(bys[0:16], -1, -1)
    d_features = call(
        spread_kernel, True, like((8, 512, CIN), BF16),
        [
            pltpu.VMEM((648, COUT), F32), pltpu.VMEM((576, SLOTS9), F32),
            pltpu.VMEM((576, SLOTS9), F32), pltpu.VMEM((1024, LANES), F32), slots,
        ],
        neighbors, db, bxr, byr, bxyr, wp, occupancy,
    )
    copies = call(total_kernel, False, like((64, SHARD, COUT), BF16), [], pieces)
    mine = lax.all_to_all(copies, CHIPS, 0, 0, tiled=True).reshape(HALF, COUT)
    other = lax.ppermute(mine, "core", swap)
    d_weight, d_key, d_value, d_query, d_bias = call(
        final_kernel, False,
        [
            like((27 * CIN, COUT)), like((COUT, COUT)), like((COUT, COUT)), like((NQ, COUT)),
            like((1, COUT)),
        ],
        [pltpu.VMEM((2 * HALF, COUT), F32)],
        mine, other,
    )
    return (
        pooled.reshape(1, 2, NQ, COUT), d_features[None], d_weight, d_bias.reshape(COUT),
        d_key, d_value, d_query,
    )


def solution(mesh):
    fine = Mesh(mesh.devices.reshape(4, 16, 2), ("section", "chip", "core"))
    in_specs = (
        P("section", SPACE, None, None),
        P("section", SPACE, None),
        P(None, SPACE),
        P("section", SPACE, None),
        P("section", SPACE, None, None),
        P(),
        P(),
        P(),
        P(),
        P(),
    )
    out_specs = (
        P("section", SPACE, None, None),
        P("section", SPACE, None, None),
        P(),
        P(),
        P(),
        P(),
        P(),
    )
    return jax.shard_map(
        on_device, mesh=fine, in_specs=in_specs, out_specs=out_specs, check_vma=False
    )
```

time: 444 us -> 123 us (0.28); the launches traced: 436 us -> 122 us
  waiting for transfers between devices: 166 us -> 7.2 us
  matrix products: 106 us -> 0 us
  local copies, waits for them, and re-layouts: 42.3 us -> 14.6 us
  between operations: 15.6 us -> 0.92 us
  Pallas kernels: 0 us -> 13.4 us
  blocking collectives: 65.2 us -> 56.9 us
  starting transfers between devices: 34.5 us -> 27.6 us
    psum x1 -> x0, waiting for transfers between devices: 138 us -> none  [on_device(): lax.psum((d_weight, d_bias, d_key, d_value, d_query), ('section', 'space'))]
    dot_general x93 -> x0, matrix products: 106 us -> none  [the longest x27 57.2 us: on_device(): jnp.einsum('bxyzc,ic->bxyzi', d_partial, tap_weight, preferred_element_ty...]
    psum x1 -> x0, blocking collectives: 65.2 us -> none  [on_device(): lax.psum((d_weight, d_bias, d_key, d_value, d_query), ('section', 'space'))]
    all_to_all x0 -> x3, blocking collectives: none -> 56.9 us  [the longest x1 22 us: on_device(): lax.all_to_all(half.reshape(64, SHARD, COUT), CHIPS, 0, 0, tiled=True)]
    all_to_all x3 -> x1, waiting for transfers between devices: 25.8 us -> 0.01 us  [on_device(): lax.all_to_all(jnp.broadcast_to(cot, (32, 16, COUT)), SPACE, 0, 0, tiled=...]
    pallas_call x0 -> x7, Pallas kernels: none -> 13.4 us  [call(): pl.pallas_call(kernel, out_shape=outs, in_specs=in_specs, out_specs=jax.t...]
    all_to_all x3 -> x1, starting transfers between devices: 21.7 us -> 9.56 us  [on_device(): lax.all_to_all(jnp.broadcast_to(cot, (32, 16, COUT)), SPACE, 0, 0, tiled=...]
    gather x12 -> x0, local copies, waits for them, and re-layouts: 7.84 us -> none  [the longest x6 3.68 us: pull(): result = jnp.where(near, plane[place], 0.0)]
  transfers between devices with their start and end apart: 8 -> 9, of which waited for: 5 -> 2; matrix products, arithmetic and copies ran while one was open for 8% -> 5% of each run, Pallas kernels for 0% -> 3%
where the time goes in v1:
time: 123 us; the launch traced here: 122 us
  blocking collectives  56.9 us (46%)
  starting transfers between devices  27.6 us (22%)
  local copies, waits for them, and re-layouts  14.6 us (12%)
  Pallas kernels  13.4 us (11%)
  waiting for transfers between devices  7.2 us (6%)
  other arithmetic  1.4 us (1%)
    all_to_all x1, blocking collectives, on_device(): lax.all_to_all(half.reshape(64, SHARD, COUT), CHIPS, 0, 0, tiled=True)  22 us
    all_to_all x1, blocking collectives, on_device(): mine = lax.all_to_all(copies, CHIPS, 0, 0, tiled=True).reshape(HALF, COUT)  18.4 us
    all_to_all x1, blocking collectives, on_device(): lax.all_to_all(send.reshape(32, 16, 256), SPACE, 0, 0, tiled=True)  16.5 us
    ppermute x6, starting transfers between devices, shift(): return lax.ppermute(shard, SPACE, pairs)  14.6 us
    pallas_call x7, Pallas kernels, call(): pl.pallas_call(kernel, out_shape=outs, in_specs=in_specs, out_specs=jax.t...  13.4 us
    unnamed x25, local copies, waits for them, and re-layouts  12.8 us
    all_to_all x1, starting transfers between devices, on_device(): lax.all_to_all(jnp.broadcast_to(cot, (32, 16, COUT)), SPACE, 0, 0, tiled=...  9.56 us
    ppermute x6, waiting for transfers between devices, shift(): return lax.ppermute(shard, SPACE, pairs)  5.57 us
  transfers between devices with their start and end apart: 9, of which 2 were waited for; matrix products, arithmetic and copies ran while one was open for 5% of the time, Pallas kernels for 3%

profile of v1, /device:TPU:1, one launch (start us, length us, event | category | flops | bytes accessed | tf_op | source)
XLA Modules:
  0.0 122.0 jit_solution(11936558647882290456)
XLA Ops:
  2.1 9.6 %all-to-all-start = ((bf16[32,16,192]{2,1,0:T(8,128)(2,1)}), bf16[32,16,192]{2,1,0:T(8,128)(2,1)S(1)}, u32[]{:S(2)}, u32[]{:S(2)}) async-start(bf16[32,16,192]{2,1,0:T(8,128)(2,1)} %broadcast_in_dim.8), calls=%async_computation | async-start | bytes 524288 | tf_op jit(solution)/shard_map/all_to_all | solution.py:374
  11.7 1.6 %copy.21 = bf16[1,8,512,96]{3,2,1,0:T(8,128)(2,1)S(1)} copy(bf16[1,8,512,96]{2,3,1,0:T(8,128)(2,1)} %param.10) | data formatting | bytes 1572864 | tf_op args[0]
  13.3 1.5 %place_kernel.1 = (bf16[16,4,64,128]{3,2,1,0:T(8,128)(2,1)S(1)}, bf16[256,128]{1,0:T(8,128)(2,1)S(1)}, bf16[256,128]{1,0:T(8,128)(2,1)S(1)}) custom-call(s32[6,8]{1,0:T(8,128)S(1)} %copy-done.6, bf16[8,512,96]{2,1,0:T(8,128)(2,1)S(1)} %bitcast.17, s32[8,512]{1,0:T(8,128)S(1)} %bitcast.23), custom_call_target="tpu_custom_call" | custom-call | tf_op jit(solution)/shard_map/place_kernel/pallas_call | solution.py:347
  14.9 3.5 %collective-permute-start = (bf16[256,128]{1,0:T(8,128)(2,1)S(1)}, bf16[256,128]{1,0:T(8,128)(2,1)S(1)}, u32[]{:S(2)}, u32[]{:S(2)}) collective-permute-start(bf16[256,128]{1,0:T(8,128)(2,1)S(1)} %get-tuple-element.33), channel_id=1, source_target_pairs={{0,1},{1,2},{2,3},{3,4},{4,5},{5,6},{6,7},{8,9},{9,10},{10,11},{11... | collective-permute-start | bytes 196616 | tf_op jit(solution)/shard_map/ppermute | solution.py:364
  18.4 3.1 %collective-permute-start.1 = (bf16[256,128]{1,0:T(8,128)(2,1)S(1)}, bf16[256,128]{1,0:T(8,128)(2,1)S(1)}, u32[]{:S(2)}, u32[]{:S(2)}) collective-permute-start(bf16[256,128]{1,0:T(8,128)(2,1)S(1)} %get-tuple-element.34), channel_id=1, source_target_pairs={{0,8},{1,9},{2,10},{3,11},{4,12},{5,13},{6,14},{7,15},{8,16},{9,17... | collective-permute-start | bytes 196616 | tf_op jit(solution)/shard_map/ppermute | solution.py:364
  21.5 3.2 %collective-permute-start.2 = (bf16[16,128]{1,0:T(8,128)(2,1)S(1)}, bf16[16,128]{1,0:T(8,128)(2,1)S(1)}, u32[]{:S(2)}, u32[]{:S(2)}) collective-permute-start(bf16[16,128]{1,0:T(8,128)(2,1)S(1)} %slice.6), channel_id=1, source_target_pairs={{0,9},{1,10},{2,11},{3,12},{4,13},{5,14},{6,15},{8,17},{9,18},{10,... | collective-permute-start | bytes 12296 | tf_op jit(solution)/shard_map/ppermute | solution.py:364
  26.0 2.1 %copy.22.w_ref = bf16[2592,192]{1,0:T(8,128)(2,1)S(1)} copy(bf16[2592,192]{0,1:T(8,128)(2,1)} %param.15) | data formatting | bytes 1990656 | tf_op args[5]
  28.2 4.9 %forward_kernel.1 = (bf16[576,1152]{1,0:T(8,128)(2,1)S(1)}, bf16[512,1152]{1,0:T(8,128)(2,1)S(1)}, bf16[3456,192]{1,0:T(8,128)(2,1)S(1)}, f32[512,192]{1,0:T(8,1...) custom-call(s32[6,8]{1,0:T(8,128)S(1)} %copy-done.6, ...), custom_call_target="tpu_custom_call" | custom-call | tf_op jit(solution)/shard_map/forward_kernel/pallas_call | solution.py:347
  33.1 1.2 copy-done.1
  34.3 16.5 %all_to_all.20 = f32[32,16,256]{2,1,0:T(8,128)S(1)} all-to-all(f32[32,16,256]{2,1,0:T(8,128)S(1)} %bitcast.22), channel_id=1, replica_groups=mesh['section'=4,'chip'=16,'core'=2] {'chip','core'}, dimensions={0} | all-to-all | bytes 1048576 | tf_op jit(solution)/shard_map/all_to_all | solution.py:397
  50.8 2.9 %backward_kernel.1 = (f32[16,192]{1,0:T(8,128)}, bf16[512,192]{1,0:T(8,128)(2,1)S(1)}, bf16[64,192]{1,0:T(8,128)(2,1)S(1)}, bf16[64,192]{1,0:T(8,128)(2,1)S(1)},...) custom-call(f32[512,256]{1,0:T(8,128)S(1)} %bitcast.21, bf16[576,1152]{1,0:T(8,128)(2,1)S(1)} %get-tuple-element.36.podd_ref, ...), custom_call_target="tpu_custom_call" | custom-call | tf_op jit(solution)/shard_map/backward_kernel/pallas_call | solution.py:347
  54.5 1.6 %collective-permute-done.6 = bf16[1536,192]{0,1:T(8,128)(2,1)S(1)} collective-permute-done((bf16[1536,192]{0,1:T(8,128)(2,1)S(1)}, bf16[1536,192]{0,1:T(8,128)(2,1)S(1)}, u32[]{:S(2)}, u32[]{:S(2)}) %collective-permute-start.6) | collective-permute-done | bytes 589856 | tf_op jit(solution)/shard_map/ppermute | solution.py:409
  56.6 22.0 %all_to_all.21.recv_ref = bf16[64,24,192]{2,1,0:T(8,128)(2,1)S(1)} all-to-all(bf16[64,24,192]{2,1,0:T(8,128)(2,1)S(1)} %bitcast.18), channel_id=1, replica_groups=mesh['section'=4,'chip'=16,'core'=2] {'section','chip'}, dimensions={0} | all-to-all | bytes 1179648 | tf_op jit(solution)/shard_map/all_to_all | solution.py:411
  78.8 18.4 %all_to_all.22 = bf16[64,24,192]{2,1,0:T(8,128)(2,1)S(1)} all-to-all(bf16[64,24,192]{2,1,0:T(8,128)(2,1)S(1)} %total_kernel.1), channel_id=1, replica_groups=mesh['section'=4,'chip'=16,'core'=2] {'section','chip'}, dimensions={0} | all-to-all | bytes 1179648 | tf_op jit(solution)/shard_map/all_to_all | solution.py:424
  97.4 3.0 %collective-permute-start.7 = (bf16[1536,192]{0,1:T(8,128)(2,1)S(1)}, bf16[1536,192]{0,1:T(8,128)(2,1)S(1)}, u32[]{:S(2)}, u32[]{:S(2)}) collective-permute-start(bf16[1536,192]{0,1:T(8,128)(2,1)S(1)} %copy.25), channel_id=1, source_target_pairs={{0,1},{1,0},{2,3},{3,2},{4,5},{5,4},{6,7},{7,6},{8,9},{9,8},{10,11... | collective-permute-start | bytes 1769480 | tf_op jit(solution)/shard_map/ppermute | solution.py:425
  100.4 1.9 %collective-permute-start.3 = (bf16[64,192]{1,0:T(8,128)(2,1)S(1)}, bf16[64,192]{1,0:T(8,128)(2,1)S(1)}, u32[]{:S(2)}, u32[]{:S(2)}) collective-permute-start(bf16[64,192]{1,0:T(8,128)(2,1)S(1)} %get-tuple-element.47), channel_id=1, source_target_pairs={{1,0},{2,1},{3,2},{4,3},{5,4},{6,5},{7,6},{9,8},{10,9},{11,10},{12... | collective-permute-start | bytes 73736 | tf_op jit(solution)/shard_map/ppermute | solution.py:364
  102.3 1.3 %collective-permute-start.4 = (bf16[64,192]{1,0:T(8,128)(2,1)S(1)}, bf16[64,192]{1,0:T(8,128)(2,1)S(1)}, u32[]{:S(2)}, u32[]{:S(2)}) collective-permute-start(bf16[64,192]{1,0:T(8,128)(2,1)S(1)} %get-tuple-element.48), channel_id=1, source_target_pairs={{8,0},{9,1},{10,2},{11,3},{12,4},{13,5},{14,6},{15,7},{16,8},{17,9... | collective-permute-start | bytes 73736 | tf_op jit(solution)/shard_map/ppermute | solution.py:364
  103.6 1.5 %collective-permute-start.5 = (bf16[16,192]{1,0:T(8,128)(2,1)S(1)}, bf16[16,192]{1,0:T(8,128)(2,1)S(1)}, u32[]{:S(2)}, u32[]{:S(2)}) collective-permute-start(bf16[16,192]{1,0:T(8,128)(2,1)S(1)} %slice.7), channel_id=1, source_target_pairs={{9,0},{10,1},{11,2},{12,3},{13,4},{14,5},{15,6},{17,8},{18,9},{19,... | collective-permute-start | bytes 18440 | tf_op jit(solution)/shard_map/ppermute | solution.py:364
  105.1 5.6 %collective-permute-done.5.xyr_ref = bf16[16,192]{1,0:T(8,128)(2,1)S(1)} collective-permute-done((bf16[16,192]{1,0:T(8,128)(2,1)S(1)}, bf16[16,192]{1,0:T(8,128)(2,1)S(1)}, u32[]{:S(2)}, u32[]{:S(2)}) %collective-permute-start.5) | collective-permute-done | bytes 6176 | tf_op jit(solution)/shard_map/ppermute | solution.py:364
  110.6 1.5 %copy-done.2 = bf16[3456,192]{1,0:T(8,128)(2,1)S(1)} copy-done((bf16[3456,192]{1,0:T(8,128)(2,1)S(1)}, bf16[3456,192]{1,0:T(8,128)(2,1)}, u32[]{:S(2)}) %copy-start.2) | copy-done | bytes 1327128
  112.1 2.5 %spread_kernel.1 = bf16[8,512,96]{2,1,0:T(8,128)(2,1)S(1)} custom-call(s32[6,8]{1,0:T(8,128)S(1)} %copy-done.6, bf16[512,192]{1,0:T(8,128)(2,1)S(1)} %get-tuple-element.46.db_ref, bf16[64,192]{1,0:T(8,128)(2,1)S(1)} %collective-permute-done.3.xr_ref, bf16[64,192]{1,0:T(8,128)(2,1)S(1)} %collective-permute-done.4.yr_ref, ...), custom_call_target="tpu_custom_call" | custom-call | tf_op jit(solution)/shard_map/spread_kernel/pallas_call | solution.py:347
  114.6 1.2 %copy.27 = bf16[1,8,512,96]{2,3,1,0:T(8,128)(2,1)} copy(bf16[1,8,512,96]{3,2,1,0:T(8,128)(2,1)S(1)} %bitcast.16) | data formatting | bytes 1572864
  117.3 1.5 %copy-done = f32[2592,192]{1,0:T(8,128)} copy-done((f32[2592,192]{1,0:T(8,128)}, f32[2592,192]{1,0:T(8,128)S(1)}, u32[]{:S(2)}) %copy-start) | copy-done | bytes 1990680
  118.8 3.2 %copy.28 = f32[2592,192]{0,1:T(8,128)} copy(f32[2592,192]{1,0:T(8,128)} %copy-done) | data formatting | bytes 3981312
  (39 shorter events, 5.9 us)
Async XLA Ops:
  0.6 12.7 %copy-start.6 = (s32[6,8]{1,0:T(8,128)S(1)}, s32[6,8]{1,0:T(8,128)}, u32[]{:S(2)}) copy-start(s32[6,8]{1,0:T(8,128)} %near_ref.5) | copy-start | bytes 580
  0.6 12.7 %copy-start.5 = (s32[1,8,512]{2,1,0:T(8,128)S(1)}, s32[1,8,512]{2,1,0:T(8,128)}, u32[]{:S(2)}) copy-start(s32[1,8,512]{2,1,0:T(8,128)} %param.11) | copy-start | bytes 49156
  2.1 23.2 %copy-start.9 = (s32[1,512,1]{1,2,0:T(1,128)S(1)}, s32[1,512,1]{1,2,0:T(1,128)}, u32[]{:S(2)}) copy-start(s32[1,512,1]{1,2,0:T(1,128)} %param.13) | copy-start | bytes 6148
  2.1 26.0 %all-to-all-start = ((bf16[32,16,192]{2,1,0:T(8,128)(2,1)}), bf16[32,16,192]{2,1,0:T(8,128)(2,1)S(1)}, u32[]{:S(2)}, u32[]{:S(2)}) async-start(bf16[32,16,192]{2,1,0:T(8,128)(2,1)} %broadcast_in_dim.8), calls=%async_computation | async-start | bytes 524288 | tf_op jit(solution)/shard_map/all_to_all | solution.py:374
  13.3 14.9 %copy-start.3 = (f32[192,192]{1,0:T(8,128)S(1)}, f32[192,192]{1,0:T(8,128)}, u32[]{:S(2)}) copy-start(f32[192,192]{1,0:T(8,128)} %key_ref.3) | copy-start | bytes 442372
  13.3 14.9 %copy-start.4 = (f32[192,192]{1,0:T(8,128)S(1)}, f32[192,192]{1,0:T(8,128)}, u32[]{:S(2)}) copy-start(f32[192,192]{1,0:T(8,128)} %val_ref.3) | copy-start | bytes 442372
  13.3 14.9 %copy-start.7 = (f32[8,192]{1,0:T(8,128)S(1)}, f32[8,192]{1,0:T(8,128)}, u32[]{:S(2)}) copy-start(f32[8,192]{1,0:T(8,128)} %query_ref.3) | copy-start | bytes 18436
  13.3 14.9 %copy-start.8 = (f32[192]{0:T(256)S(1)}, f32[192]{0:T(256)}, u32[]{:S(2)}) copy-start(f32[192]{0:T(256)} %param.16) | copy-start | bytes 2308
  14.9 13.2 %collective-permute-start = (bf16[256,128]{1,0:T(8,128)(2,1)S(1)}, bf16[256,128]{1,0:T(8,128)(2,1)S(1)}, u32[]{:S(2)}, u32[]{:S(2)}) collective-permute-start(bf16[256,128]{1,0:T(8,128)(2,1)S(1)} %get-tuple-element.33), channel_id=1, source_target_pairs={{0,1},{1,2},{2,3},{3,4},{4,5},{5,6},{6,7},{8,9},{9,10},{10,11},{11... | collective-permute-start | bytes 196616 | tf_op jit(solution)/shard_map/ppermute | solution.py:364
  18.4 9.7 %collective-permute-start.1 = (bf16[256,128]{1,0:T(8,128)(2,1)S(1)}, bf16[256,128]{1,0:T(8,128)(2,1)S(1)}, u32[]{:S(2)}, u32[]{:S(2)}) collective-permute-start(bf16[256,128]{1,0:T(8,128)(2,1)S(1)} %get-tuple-element.34), channel_id=1, source_target_pairs={{0,8},{1,9},{2,10},{3,11},{4,12},{5,13},{6,14},{7,15},{8,16},{9,17... | collective-permute-start | bytes 196616 | tf_op jit(solution)/shard_map/ppermute | solution.py:364
  21.5 6.6 %collective-permute-start.2 = (bf16[16,128]{1,0:T(8,128)(2,1)S(1)}, bf16[16,128]{1,0:T(8,128)(2,1)S(1)}, u32[]{:S(2)}, u32[]{:S(2)}) collective-permute-start(bf16[16,128]{1,0:T(8,128)(2,1)S(1)} %slice.6), channel_id=1, source_target_pairs={{0,9},{1,10},{2,11},{3,12},{4,13},{5,14},{6,15},{8,17},{9,18},{10,... | collective-permute-start | bytes 12296 | tf_op jit(solution)/shard_map/ppermute | solution.py:364
  33.1 1.2 copy-start.1
  54.0 2.1 %collective-permute-start.6 = (bf16[1536,192]{0,1:T(8,128)(2,1)S(1)}, bf16[1536,192]{0,1:T(8,128)(2,1)S(1)}, u32[]{:S(2)}, u32[]{:S(2)}) collective-permute-start(bf16[1536,192]{0,1:T(8,128)(2,1)S(1)} %copy.23), channel_id=1, source_target_pairs={{0,1},{1,0},{2,3},{3,2},{4,5},{5,4},{6,7},{7,6},{8,9},{9,8},{10,11... | collective-permute-start | bytes 1769480 | tf_op jit(solution)/shard_map/ppermute | solution.py:409
  97.4 18.5 %collective-permute-start.7 = (bf16[1536,192]{0,1:T(8,128)(2,1)S(1)}, bf16[1536,192]{0,1:T(8,128)(2,1)S(1)}, u32[]{:S(2)}, u32[]{:S(2)}) collective-permute-start(bf16[1536,192]{0,1:T(8,128)(2,1)S(1)} %copy.25), channel_id=1, source_target_pairs={{0,1},{1,0},{2,3},{3,2},{4,5},{5,4},{6,7},{7,6},{8,9},{9,8},{10,11... | collective-permute-start | bytes 1769480 | tf_op jit(solution)/shard_map/ppermute | solution.py:425
  100.4 10.3 %collective-permute-start.3 = (bf16[64,192]{1,0:T(8,128)(2,1)S(1)}, bf16[64,192]{1,0:T(8,128)(2,1)S(1)}, u32[]{:S(2)}, u32[]{:S(2)}) collective-permute-start(bf16[64,192]{1,0:T(8,128)(2,1)S(1)} %get-tuple-element.47), channel_id=1, source_target_pairs={{1,0},{2,1},{3,2},{4,3},{5,4},{6,5},{7,6},{9,8},{10,9},{11,10},{12... | collective-permute-start | bytes 73736 | tf_op jit(solution)/shard_map/ppermute | solution.py:364
  102.3 8.4 %collective-permute-start.4 = (bf16[64,192]{1,0:T(8,128)(2,1)S(1)}, bf16[64,192]{1,0:T(8,128)(2,1)S(1)}, u32[]{:S(2)}, u32[]{:S(2)}) collective-permute-start(bf16[64,192]{1,0:T(8,128)(2,1)S(1)} %get-tuple-element.48), channel_id=1, source_target_pairs={{8,0},{9,1},{10,2},{11,3},{12,4},{13,5},{14,6},{15,7},{16,8},{17,9... | collective-permute-start | bytes 73736 | tf_op jit(solution)/shard_map/ppermute | solution.py:364
  103.6 7.0 %collective-permute-start.5 = (bf16[16,192]{1,0:T(8,128)(2,1)S(1)}, bf16[16,192]{1,0:T(8,128)(2,1)S(1)}, u32[]{:S(2)}, u32[]{:S(2)}) collective-permute-start(bf16[16,192]{1,0:T(8,128)(2,1)S(1)} %slice.7), channel_id=1, source_target_pairs={{9,0},{10,1},{11,2},{12,3},{13,4},{14,5},{15,6},{17,8},{18,9},{19,... | collective-permute-start | bytes 18440 | tf_op jit(solution)/shard_map/ppermute | solution.py:364
  110.6 1.5 %copy-start.2 = (bf16[3456,192]{1,0:T(8,128)(2,1)S(1)}, bf16[3456,192]{1,0:T(8,128)(2,1)}, u32[]{:S(2)}) copy-start(bf16[3456,192]{1,0:T(8,128)(2,1)} %copy-done.1) | copy-start | bytes 3981316
  117.3 1.5 %copy-start = (f32[2592,192]{1,0:T(8,128)}, f32[2592,192]{1,0:T(8,128)S(1)}, u32[]{:S(2)}) copy-start(f32[2592,192]{1,0:T(8,128)S(1)} %get-tuple-element.66) | copy-start | bytes 5971972

commit v2 on v1

--- a/solution.py
+++ b/solution.py
@@ -13,8 +13,10 @@
 LANES = 128
 SLOTS9 = 9 * LANES
 GROUPS, NQ = 64, 8
-SHARD = 24
+KDIM = 27 * CIN
+SHARD = 40
 HALF = 64 * SHARD
+WIDE = 24 * LANES
 F32, BF16 = jnp.float32, jnp.bfloat16
 SPACE = ("chip", "core")
 CHIPS = ("section", "chip")
@@ -55,22 +57,19 @@
         slot_ref[place] = slot
 
 
-def placed_occupancy(occ_ref, slot_ref):
-    rows = [occ_ref[pl.ds(slot_ref[p], 1), :] for p in range(8)]
-    return jnp.concatenate(rows, axis=0).astype(F32).T
-
-
-def place_kernel(near_ref, feat_ref, occ_ref, v_ref, xs_ref, ys_ref, rows_ref, slot_ref):
+def place_kernel(
+    near_ref, feat_ref, occ_ref, cot_ref, v_ref, xs_ref, ys_ref, early_ref, rows_ref, slot_ref
+):
     find_slots(near_ref, slot_ref)
-    occ = placed_occupancy(occ_ref, slot_ref)
     rows_ref[...] = jnp.zeros_like(rows_ref)
     for by in range(2):
         for bx in range(2):
             pair = []
             for bz in range(2):
                 place = bx + 2 * by + 4 * bz
-                block = feat_ref[slot_ref[place]].astype(F32)
-                block = jnp.where(occ[:, place : place + 1] > 0, block, 0.0)
+                slot = slot_ref[place]
+                block = feat_ref[slot].astype(F32)
+                block = jnp.where(occ_ref[pl.ds(slot, 1), :] > 0, block, 0.0).T
                 pair.append(block.reshape(64, 8, CIN))
             rows_ref[:, 0:CIN] = jnp.stack(pair, axis=1).reshape(1024, CIN)
             for pz in range(2):
@@ -87,23 +86,31 @@
                     jnp.stack(edge, axis=1).reshape(128, LANES).astype(BF16)
                 )
     xs_ref[...] = v_ref[15].reshape(256, LANES)
+    early = jnp.concatenate(
+        [cot_ref[...].astype(BF16), jnp.zeros((16, 64), BF16), ys_ref[240:256, :]], axis=1
+    )
+    early_ref[...] = jnp.broadcast_to(early[None], early_ref.shape)
 
 
 def forward_kernel(
-    near_ref, v_ref, xr_ref, yr_ref, xyr_ref, w_ref, bias_ref, key_ref, val_ref, query_ref,
-    routes_ref, cot_ref,
+    near_ref, v_ref, xr_ref, yr_ref, w_ref, bias_ref, key_ref, val_ref, query_ref,
+    routes_ref, early_ref,
     podd_ref, peven_ref, wp_ref, slope_ref, hid_ref, ku_ref, kn_ref, wt_ref, tt_ref, rr_ref,
-    send_ref, slot_ref,
+    send_ref, slot_ref, routes8_ref,
 ):
     find_slots(near_ref, slot_ref)
     wp_ref[...] = jnp.zeros_like(wp_ref)
     for tap in range(27):
-        wp_ref[pl.ds(tap * LANES, CIN), :] = w_ref[pl.ds(tap * CIN, CIN), :]
+        wp_ref[:, pl.ds(tap * LANES, CIN)] = w_ref[:, pl.ds(tap * CIN, CIN)]
+    here = lax.axis_index("chip") * 2 + lax.axis_index("core")
+    inner = jnp.logical_and(here >= 8, lax.rem(here, 8) > 0)
+    corner = early_ref[pl.ds(pl.multiple_of(16 * jnp.maximum(here - 9, 0), 16), 16), 256:384]
+    corner = jnp.where(inner, corner.astype(F32), 0.0)
     first = lax.broadcasted_iota(jnp.int32, (64, LANES), 0) % 8 == 0
     for x in range(-1, 16):
         if x < 0:
             planes = xr_ref[...].astype(F32).reshape(4, 64, LANES)
-            edge = xyr_ref[...].astype(F32)
+            edge = corner
         else:
             planes = v_ref[x].astype(F32)
             edge = yr_ref[pl.ds(16 * x, 16), :].astype(F32)
@@ -122,9 +129,9 @@
                 column = (3 * b + c) * LANES
                 out_ref[pl.ds(row, 64), pl.ds(column, LANES)] = piece.astype(BF16)
     before = (
-        nn(podd_ref[0:512, :], wp_ref[0:SLOTS9, :])
-        + nn(peven_ref[...], wp_ref[SLOTS9 : 2 * SLOTS9, :])
-        + nn(podd_ref[64:576, :], wp_ref[2 * SLOTS9 : 3 * SLOTS9, :])
+        nt(podd_ref[0:512, :], wp_ref[:, 0:SLOTS9])
+        + nt(peven_ref[...], wp_ref[:, SLOTS9 : 2 * SLOTS9])
+        + nt(podd_ref[64:576, :], wp_ref[:, 2 * SLOTS9 : 3 * SLOTS9])
         + bias_ref[...]
     )
     root = 0.7978845608028654
@@ -151,8 +158,10 @@
     weights = jnp.exp(TEMPER * (nt(qh, uh) + nt(ql, uh) + nt(qh, ul)))
     wt_ref[...] = weights
 
+    for slot in range(8):
+        routes8_ref[slot : slot + 1, :] = routes_ref[:, 64 * slot : 64 * slot + 64]
     routes = jnp.concatenate(
-        [routes_ref[pl.ds(slot_ref[p], 1), :] for p in range(8)], axis=0
+        [routes8_ref[pl.ds(slot_ref[p], 1), :] for p in range(8)], axis=0
     ).astype(BF16)
     row = lax.broadcasted_iota(jnp.int32, (64, 512), 1)
     inside = ((row >> 6) & 3) * 16 + ((row >> 3) & 3) * 4 + (row & 3)
@@ -170,7 +179,7 @@
     ).astype(BF16)
     vb = values.astype(BF16)
     sums = nn(shares, jnp.concatenate([vb, jnp.ones((512, 64), BF16)], axis=1))
-    cot = cot_ref[...]
+    cot = early_ref[:, 0:COUT]
     inner = jnp.sum(sums[:, 0:COUT] * cot.astype(F32), axis=-1, keepdims=True)
     lane = lax.broadcasted_iota(jnp.int32, (8, 64), 1)
     mass = jnp.zeros((8, 64), F32)
@@ -179,8 +188,8 @@
         mass = jnp.where(lane == g, sums[8 * g : 8 * g + 8, COUT:256], mass)
         dots = jnp.where(lane == g, inner[8 * g : 8 * g + 8], dots)
     table = jnp.concatenate([mass, dots], axis=0)
-    send_ref[:, 0:COUT] = sums[:, 0:COUT]
-    send_ref[:, COUT:256] = jnp.concatenate([table] * 32, axis=0)
+    send_ref[:, 0:COUT] = sums[:, 0:COUT].astype(BF16)
+    send_ref[:, COUT:256] = jnp.concatenate([table.astype(BF16)] * 32, axis=0)
 
     meets = nt(cot, vb)
     total = jnp.zeros((8, 512), F32)
@@ -191,12 +200,10 @@
 
 def backward_kernel(
     recv_ref, podd_ref, peven_ref, slope_ref, hid_ref, ku_ref, kn_ref, wt_ref, tt_ref, rr_ref,
-    cot_ref, key_ref, val_ref, query_ref,
+    early_ref, key_ref, val_ref, query_ref,
     pooled_ref, db_ref, xs_ref, ys_ref, keep_ref, give_ref, sum_ref,
 ):
-    got = recv_ref[0:16, :]
-    for source in range(1, 32):
-        got = got + recv_ref[16 * source : 16 * source + 16, :]
+    got = jnp.sum(recv_ref[...].reshape(32, 16, 256).astype(F32), axis=0)
     mass = got[0:8, COUT:256]
     dots = got[8:16, COUT:256]
     here = lax.axis_index("chip") * 2 + lax.axis_index("core")
@@ -224,7 +231,7 @@
     shares = jnp.concatenate(
         [jnp.where(group == float(g), scaled, 0.0) for g in range(GROUPS)], axis=0
     ).astype(BF16)
-    d_value = tn(shares, cot_ref[...]).astype(BF16)
+    d_value = tn(shares, early_ref[:, 0:COUT]).astype(BF16)
 
     queries = query_ref[...]
     qn = lax.rsqrt(jnp.sum(queries * queries, axis=-1, keepdims=True) + EPS)
@@ -247,24 +254,29 @@
     hid = hid_ref[...]
     parts = (podd_ref[0:512, :], peven_ref[...], podd_ref[64:576, :])
     for a in range(3):
-        grad = tn(parts[a], db)
+        grad = tn(db, parts[a])
         for tap in range(9):
-            sum_ref[pl.ds((9 * a + tap) * CIN, CIN), :] = grad[tap * LANES : tap * LANES + CIN]
-    base = 27 * CIN
-    sum_ref[pl.ds(base, COUT), :] = tn(hid, d_key)
-    sum_ref[pl.ds(base + COUT, COUT), :] = tn(hid, d_value)
-    sum_ref[pl.ds(base + 2 * COUT, 8), :] = d_query
-    bias = jnp.sum(d_before, axis=0, keepdims=True)
-    sum_ref[pl.ds(base + 2 * COUT + 8, 8), :] = jnp.broadcast_to(bias, (8, COUT))
-    end = base + 2 * COUT + 16
-    sum_ref[pl.ds(end, 2 * HALF - end), :] = jnp.zeros((2 * HALF - end, COUT), F32)
-    core = lax.axis_index("core")
-    keep_ref[...] = sum_ref[pl.ds(pl.multiple_of(core * HALF, HALF), HALF), :].astype(BF16)
-    give_ref[...] = sum_ref[pl.ds(pl.multiple_of((1 - core) * HALF, HALF), HALF), :].astype(BF16)
+            piece = grad[:, tap * LANES : tap * LANES + CIN]
+            sum_ref[:, pl.ds((9 * a + tap) * CIN, CIN)] = piece
+    sum_ref[:, KDIM : KDIM + COUT] = tn(hid, d_key)
+    sum_ref[:, KDIM + COUT : KDIM + 2 * COUT] = tn(hid, d_value)
+    bias = jnp.broadcast_to(jnp.sum(d_before, axis=0, keepdims=True), (8, COUT))
+    small = [d_query[:, 0:CIN], d_query[:, CIN:COUT], bias[:, 0:CIN], bias[:, CIN:COUT]]
+    small = jnp.concatenate(small + [jnp.zeros((COUT - 32, CIN), F32)], axis=0)
+    sum_ref[:, KDIM + 2 * COUT : WIDE] = small
+    low = lax.axis_index("core") == 0
+    for t in range(12):
+        left = sum_ref[:, LANES * t : LANES * (t + 1)]
+        right = sum_ref[:, LANES * (t + 12) : LANES * (t + 13)]
+        keep_ref[COUT * t : COUT * (t + 1), :] = jnp.where(low, left, right)
+        give_ref[COUT * t : COUT * (t + 1), :] = jnp.where(low, right, left).astype(BF16)
+    rest = HALF - 12 * COUT
+    keep_ref[12 * COUT : HALF, :] = jnp.zeros((rest, LANES), F32)
+    give_ref[12 * COUT : HALF, :] = jnp.zeros((rest, LANES), BF16)
 
 
 def add_kernel(a_ref, b_ref, out_ref):
-    out_ref[...] = (a_ref[...].astype(F32) + b_ref[...].astype(F32)).astype(BF16)
+    out_ref[...] = (a_ref[...] + b_ref[...].astype(F32)).astype(BF16)
 
 
 def total_kernel(recv_ref, out_ref):
@@ -273,15 +285,18 @@
 
 
 def final_kernel(mine_ref, other_ref, dw_ref, dk_ref, dv_ref, dq_ref, dbias_ref, all_ref):
-    core = lax.axis_index("core")
-    all_ref[pl.ds(pl.multiple_of(core * HALF, HALF), HALF), :] = mine_ref[...].astype(F32)
-    all_ref[pl.ds(pl.multiple_of((1 - core) * HALF, HALF), HALF), :] = other_ref[...].astype(F32)
-    base = 27 * CIN
-    dw_ref[...] = all_ref[0:base, :]
-    dk_ref[...] = all_ref[base : base + COUT, :]
-    dv_ref[...] = all_ref[base + COUT : base + 2 * COUT, :]
-    dq_ref[...] = all_ref[base + 2 * COUT : base + 2 * COUT + 8, :]
-    dbias_ref[...] = all_ref[base + 2 * COUT + 8 : base + 2 * COUT + 9, :]
+    low = lax.axis_index("core") == 0
+    for t in range(12):
+        mine = mine_ref[COUT * t : COUT * (t + 1), :].astype(F32)
+        other = other_ref[COUT * t : COUT * (t + 1), :].astype(F32)
+        all_ref[:, LANES * t : LANES * (t + 1)] = jnp.where(low, mine, other)
+        all_ref[:, LANES * (t + 12) : LANES * (t + 13)] = jnp.where(low, other, mine)
+    dw_ref[...] = all_ref[:, 0:KDIM]
+    dk_ref[...] = all_ref[:, KDIM : KDIM + COUT]
+    dv_ref[...] = all_ref[:, KDIM + COUT : KDIM + 2 * COUT]
+    small = all_ref[0:32, KDIM + 2 * COUT : WIDE]
+    dq_ref[...] = jnp.concatenate([small[0:8], small[8:16]], axis=1)
+    dbias_ref[...] = jnp.concatenate([small[16:17], small[24:25]], axis=1)
 
 
 def spread_kernel(
@@ -289,7 +304,6 @@
     ext_ref, even_ref, odd_ref, rows_ref, slot_ref,
 ):
     find_slots(near_ref, slot_ref)
-    occ = placed_occupancy(occ_ref, slot_ref)
     edge = yr_ref[...].astype(F32)
     for jx in range(8):
         ext_ref[pl.ds(72 * jx, 64), :] = db_ref[pl.ds(64 * jx, 64), :].astype(F32)
@@ -298,8 +312,8 @@
     ext_ref[pl.ds(640, 8), :] = xyr_ref[...].astype(F32)[0:8]
     low = ext_ref[0:576, :].astype(BF16)
     high = ext_ref[72:648, :].astype(BF16)
-    even_ref[...] = nt(low, wp_ref[SLOTS9 : 2 * SLOTS9, :])
-    odd_ref[...] = nt(low, wp_ref[2 * SLOTS9 : 3 * SLOTS9, :]) + nt(high, wp_ref[0:SLOTS9, :])
+    even_ref[...] = nn(low, wp_ref[:, SLOTS9 : 2 * SLOTS9])
+    odd_ref[...] = nn(low, wp_ref[:, 2 * SLOTS9 : 3 * SLOTS9]) + nn(high, wp_ref[:, 0:SLOTS9])
     last = lax.broadcasted_iota(jnp.int32, (32, LANES), 0) % 8 == 7
 
     def up(piece):
@@ -325,9 +339,10 @@
             tile = rows_ref[...].reshape(64, 2, 8, LANES)
             for bz in range(2):
                 place = bx + 2 * by + 4 * bz
-                block = tile[:, bz].reshape(512, LANES)[:, 0:CIN]
-                block = jnp.where(occ[:, place : place + 1] > 0, block, 0.0)
-                out_ref[slot_ref[place]] = block.astype(BF16)
+                slot = slot_ref[place]
+                block = tile[:, bz].reshape(512, LANES).T[0:CIN]
+                block = jnp.where(occ_ref[pl.ds(slot, 1), :] > 0, block, 0.0)
+                out_ref[slot] = block.astype(BF16)
 
 
 def vm():
@@ -368,73 +383,73 @@
     features, occupancy, neighbors, routes, cotangent, conv_weight, conv_bias,
     key_weight, value_weight, queries,
 ):
-    features, occupancy = features[0], occupancy[0]
+    features, occupancy = jnp.swapaxes(features[0], 1, 2), occupancy[0]
     slots = pltpu.SMEM((8,), jnp.int32)
-    cot = cotangent[0].astype(BF16).reshape(1, 16, COUT)
-    cot_all = lax.all_to_all(jnp.broadcast_to(cot, (32, 16, COUT)), SPACE, 0, 0, tiled=True)
-    cot_all = cot_all.reshape(512, COUT)
-
-    v, xs, ys = call(
+    v, xs, ys, early = call(
         place_kernel, True,
-        [like((16, 4, 64, LANES), BF16), like((256, LANES), BF16), like((256, LANES), BF16)],
+        [
+            like((16, 4, 64, LANES), BF16), like((256, LANES), BF16), like((256, LANES), BF16),
+            like((32, 16, 3 * LANES), BF16),
+        ],
         [pltpu.VMEM((1024, LANES), F32), slots],
-        neighbors, features, occupancy,
-    )
+        neighbors, features, occupancy, cotangent.reshape(16, COUT),
+    )
+    early = lax.all_to_all(early, SPACE, 0, 0, tiled=True).reshape(512, 3 * LANES)
     xr = shift(xs, 1, 0)
     yr = shift(ys, 0, 1)
-    xyr = shift(ys[240:256], 1, 1)
     podd, peven, wp, slope, hid, ku, kn, wt, tt, rr, send = call(
         forward_kernel, True,
         [
-            like((576, SLOTS9), BF16), like((512, SLOTS9), BF16), like((27 * LANES, COUT), BF16),
+            like((576, SLOTS9), BF16), like((512, SLOTS9), BF16), like((COUT, 27 * LANES), BF16),
             like((512, COUT)), like((512, COUT), BF16), like((512, COUT)), like((512, 1)),
-            like((8, 512)), like((8, 512)), like((8, 512)), like((512, 256)),
+            like((8, 512)), like((8, 512)), like((8, 512)), like((512, 256), BF16),
         ],
-        [slots],
-        neighbors, v, xr, yr, xyr, conv_weight, conv_bias.reshape(1, COUT), key_weight,
-        value_weight, queries, routes.reshape(8, 64), cot_all,
+        [slots, pltpu.VMEM((8, 64), jnp.int32)],
+        neighbors, v, xr, yr, conv_weight.T, conv_bias.reshape(1, COUT), key_weight,
+        value_weight, queries, routes.reshape(1, 512), early,
     )
     recv = lax.all_to_all(send.reshape(32, 16, 256), SPACE, 0, 0, tiled=True).reshape(512, 256)
     pooled, db, bxs, bys, keep, give = call(
         backward_kernel, False,
         [
             like((16, COUT)), like((512, COUT), BF16), like((64, COUT), BF16),
-            like((64, COUT), BF16), like((HALF, COUT), BF16), like((HALF, COUT), BF16),
+            like((64, COUT), BF16), like((HALF, LANES)), like((HALF, LANES), BF16),
         ],
-        [pltpu.VMEM((2 * HALF, COUT), F32)],
-        recv, podd, peven, slope, hid, ku, kn, wt, tt, rr, cot_all, key_weight, value_weight,
+        [pltpu.VMEM((COUT, WIDE), F32)],
+        recv, podd, peven, slope, hid, ku, kn, wt, tt, rr, early, key_weight, value_weight,
         queries,
     )
     swap = [(0, 1), (1, 0)]
     taken = lax.ppermute(give, "core", swap)
-    half = call(add_kernel, False, like((HALF, COUT), BF16), [], keep, taken)
-    pieces = lax.all_to_all(half.reshape(64, SHARD, COUT), CHIPS, 0, 0, tiled=True)
+    half = call(add_kernel, False, like((HALF, LANES), BF16), [], keep, taken)
+    pieces = lax.all_to_all(half.reshape(64, SHARD, LANES), CHIPS, 0, 0, tiled=True)
     bxr = shift(bxs, -1, 0)
     byr = shift(bys, 0, -1)
     bxyr = shift(bys[0:16], -1, -1)
     d_features = call(
-        spread_kernel, True, like((8, 512, CIN), BF16),
+        spread_kernel, True, like((8, CIN, 512), BF16),
         [
             pltpu.VMEM((648, COUT), F32), pltpu.VMEM((576, SLOTS9), F32),
             pltpu.VMEM((576, SLOTS9), F32), pltpu.VMEM((1024, LANES), F32), slots,
         ],
         neighbors, db, bxr, byr, bxyr, wp, occupancy,
     )
-    copies = call(total_kernel, False, like((64, SHARD, COUT), BF16), [], pieces)
-    mine = lax.all_to_all(copies, CHIPS, 0, 0, tiled=True).reshape(HALF, COUT)
+    pieces, d_features = lax.optimization_barrier((pieces, d_features))
+    copies = call(total_kernel, False, like((64, SHARD, LANES), BF16), [], pieces)
+    mine = lax.all_to_all(copies, CHIPS, 0, 0, tiled=True).reshape(HALF, LANES)
     other = lax.ppermute(mine, "core", swap)
     d_weight, d_key, d_value, d_query, d_bias = call(
         final_kernel, False,
         [
-            like((27 * CIN, COUT)), like((COUT, COUT)), like((COUT, COUT)), like((NQ, COUT)),
+            like((COUT, KDIM)), like((COUT, COUT)), like((COUT, COUT)), like((NQ, COUT)),
             like((1, COUT)),
         ],
-        [pltpu.VMEM((2 * HALF, COUT), F32)],
+        [pltpu.VMEM((COUT, WIDE), F32)],
         mine, other,
     )
     return (
-        pooled.reshape(1, 2, NQ, COUT), d_features[None], d_weight, d_bias.reshape(COUT),
-        d_key, d_value, d_query,
+        pooled.reshape(1, 2, NQ, COUT), jnp.swapaxes(d_features, 1, 2)[None], d_weight.T,
+        d_bias.reshape(COUT), d_key, d_value, d_query,
     )
 
 

time: 123 us -> 102 us (0.83)
  blocking collectives: 56.9 us -> 39.3 us
  local copies, waits for them, and re-layouts: 14.6 us -> 4.54 us
  waiting for transfers between devices: 7.2 us -> 12.8 us
  Pallas kernels: 13.4 us -> 14.9 us
  other arithmetic: 1.4 us -> 0 us
    all_to_all x2 -> x1, blocking collectives: 40.4 us -> 24.7 us  [on_device(): mine = lax.all_to_all(copies, CHIPS, 0, 0, tiled=True).reshape(HALF, LANES)]
    unnamed x25 -> x24, local copies, waits for them, and re-layouts: 12.8 us -> 4.54 us
    all_to_all x1 -> x2, starting transfers between devices: 9.56 us -> 16.1 us  [the longest x1 9.43 us: on_device(): lax.all_to_all(early, SPACE, 0, 0, tiled=True).reshape(512, 3 * LANES)]
    ppermute x6 -> x5, starting transfers between devices: 14.6 us -> 11.7 us  [shift(): return lax.ppermute(shard, SPACE, pairs)]
    ppermute x1, starting transfers between devices: 2.95 us -> 0.67 us  [on_device(): other = lax.ppermute(mine, 'core', swap)]
    all_to_all x1 -> x2, waiting for transfers between devices: 0.01 us -> 1.93 us  [the longest x1 1.8 us: on_device(): lax.all_to_all(early, SPACE, 0, 0, tiled=True).reshape(512, 3 * LANES)]
    all_to_all x1, blocking collectives: 16.5 us -> 14.6 us  [on_device(): lax.all_to_all(send.reshape(32, 16, 256), SPACE, 0, 0, tiled=True)]
    ppermute x6 -> x5, waiting for transfers between devices: 5.57 us -> 7.31 us  [shift(): return lax.ppermute(shard, SPACE, pairs)]
  transfers between devices with their start and end apart: 9 -> 9, of which waited for: 2 -> 6; matrix products, arithmetic and copies ran while one was open for 5% -> 0% of each run, Pallas kernels for 3% -> 3%
where the time goes in v2:
time: 102 us; the launch traced here: 101 us
  blocking collectives  39.3 us (39%)
  starting transfers between devices  28.8 us (28%)
  Pallas kernels  14.9 us (15%)
  waiting for transfers between devices  12.8 us (13%)
  local copies, waits for them, and re-layouts  4.54 us (4%)
    all_to_all x1, blocking collectives, on_device(): mine = lax.all_to_all(copies, CHIPS, 0, 0, tiled=True).reshape(HALF, LANES)  24.7 us
    pallas_call x7, Pallas kernels, call(): pl.pallas_call(kernel, out_shape=outs, in_specs=in_specs, out_specs=jax.t...  14.9 us
    all_to_all x1, blocking collectives, on_device(): lax.all_to_all(send.reshape(32, 16, 256), SPACE, 0, 0, tiled=True)  14.6 us
    ppermute x5, starting transfers between devices, shift(): return lax.ppermute(shard, SPACE, pairs)  11.7 us
    all_to_all x1, starting transfers between devices, on_device(): lax.all_to_all(early, SPACE, 0, 0, tiled=True).reshape(512, 3 * LANES)  9.43 us
    ppermute x5, waiting for transfers between devices, shift(): return lax.ppermute(shard, SPACE, pairs)  7.31 us
    all_to_all x1, starting transfers between devices, on_device(): lax.all_to_all(half.reshape(64, SHARD, LANES), CHIPS, 0, 0, tiled=True)  6.66 us
    unnamed x24, local copies, waits for them, and re-layouts  4.54 us
  transfers between devices with their start and end apart: 9, of which 6 were waited for; matrix products, arithmetic and copies ran while one was open for 0% of the time, Pallas kernels for 3%

profile of v2, /device:TPU:1, one launch (start us, length us, event | category | flops | bytes accessed | tf_op | source)
XLA Modules:
  0.0 101.2 jit_solution(4370031421648955942)
XLA Ops:
  0.7 1.2 %copy-done.3 = bf16[1,8,512,96]{2,3,1,0:T(8,128)(2,1)S(1)} copy-done((bf16[1,8,512,96]{2,3,1,0:T(8,128)(2,1)S(1)}, bf16[1,8,512,96]{2,3,1,0:T(8,128)(2,1)}, u32[]{:S(2)}) %copy-start.3) | copy-done | bytes 786456
  1.8 0.7 copy-done.4
  3.2 0.7 copy-done.9
  4.0 1.9 %place_kernel.1 = (bf16[16,4,64,128]{3,2,1,0:T(8,128)(2,1)S(1)}, bf16[256,128]{1,0:T(8,128)(2,1)S(1)}, bf16[256,128]{1,0:T(8,128)(2,1)S(1)}, bf16[32,16,384]{2,1,0:T(8,128)(2,1)}) custom-call(s32[6,8]{1,0:T(8,128)S(1)} %copy-done.6, bf16[8,96,512]{2,1,0:T(8,128)(2,1)S(1)} %bitcast.25, s32[8,512]{1,0:T(8,128)S(1)} %bitcast.27, f32[16,192]{1,0:T(8,128)S(1)} %bitcast.29), custom_call_target="tpu_custom_call" | custom-call | tf_op jit(solution)/shard_map/place_kernel/pallas_call | solution.py:362
  5.9 9.4 %all-to-all-start = ((bf16[32,16,384]{2,1,0:T(8,128)(2,1)}), bf16[32,16,384]{2,1,0:T(8,128)(2,1)S(1)}, u32[]{:S(2)}, u32[]{:S(2)}) async-start(bf16[32,16,384]{2,1,0:T(8,128)(2,1)} %get-tuple-element.38), calls=%async_computation | async-start | bytes 786432 | tf_op jit(solution)/shard_map/all_to_all | solution.py:397
  15.3 3.5 %collective-permute-start = (bf16[256,128]{1,0:T(8,128)(2,1)S(1)}, bf16[256,128]{1,0:T(8,128)(2,1)S(1)}, u32[]{:S(2)}, u32[]{:S(2)}) collective-permute-start(bf16[256,128]{1,0:T(8,128)(2,1)S(1)} %get-tuple-element.36), channel_id=1, source_target_pairs={{0,1},{1,2},{2,3},{3,4},{4,5},{5,6},{6,7},{8,9},{9,10},{10,11},{11... | collective-permute-start | bytes 196616 | tf_op jit(solution)/shard_map/ppermute | solution.py:379
  18.9 3.1 %collective-permute-start.1 = (bf16[256,128]{1,0:T(8,128)(2,1)S(1)}, bf16[256,128]{1,0:T(8,128)(2,1)S(1)}, u32[]{:S(2)}, u32[]{:S(2)}) collective-permute-start(bf16[256,128]{1,0:T(8,128)(2,1)S(1)} %get-tuple-element.37), channel_id=1, source_target_pairs={{0,8},{1,9},{2,10},{3,11},{4,12},{5,13},{6,14},{7,15},{8,16},{9,17... | collective-permute-start | bytes 196616 | tf_op jit(solution)/shard_map/ppermute | solution.py:379
  22.0 1.8 %collective-permute-done.1.yr_ref = bf16[256,128]{1,0:T(8,128)(2,1)S(1)} collective-permute-done((bf16[256,128]{1,0:T(8,128)(2,1)S(1)}, bf16[256,128]{1,0:T(8,128)(2,1)S(1)}, u32[]{:S(2)}, u32[]{:S(2)}) %collective-permute-start.1) | collective-permute-done | bytes 65568 | tf_op jit(solution)/shard_map/ppermute | solution.py:379
  23.8 1.8 %all-to-all-done = bf16[32,16,384]{2,1,0:T(8,128)(2,1)S(1)} async-done(((bf16[32,16,384]{2,1,0:T(8,128)(2,1)}), bf16[32,16,384]{2,1,0:T(8,128)(2,1)S(1)}, u32[]{:S(2)}, u32[]{:S(2)}) %all-to-all-start) | async-done | bytes 393248 | tf_op jit(solution)/shard_map/all_to_all | solution.py:397
  25.7 1.2 %copy-done = bf16[2592,192]{0,1:T(8,128)(2,1)S(1)} copy-done((bf16[2592,192]{0,1:T(8,128)(2,1)S(1)}, bf16[2592,192]{0,1:T(8,128)(2,1)}, u32[]{:S(2)}) %copy-start) | copy-done | bytes 995352
  26.9 4.8 %forward_kernel.1 = (bf16[576,1152]{1,0:T(8,128)(2,1)S(1)}, bf16[512,1152]{1,0:T(8,128)(2,1)S(1)}, bf16[192,3456]{1,0:T(8,128)(2,1)S(1)}, f32[512,192]{1,0:T(8,1...) custom-call(s32[6,8]{1,0:T(8,128)S(1)} %copy-done.7, ...), custom_call_target="tpu_custom_call" | custom-call | tf_op jit(solution)/shard_map/forward_kernel/pallas_call | solution.py:362
  31.7 14.6 %all_to_all.20 = bf16[32,16,256]{2,1,0:T(8,128)(2,1)S(1)} all-to-all(bf16[32,16,256]{2,1,0:T(8,128)(2,1)S(1)} %bitcast.26), channel_id=1, replica_groups=mesh['section'=4,'chip'=16,'core'=2] {'chip','core'}, dimensions={0} | all-to-all | bytes 524288 | tf_op jit(solution)/shard_map/all_to_all | solution.py:411
  46.2 2.4 %backward_kernel.1 = (f32[16,192]{1,0:T(8,128)}, bf16[512,192]{1,0:T(8,128)(2,1)S(1)}, bf16[64,192]{1,0:T(8,128)(2,1)S(1)}, bf16[64,192]{1,0:T(8,128)(2,1)S(1)},...) custom-call(bf16[512,256]{1,0:T(8,128)(2,1)S(1)} %bitcast.23, bf16[576,1152]{1,0:T(8,128)(2,1)S(1)} %get-tuple-element.40.podd_ref, ...), custom_call_target="tpu_custom_call" | custom-call | tf_op jit(solution)/shard_map/backward_kernel/pallas_call | solution.py:362
  48.9 1.9 %collective-permute-done.2.b_ref = bf16[2560,128]{1,0:T(8,128)(2,1)S(1)} collective-permute-done((bf16[2560,128]{1,0:T(8,128)(2,1)S(1)}, bf16[2560,128]{1,0:T(8,128)(2,1)S(1)}, u32[]{:S(2)}, u32[]{:S(2)}) %collective-permute-start.2) | collective-permute-done | bytes 655392 | tf_op jit(solution)/shard_map/ppermute | solution.py:423
  50.8 1.0 add_kernel.1
  51.8 6.7 %all-to-all-start.2 = ((bf16[64,40,128]{2,1,0:T(8,128)(2,1)}), bf16[64,40,128]{2,1,0:T(8,128)(2,1)S(1)}, u32[]{:S(2)}, u32[]{:S(2)}) async-start(bf16[64,40,128]{2,1,0:T(8,128)(2,1)} %bitcast.11), calls=%async_computation.2 | async-start | bytes 1310720 | tf_op jit(solution)/shard_map/all_to_all | solution.py:425
  58.4 2.5 %collective-permute-start.3 = (bf16[64,192]{1,0:T(8,128)(2,1)S(1)}, bf16[64,192]{1,0:T(8,128)(2,1)S(1)}, u32[]{:S(2)}, u32[]{:S(2)}) collective-permute-start(bf16[64,192]{1,0:T(8,128)(2,1)S(1)} %get-tuple-element.53), channel_id=1, source_target_pairs={{1,0},{2,1},{3,2},{4,3},{5,4},{6,5},{7,6},{9,8},{10,9},{11,10},{12... | collective-permute-start | bytes 73736 | tf_op jit(solution)/shard_map/ppermute | solution.py:379
  61.0 1.3 %collective-permute-start.4 = (bf16[64,192]{1,0:T(8,128)(2,1)S(1)}, bf16[64,192]{1,0:T(8,128)(2,1)S(1)}, u32[]{:S(2)}, u32[]{:S(2)}) collective-permute-start(bf16[64,192]{1,0:T(8,128)(2,1)S(1)} %get-tuple-element.54), channel_id=1, source_target_pairs={{8,0},{9,1},{10,2},{11,3},{12,4},{13,5},{14,6},{15,7},{16,8},{17,9... | collective-permute-start | bytes 73736 | tf_op jit(solution)/shard_map/ppermute | solution.py:379
  62.3 1.3 %collective-permute-start.5 = (bf16[16,192]{1,0:T(8,128)(2,1)S(1)}, bf16[16,192]{1,0:T(8,128)(2,1)S(1)}, u32[]{:S(2)}, u32[]{:S(2)}) collective-permute-start(bf16[16,192]{1,0:T(8,128)(2,1)S(1)} %slice.3), channel_id=1, source_target_pairs={{9,0},{10,1},{11,2},{12,3},{13,4},{14,5},{15,6},{17,8},{18,9},{19,... | collective-permute-start | bytes 18440 | tf_op jit(solution)/shard_map/ppermute | solution.py:379
  63.6 5.5 %collective-permute-done.5.xyr_ref = bf16[16,192]{1,0:T(8,128)(2,1)S(1)} collective-permute-done((bf16[16,192]{1,0:T(8,128)(2,1)S(1)}, bf16[16,192]{1,0:T(8,128)(2,1)S(1)}, u32[]{:S(2)}, u32[]{:S(2)}) %collective-permute-start.5) | collective-permute-done | bytes 6176 | tf_op jit(solution)/shard_map/ppermute | solution.py:379
  69.1 3.2 %spread_kernel.1 = bf16[8,96,512]{2,1,0:T(8,128)(2,1)} custom-call(s32[6,8]{1,0:T(8,128)S(1)} %copy-done.7, bf16[512,192]{1,0:T(8,128)(2,1)S(1)} %get-tuple-element.52.db_ref, bf16[64,192]{1,0:T(8,128)(2,1)S(1)} %collective-permute-done.3.xr_ref, bf16[64,192]{1,0:T(8,128)(2,1)S(1)} %collective-permute-done.4.yr_ref, ...), custom_call_target="tpu_custom_call" | custom-call | tf_op jit(solution)/shard_map/spread_kernel/pallas_call | solution.py:362
  72.5 24.7 %all_to_all.21 = bf16[64,40,128]{2,1,0:T(8,128)(2,1)S(1)} all-to-all(bf16[64,40,128]{2,1,0:T(8,128)(2,1)S(1)} %total_kernel.1), channel_id=1, replica_groups=mesh['section'=4,'chip'=16,'core'=2] {'section','chip'}, dimensions={0} | all-to-all | bytes 1310720 | tf_op jit(solution)/shard_map/all_to_all | solution.py:439
  97.9 1.7 %collective-permute-done.6.other_ref = bf16[2560,128]{1,0:T(8,128)(2,1)S(1)} collective-permute-done((bf16[2560,128]{1,0:T(8,128)(2,1)S(1)}, bf16[2560,128]{1,0:T(8,128)(2,1)S(1)}, u32[]{:S(2)}, u32[]{:S(2)}) %collective-permute-start.6) | collective-permute-done | bytes 655392 | tf_op jit(solution)/shard_map/ppermute | solution.py:440
  99.6 1.6 %final_kernel.1 = (f32[192,2592]{1,0:T(8,128)}, f32[192,192]{1,0:T(8,128)}, f32[192,192]{1,0:T(8,128)}, f32[8,192]{1,0:T(8,128)}, f32[1,192]{1,0:T(1,128)}) custom-call(bf16[2560,128]{1,0:T(8,128)(2,1)S(1)} %bitcast.22, bf16[2560,128]{1,0:T(8,128)(2,1)S(1)} %collective-permute-done.6.other_ref), custom_call_target="tpu_custom_call" | custom-call | tf_op jit(solution)/shard_map/final_kernel/pallas_call | solution.py:362
  (28 shorter events, 2.0 us)
Async XLA Ops:
  0.6 25.0 %copy-start.2 = (f32[192,192]{1,0:T(8,128)S(1)}, f32[192,192]{1,0:T(8,128)}, u32[]{:S(2)}) copy-start(f32[192,192]{1,0:T(8,128)} %val_ref.3) | copy-start | bytes 442372
  0.6 25.0 %copy-start.1 = (f32[192,192]{1,0:T(8,128)S(1)}, f32[192,192]{1,0:T(8,128)}, u32[]{:S(2)}) copy-start(f32[192,192]{1,0:T(8,128)} %key_ref.3) | copy-start | bytes 442372
  0.7 1.2 %copy-start.3 = (bf16[1,8,512,96]{2,3,1,0:T(8,128)(2,1)S(1)}, bf16[1,8,512,96]{2,3,1,0:T(8,128)(2,1)}, u32[]{:S(2)}) copy-start(bf16[1,8,512,96]{2,3,1,0:T(8,128)(2,1)} %param.10) | copy-start | bytes 2359300
  1.8 0.7 copy-start.4
  2.6 0.7 copy-start.6
  3.2 0.7 copy-start.9
  4.0 21.7 %copy-start.7 = (s32[6,8]{1,0:T(8,128)S(1)}, s32[6,8]{1,0:T(8,128)}, u32[]{:S(2)}) copy-start(s32[6,8]{1,0:T(8,128)} %near_ref.5) | copy-start | bytes 580
  4.0 21.7 %copy-start.8 = (f32[8,192]{1,0:T(8,128)S(1)}, f32[8,192]{1,0:T(8,128)}, u32[]{:S(2)}) copy-start(f32[8,192]{1,0:T(8,128)} %query_ref.3) | copy-start | bytes 18436
  4.0 21.7 %copy-start.10 = (s32[1,512,1]{1,2,0:T(1,128)S(1)}, s32[1,512,1]{1,2,0:T(1,128)}, u32[]{:S(2)}) copy-start(s32[1,512,1]{1,2,0:T(1,128)} %param.13) | copy-start | bytes 6148
  4.0 21.7 %copy-start.11 = (f32[192]{0:T(256)S(1)}, f32[192]{0:T(256)}, u32[]{:S(2)}) copy-start(f32[192]{0:T(256)} %param.16) | copy-start | bytes 2308
  5.9 19.7 %all-to-all-start = ((bf16[32,16,384]{2,1,0:T(8,128)(2,1)}), bf16[32,16,384]{2,1,0:T(8,128)(2,1)S(1)}, u32[]{:S(2)}, u32[]{:S(2)}) async-start(bf16[32,16,384]{2,1,0:T(8,128)(2,1)} %get-tuple-element.38), calls=%async_computation | async-start | bytes 786432 | tf_op jit(solution)/shard_map/all_to_all | solution.py:397
  15.3 6.7 %collective-permute-start = (bf16[256,128]{1,0:T(8,128)(2,1)S(1)}, bf16[256,128]{1,0:T(8,128)(2,1)S(1)}, u32[]{:S(2)}, u32[]{:S(2)}) collective-permute-start(bf16[256,128]{1,0:T(8,128)(2,1)S(1)} %get-tuple-element.36), channel_id=1, source_target_pairs={{0,1},{1,2},{2,3},{3,4},{4,5},{5,6},{6,7},{8,9},{9,10},{10,11},{11... | collective-permute-start | bytes 196616 | tf_op jit(solution)/shard_map/ppermute | solution.py:379
  18.9 4.9 %collective-permute-start.1 = (bf16[256,128]{1,0:T(8,128)(2,1)S(1)}, bf16[256,128]{1,0:T(8,128)(2,1)S(1)}, u32[]{:S(2)}, u32[]{:S(2)}) collective-permute-start(bf16[256,128]{1,0:T(8,128)(2,1)S(1)} %get-tuple-element.37), channel_id=1, source_target_pairs={{0,8},{1,9},{2,10},{3,11},{4,12},{5,13},{6,14},{7,15},{8,16},{9,17... | collective-permute-start | bytes 196616 | tf_op jit(solution)/shard_map/ppermute | solution.py:379
  25.6 1.2 %copy-start = (bf16[2592,192]{0,1:T(8,128)(2,1)S(1)}, bf16[2592,192]{0,1:T(8,128)(2,1)}, u32[]{:S(2)}) copy-start(bf16[2592,192]{0,1:T(8,128)(2,1)} %param.15) | copy-start | bytes 2985988
  48.6 2.2 %collective-permute-start.2 = (bf16[2560,128]{1,0:T(8,128)(2,1)S(1)}, bf16[2560,128]{1,0:T(8,128)(2,1)S(1)}, u32[]{:S(2)}, u32[]{:S(2)}) collective-permute-start(bf16[2560,128]{1,0:T(8,128)(2,1)S(1)} %get-tuple-element.51), channel_id=1, source_target_pairs={{0,1},{1,0},{2,3},{3,2},{4,5},{5,4},{6,7},{7,6},{8,9},{9,8},{10,11... | collective-permute-start | bytes 1966088 | tf_op jit(solution)/shard_map/ppermute | solution.py:423
  50.8 18.3 %copy-start.5 = (s32[1,8,512]{2,1,0:T(8,128)S(1)}, s32[1,8,512]{2,1,0:T(8,128)}, u32[]{:S(2)}) copy-start(s32[1,8,512]{2,1,0:T(8,128)} %param.11) | copy-start | bytes 49156
  51.8 20.6 %all-to-all-start.2 = ((bf16[64,40,128]{2,1,0:T(8,128)(2,1)}), bf16[64,40,128]{2,1,0:T(8,128)(2,1)S(1)}, u32[]{:S(2)}, u32[]{:S(2)}) async-start(bf16[64,40,128]{2,1,0:T(8,128)(2,1)} %bitcast.11), calls=%async_computation.2 | async-start | bytes 1310720 | tf_op jit(solution)/shard_map/all_to_all | solution.py:425
  58.4 10.6 %collective-permute-start.3 = (bf16[64,192]{1,0:T(8,128)(2,1)S(1)}, bf16[64,192]{1,0:T(8,128)(2,1)S(1)}, u32[]{:S(2)}, u32[]{:S(2)}) collective-permute-start(bf16[64,192]{1,0:T(8,128)(2,1)S(1)} %get-tuple-element.53), channel_id=1, source_target_pairs={{1,0},{2,1},{3,2},{4,3},{5,4},{6,5},{7,6},{9,8},{10,9},{11,10},{12... | collective-permute-start | bytes 73736 | tf_op jit(solution)/shard_map/ppermute | solution.py:379
  61.0 8.1 %collective-permute-start.4 = (bf16[64,192]{1,0:T(8,128)(2,1)S(1)}, bf16[64,192]{1,0:T(8,128)(2,1)S(1)}, u32[]{:S(2)}, u32[]{:S(2)}) collective-permute-start(bf16[64,192]{1,0:T(8,128)(2,1)S(1)} %get-tuple-element.54), channel_id=1, source_target_pairs={{8,0},{9,1},{10,2},{11,3},{12,4},{13,5},{14,6},{15,7},{16,8},{17,9... | collective-permute-start | bytes 73736 | tf_op jit(solution)/shard_map/ppermute | solution.py:379
  62.3 6.8 %collective-permute-start.5 = (bf16[16,192]{1,0:T(8,128)(2,1)S(1)}, bf16[16,192]{1,0:T(8,128)(2,1)S(1)}, u32[]{:S(2)}, u32[]{:S(2)}) collective-permute-start(bf16[16,192]{1,0:T(8,128)(2,1)S(1)} %slice.3), channel_id=1, source_target_pairs={{9,0},{10,1},{11,2},{12,3},{13,4},{14,5},{15,6},{17,8},{18,9},{19,... | collective-permute-start | bytes 18440 | tf_op jit(solution)/shard_map/ppermute | solution.py:379
  97.2 2.4 %collective-permute-start.6 = (bf16[2560,128]{1,0:T(8,128)(2,1)S(1)}, bf16[2560,128]{1,0:T(8,128)(2,1)S(1)}, u32[]{:S(2)}, u32[]{:S(2)}) collective-permute-start(bf16[2560,128]{1,0:T(8,128)(2,1)S(1)} %bitcast.21), channel_id=1, source_target_pairs={{0,1},{1,0},{2,3},{3,2},{4,5},{5,4},{6,7},{7,6},{8,9},{9,8},{10,11... | collective-permute-start | bytes 1966088 | tf_op jit(solution)/shard_map/ppermute | solution.py:440

commit v3 on v2

--- a/solution.py
+++ b/solution.py
@@ -58,10 +58,23 @@
 
 
 def place_kernel(
-    near_ref, feat_ref, occ_ref, cot_ref, v_ref, xs_ref, ys_ref, early_ref, rows_ref, slot_ref
+    near_hbm, feat_hbm, occ_hbm, cot_hbm, v_ref, xs_ref, ys_ref, early_ref,
+    near_ref, feat_ref, occ_ref, cot_ref, rows_ref, slot_ref, sems,
 ):
+    copies = [
+        pltpu.make_async_copy(source, target, sems.at[i])
+        for i, (source, target) in enumerate(
+            (
+                (near_hbm, near_ref), (feat_hbm, feat_ref), (occ_hbm, occ_ref), (cot_hbm, cot_ref),
+            )
+        )
+    ]
+    for copy in copies:
+        copy.start()
+    rows_ref[...] = jnp.zeros_like(rows_ref)
+    for copy in copies:
+        copy.wait()
     find_slots(near_ref, slot_ref)
-    rows_ref[...] = jnp.zeros_like(rows_ref)
     for by in range(2):
         for bx in range(2):
             pair = []
@@ -93,15 +106,15 @@
 
 
 def forward_kernel(
-    near_ref, v_ref, xr_ref, yr_ref, w_ref, bias_ref, key_ref, val_ref, query_ref,
+    near_ref, w_hbm, v_ref, xr_ref, yr_ref, bias_ref, key_ref, val_ref, query_ref,
     routes_ref, early_ref,
     podd_ref, peven_ref, wp_ref, slope_ref, hid_ref, ku_ref, kn_ref, wt_ref, tt_ref, rr_ref,
-    send_ref, slot_ref, routes8_ref,
+    send_ref, slot_ref, routes8_ref, w_ref, sem,
 ):
+    fetch = pltpu.make_async_copy(w_hbm, w_ref, sem)
+    fetch.start()
     find_slots(near_ref, slot_ref)
     wp_ref[...] = jnp.zeros_like(wp_ref)
-    for tap in range(27):
-        wp_ref[:, pl.ds(tap * LANES, CIN)] = w_ref[:, pl.ds(tap * CIN, CIN)]
     here = lax.axis_index("chip") * 2 + lax.axis_index("core")
     inner = jnp.logical_and(here >= 8, lax.rem(here, 8) > 0)
     corner = early_ref[pl.ds(pl.multiple_of(16 * jnp.maximum(here - 9, 0), 16), 16), 256:384]
@@ -128,6 +141,9 @@
                     piece = jnp.where(first, 0.0, pltpu.roll(piece, 1, 0))
                 column = (3 * b + c) * LANES
                 out_ref[pl.ds(row, 64), pl.ds(column, LANES)] = piece.astype(BF16)
+    fetch.wait()
+    for tap in range(27):
+        wp_ref[:, pl.ds(tap * LANES, CIN)] = w_ref[:, pl.ds(tap * CIN, CIN)]
     before = (
         nt(podd_ref[0:512, :], wp_ref[:, 0:SLOTS9])
         + nt(peven_ref[...], wp_ref[:, SLOTS9 : 2 * SLOTS9])
@@ -349,16 +365,18 @@
     return pl.BlockSpec(memory_space=pltpu.VMEM)
 
 
-def sm():
-    return pl.BlockSpec(memory_space=pltpu.SMEM)
-
-
 def like(shape, dtype=F32):
     return jax.ShapeDtypeStruct(shape, dtype)
 
 
-def call(kernel, first_scalar, outs, scratch, *args):
-    in_specs = [sm() if i == 0 and first_scalar else vm() for i in range(len(args))]
+def call(kernel, kinds, outs, scratch, *args):
+    spaces = {"s": pltpu.SMEM, "h": pltpu.HBM, "v": pltpu.VMEM}
+    kinds = kinds + "v" * (len(args) - len(kinds))
+    in_specs = [pl.BlockSpec(memory_space=spaces[kind]) for kind in kinds]
+    args = [
+        pltpu.with_memory_space_constraint(arg, pltpu.HBM) if kind == "h" else arg
+        for arg, kind in zip(args, kinds, strict=True)
+    ]
     return pl.pallas_call(
         kernel,
         out_shape=outs,
@@ -386,31 +404,38 @@
     features, occupancy = jnp.swapaxes(features[0], 1, 2), occupancy[0]
     slots = pltpu.SMEM((8,), jnp.int32)
     v, xs, ys, early = call(
-        place_kernel, True,
+        place_kernel, "hhhh",
         [
             like((16, 4, 64, LANES), BF16), like((256, LANES), BF16), like((256, LANES), BF16),
             like((32, 16, 3 * LANES), BF16),
         ],
-        [pltpu.VMEM((1024, LANES), F32), slots],
+        [
+            pltpu.SMEM((6, 8), jnp.int32), pltpu.VMEM((8, CIN, 512), BF16),
+            pltpu.VMEM((8, 512), jnp.int32), pltpu.VMEM((16, COUT), F32),
+            pltpu.VMEM((1024, LANES), F32), slots, pltpu.SemaphoreType.DMA((4,)),
+        ],
         neighbors, features, occupancy, cotangent.reshape(16, COUT),
     )
     early = lax.all_to_all(early, SPACE, 0, 0, tiled=True).reshape(512, 3 * LANES)
     xr = shift(xs, 1, 0)
     yr = shift(ys, 0, 1)
     podd, peven, wp, slope, hid, ku, kn, wt, tt, rr, send = call(
-        forward_kernel, True,
+        forward_kernel, "sh",
         [
             like((576, SLOTS9), BF16), like((512, SLOTS9), BF16), like((COUT, 27 * LANES), BF16),
             like((512, COUT)), like((512, COUT), BF16), like((512, COUT)), like((512, 1)),
             like((8, 512)), like((8, 512)), like((8, 512)), like((512, 256), BF16),
         ],
-        [slots, pltpu.VMEM((8, 64), jnp.int32)],
-        neighbors, v, xr, yr, conv_weight.T, conv_bias.reshape(1, COUT), key_weight,
+        [
+            slots, pltpu.VMEM((8, 64), jnp.int32), pltpu.VMEM((COUT, KDIM), BF16),
+            pltpu.SemaphoreType.DMA,
+        ],
+        neighbors, conv_weight.T, v, xr, yr, conv_bias.reshape(1, COUT), key_weight,
         value_weight, queries, routes.reshape(1, 512), early,
     )
     recv = lax.all_to_all(send.reshape(32, 16, 256), SPACE, 0, 0, tiled=True).reshape(512, 256)
     pooled, db, bxs, bys, keep, give = call(
-        backward_kernel, False,
+        backward_kernel, "",
         [
             like((16, COUT)), like((512, COUT), BF16), like((64, COUT), BF16),
             like((64, COUT), BF16), like((HALF, LANES)), like((HALF, LANES), BF16),
@@ -421,25 +446,26 @@
     )
     swap = [(0, 1), (1, 0)]
     taken = lax.ppermute(give, "core", swap)
-    half = call(add_kernel, False, like((HALF, LANES), BF16), [], keep, taken)
+    half = call(add_kernel, "", like((HALF, LANES), BF16), [], keep, taken)
     pieces = lax.all_to_all(half.reshape(64, SHARD, LANES), CHIPS, 0, 0, tiled=True)
     bxr = shift(bxs, -1, 0)
     byr = shift(bys, 0, -1)
     bxyr = shift(bys[0:16], -1, -1)
+    copies = call(total_kernel, "", like((64, SHARD, LANES), BF16), [], pieces)
+    bxr, byr, bxyr, copies = lax.optimization_barrier((bxr, byr, bxyr, copies))
+    mine = lax.all_to_all(copies, CHIPS, 0, 0, tiled=True).reshape(HALF, LANES)
     d_features = call(
-        spread_kernel, True, like((8, CIN, 512), BF16),
+        spread_kernel, "s", like((8, CIN, 512), BF16),
         [
             pltpu.VMEM((648, COUT), F32), pltpu.VMEM((576, SLOTS9), F32),
             pltpu.VMEM((576, SLOTS9), F32), pltpu.VMEM((1024, LANES), F32), slots,
         ],
         neighbors, db, bxr, byr, bxyr, wp, occupancy,
     )
-    pieces, d_features = lax.optimization_barrier((pieces, d_features))
-    copies = call(total_kernel, False, like((64, SHARD, LANES), BF16), [], pieces)
-    mine = lax.all_to_all(copies, CHIPS, 0, 0, tiled=True).reshape(HALF, LANES)
+    mine, d_features = lax.optimization_barrier((mine, d_features))
     other = lax.ppermute(mine, "core", swap)
     d_weight, d_key, d_value, d_query, d_bias = call(
-        final_kernel, False,
+        final_kernel, "",
         [
             like((COUT, KDIM)), like((COUT, COUT)), like((COUT, COUT)), like((NQ, COUT)),
             like((1, COUT)),

time: 102 us -> 96 us (0.941)
  blocking collectives: 39.3 us -> 14.6 us
  waiting for transfers between devices: 12.8 us -> 26.7 us
  starting transfers between devices: 28.8 us -> 35.8 us
  local copies, waits for them, and re-layouts: 4.54 us -> 0.03 us
  Pallas kernels: 14.9 us -> 17.5 us
    all_to_all x1 -> x0, blocking collectives: 24.7 us -> none  [on_device(): mine = lax.all_to_all(copies, CHIPS, 0, 0, tiled=True).reshape(HALF, LANES)]
    all_to_all x0 -> x1, waiting for transfers between devices: none -> 10.7 us  [on_device(): mine = lax.all_to_all(copies, CHIPS, 0, 0, tiled=True).reshape(HALF, LANES)]
    all_to_all x1, waiting for transfers between devices: 0.14 us -> 8.79 us  [on_device(): lax.all_to_all(half.reshape(64, SHARD, LANES), CHIPS, 0, 0, tiled=True)]
    all_to_all x0 -> x1, starting transfers between devices: none -> 5.73 us  [on_device(): mine = lax.all_to_all(copies, CHIPS, 0, 0, tiled=True).reshape(HALF, LANES)]
    ppermute x5, waiting for transfers between devices: 7.31 us -> 1.82 us  [shift(): return lax.ppermute(shard, SPACE, pairs)]
    unnamed x24 -> x14, local copies, waits for them, and re-layouts: 4.54 us -> 0.03 us
    pallas_call x7, Pallas kernels: 14.9 us -> 17.5 us  [call(): pl.pallas_call(kernel, out_shape=outs, in_specs=in_specs, out_specs=jax.t...]
    ppermute x1, starting transfers between devices: 0.67 us -> 1.91 us  [on_device(): other = lax.ppermute(mine, 'core', swap)]
  transfers between devices with their start and end apart: 9 -> 10, of which waited for: 6 -> 6; matrix products, arithmetic and copies ran while one was open for 0% -> 0% of each run, Pallas kernels for 3% -> 4%
where the time goes in v3:
time: 96 us; the launch traced here: 95.4 us
  starting transfers between devices  35.8 us (37%)
  waiting for transfers between devices  26.7 us (28%)
  Pallas kernels  17.5 us (18%)
  blocking collectives  14.6 us (15%)
    pallas_call x7, Pallas kernels, call(): pl.pallas_call(kernel, out_shape=outs, in_specs=in_specs, out_specs=jax.t...  17.5 us
    all_to_all x1, blocking collectives, on_device(): lax.all_to_all(send.reshape(32, 16, 256), SPACE, 0, 0, tiled=True)  14.6 us
    ppermute x5, starting transfers between devices, shift(): return lax.ppermute(shard, SPACE, pairs)  11.7 us
    all_to_all x1, waiting for transfers between devices, on_device(): mine = lax.all_to_all(copies, CHIPS, 0, 0, tiled=True).reshape(HALF, LANES)  10.7 us
    all_to_all x1, starting transfers between devices, on_device(): lax.all_to_all(early, SPACE, 0, 0, tiled=True).reshape(512, 3 * LANES)  9.45 us
    all_to_all x1, waiting for transfers between devices, on_device(): lax.all_to_all(half.reshape(64, SHARD, LANES), CHIPS, 0, 0, tiled=True)  8.79 us
    all_to_all x1, starting transfers between devices, on_device(): lax.all_to_all(half.reshape(64, SHARD, LANES), CHIPS, 0, 0, tiled=True)  6.66 us
    all_to_all x1, starting transfers between devices, on_device(): mine = lax.all_to_all(copies, CHIPS, 0, 0, tiled=True).reshape(HALF, LANES)  5.73 us
  transfers between devices with their start and end apart: 10, of which 6 were waited for; matrix products, arithmetic and copies ran while one was open for 0% of the time, Pallas kernels for 4%

profile of v3, /device:TPU:1, one launch (start us, length us, event | category | flops | bytes accessed | tf_op | source)
XLA Modules:
  0.0 95.4 jit_solution(4289628241796453963)
XLA Ops:
  0.7 2.5 %place_kernel.1 = (bf16[16,4,64,128]{3,2,1,0:T(8,128)(2,1)S(1)}, bf16[256,128]{1,0:T(8,128)(2,1)S(1)}, bf16[256,128]{1,0:T(8,128)(2,1)S(1)}, bf16[32,16,384]{2,1,0:T(8,128)(2,1)}) custom-call(s32[6,8]{1,0:T(8,128)} %near_ref.3, bf16[8,96,512]{2,1,0:T(8,128)(2,1)} %bitcast.30, s32[8,512]{1,0:T(8,128)} %bitcast.25, f32[16,192]{1,0:T(8,128)} %bitcast.32), custom_call_target="tpu_custom_call" | custom-call | tf_op jit(solution)/shard_map/place_kernel/pallas_call | solution.py:380
  3.2 9.4 %all-to-all-start = ((bf16[32,16,384]{2,1,0:T(8,128)(2,1)}), bf16[32,16,384]{2,1,0:T(8,128)(2,1)S(1)}, u32[]{:S(2)}, u32[]{:S(2)}) async-start(bf16[32,16,384]{2,1,0:T(8,128)(2,1)} %get-tuple-element.42), calls=%async_computation | async-start | bytes 786432 | tf_op jit(solution)/shard_map/all_to_all | solution.py:419
  12.6 3.5 %collective-permute-start = (bf16[256,128]{1,0:T(8,128)(2,1)S(1)}, bf16[256,128]{1,0:T(8,128)(2,1)S(1)}, u32[]{:S(2)}, u32[]{:S(2)}) collective-permute-start(bf16[256,128]{1,0:T(8,128)(2,1)S(1)} %get-tuple-element.40), channel_id=1, source_target_pairs={{0,1},{1,2},{2,3},{3,4},{4,5},{5,6},{6,7},{8,9},{9,10},{10,11},{11... | collective-permute-start | bytes 196616 | tf_op jit(solution)/shard_map/ppermute | solution.py:397
  16.2 3.1 %collective-permute-start.1 = (bf16[256,128]{1,0:T(8,128)(2,1)S(1)}, bf16[256,128]{1,0:T(8,128)(2,1)S(1)}, u32[]{:S(2)}, u32[]{:S(2)}) collective-permute-start(bf16[256,128]{1,0:T(8,128)(2,1)S(1)} %get-tuple-element.41), channel_id=1, source_target_pairs={{0,8},{1,9},{2,10},{3,11},{4,12},{5,13},{6,14},{7,15},{8,16},{9,17... | collective-permute-start | bytes 196616 | tf_op jit(solution)/shard_map/ppermute | solution.py:397
  19.3 1.8 %collective-permute-done.1.yr_ref = bf16[256,128]{1,0:T(8,128)(2,1)S(1)} collective-permute-done((bf16[256,128]{1,0:T(8,128)(2,1)S(1)}, bf16[256,128]{1,0:T(8,128)(2,1)S(1)}, u32[]{:S(2)}, u32[]{:S(2)}) %collective-permute-start.1) | collective-permute-done | bytes 65568 | tf_op jit(solution)/shard_map/ppermute | solution.py:397
  21.1 1.8 %all-to-all-done = bf16[32,16,384]{2,1,0:T(8,128)(2,1)S(1)} async-done(((bf16[32,16,384]{2,1,0:T(8,128)(2,1)}), bf16[32,16,384]{2,1,0:T(8,128)(2,1)S(1)}, u32[]{:S(2)}, u32[]{:S(2)}) %all-to-all-start) | async-done | bytes 393248 | tf_op jit(solution)/shard_map/all_to_all | solution.py:419
  23.0 5.9 %forward_kernel.1 = (bf16[576,1152]{1,0:T(8,128)(2,1)S(1)}, bf16[512,1152]{1,0:T(8,128)(2,1)S(1)}, bf16[192,3456]{1,0:T(8,128)(2,1)S(1)}, f32[512,192]{1,0:T(8,1...) custom-call(s32[6,8]{1,0:T(8,128)S(1)} %copy-done.3, ...), custom_call_target="tpu_custom_call" | custom-call | tf_op jit(solution)/shard_map/forward_kernel/pallas_call | solution.py:380
  28.9 14.6 %all_to_all.20 = bf16[32,16,256]{2,1,0:T(8,128)(2,1)S(1)} all-to-all(bf16[32,16,256]{2,1,0:T(8,128)(2,1)S(1)} %bitcast.24), channel_id=1, replica_groups=mesh['section'=4,'chip'=16,'core'=2] {'chip','core'}, dimensions={0} | all-to-all | bytes 524288 | tf_op jit(solution)/shard_map/all_to_all | solution.py:436
  43.5 2.4 %backward_kernel.1 = (f32[16,192]{1,0:T(8,128)}, bf16[512,192]{1,0:T(8,128)(2,1)S(1)}, bf16[64,192]{1,0:T(8,128)(2,1)S(1)}, bf16[64,192]{1,0:T(8,128)(2,1)S(1)},...) custom-call(bf16[512,256]{1,0:T(8,128)(2,1)S(1)} %bitcast.23, bf16[576,1152]{1,0:T(8,128)(2,1)S(1)} %get-tuple-element.44.podd_ref, ...), custom_call_target="tpu_custom_call" | custom-call | tf_op jit(solution)/shard_map/backward_kernel/pallas_call | solution.py:380
  45.9 0.3 collective-permute-start.5
  46.2 1.9 %collective-permute-done.5.b_ref = bf16[2560,128]{1,0:T(8,128)(2,1)S(1)} collective-permute-done((bf16[2560,128]{1,0:T(8,128)(2,1)S(1)}, bf16[2560,128]{1,0:T(8,128)(2,1)S(1)}, u32[]{:S(2)}, u32[]{:S(2)}) %collective-permute-start.5) | collective-permute-done | bytes 655392 | tf_op jit(solution)/shard_map/ppermute | solution.py:448
  48.0 1.0 %add_kernel.1 = bf16[2560,128]{1,0:T(8,128)(2,1)} custom-call(f32[2560,128]{1,0:T(8,128)S(1)} %get-tuple-element.56.a_ref, bf16[2560,128]{1,0:T(8,128)(2,1)S(1)} %collective-permute-done.5.b_ref), custom_call_target="tpu_custom_call" | custom-call | tf_op jit(solution)/shard_map/add_kernel/pallas_call | solution.py:380
  49.0 6.7 %all-to-all-start.2 = ((bf16[64,40,128]{2,1,0:T(8,128)(2,1)}), bf16[64,40,128]{2,1,0:T(8,128)(2,1)S(1)}, u32[]{:S(2)}, u32[]{:S(2)}) async-start(bf16[64,40,128]{2,1,0:T(8,128)(2,1)} %bitcast.11), calls=%async_computation.2 | async-start | bytes 1310720 | tf_op jit(solution)/shard_map/all_to_all | solution.py:450
  55.7 2.5 %collective-permute-start.2 = (bf16[64,192]{1,0:T(8,128)(2,1)S(1)}, bf16[64,192]{1,0:T(8,128)(2,1)S(1)}, u32[]{:S(2)}, u32[]{:S(2)}) collective-permute-start(bf16[64,192]{1,0:T(8,128)(2,1)S(1)} %get-tuple-element.54), channel_id=1, source_target_pairs={{1,0},{2,1},{3,2},{4,3},{5,4},{6,5},{7,6},{9,8},{10,9},{11,10},{12... | collective-permute-start | bytes 73736 | tf_op jit(solution)/shard_map/ppermute | solution.py:397
  58.2 1.3 %collective-permute-start.3 = (bf16[64,192]{1,0:T(8,128)(2,1)S(1)}, bf16[64,192]{1,0:T(8,128)(2,1)S(1)}, u32[]{:S(2)}, u32[]{:S(2)}) collective-permute-start(bf16[64,192]{1,0:T(8,128)(2,1)S(1)} %get-tuple-element.55), channel_id=1, source_target_pairs={{8,0},{9,1},{10,2},{11,3},{12,4},{13,5},{14,6},{15,7},{16,8},{17,9... | collective-permute-start | bytes 73736 | tf_op jit(solution)/shard_map/ppermute | solution.py:397
  59.5 1.3 %collective-permute-start.4 = (bf16[16,192]{1,0:T(8,128)(2,1)S(1)}, bf16[16,192]{1,0:T(8,128)(2,1)S(1)}, u32[]{:S(2)}, u32[]{:S(2)}) collective-permute-start(bf16[16,192]{1,0:T(8,128)(2,1)S(1)} %slice.3), channel_id=1, source_target_pairs={{9,0},{10,1},{11,2},{12,3},{13,4},{14,5},{15,6},{17,8},{18,9},{19,... | collective-permute-start | bytes 18440 | tf_op jit(solution)/shard_map/ppermute | solution.py:397
  60.8 8.8 %all-to-all-done.2.recv_ref = bf16[64,40,128]{2,1,0:T(8,128)(2,1)S(1)} async-done(((bf16[64,40,128]{2,1,0:T(8,128)(2,1)}), bf16[64,40,128]{2,1,0:T(8,128)(2,1)S(1)}, u32[]{:S(2)}, u32[]{:S(2)}) %all-to-all-start.2) | async-done | bytes 655392 | tf_op jit(solution)/shard_map/all_to_all | solution.py:450
  69.6 1.0 %total_kernel.1 = bf16[64,40,128]{2,1,0:T(8,128)(2,1)} custom-call(bf16[64,40,128]{2,1,0:T(8,128)(2,1)S(1)} %all-to-all-done.2.recv_ref), custom_call_target="tpu_custom_call" | custom-call | tf_op jit(solution)/shard_map/total_kernel/pallas_call | solution.py:380
  70.6 5.7 %all-to-all-start.3 = ((bf16[64,40,128]{2,1,0:T(8,128)(2,1)}), bf16[64,40,128]{2,1,0:T(8,128)(2,1)S(1)}, u32[]{:S(2)}, u32[]{:S(2)}) async-start(bf16[64,40,128]{2,1,0:T(8,128)(2,1)} %total_kernel.1), calls=%async_computation.3 | async-start | bytes 1310720 | tf_op jit(solution)/shard_map/all_to_all | solution.py:456
  76.3 3.2 %spread_kernel.1 = bf16[8,96,512]{2,1,0:T(8,128)(2,1)} custom-call(s32[6,8]{1,0:T(8,128)S(1)} %copy-done.3, bf16[512,192]{1,0:T(8,128)(2,1)S(1)} %get-tuple-element.59.db_ref, bf16[64,192]{1,0:T(8,128)(2,1)S(1)} %collective-permute-done.2.xr_ref, bf16[64,192]{1,0:T(8,128)(2,1)S(1)} %collective-permute-done.3.yr_ref, ...), custom_call_target="tpu_custom_call" | custom-call | tf_op jit(solution)/shard_map/spread_kernel/pallas_call | solution.py:380
  79.5 10.7 %all-to-all-done.3 = bf16[64,40,128]{2,1,0:T(8,128)(2,1)S(1)} async-done(((bf16[64,40,128]{2,1,0:T(8,128)(2,1)}), bf16[64,40,128]{2,1,0:T(8,128)(2,1)S(1)}, u32[]{:S(2)}, u32[]{:S(2)}) %all-to-all-start.3) | async-done | bytes 655392 | tf_op jit(solution)/shard_map/all_to_all | solution.py:456
  90.2 1.9 %collective-permute-start.6 = (bf16[2560,128]{1,0:T(8,128)(2,1)S(1)}, bf16[2560,128]{1,0:T(8,128)(2,1)S(1)}, u32[]{:S(2)}, u32[]{:S(2)}) collective-permute-start(bf16[2560,128]{1,0:T(8,128)(2,1)S(1)} %bitcast.21), channel_id=1, source_target_pairs={{0,1},{1,0},{2,3},{3,2},{4,5},{5,4},{6,7},{7,6},{8,9},{9,8},{10,11... | collective-permute-start | bytes 1966088 | tf_op jit(solution)/shard_map/ppermute | solution.py:466
  92.1 1.7 %collective-permute-done.6.other_ref = bf16[2560,128]{1,0:T(8,128)(2,1)S(1)} collective-permute-done((bf16[2560,128]{1,0:T(8,128)(2,1)S(1)}, bf16[2560,128]{1,0:T(8,128)(2,1)S(1)}, u32[]{:S(2)}, u32[]{:S(2)}) %collective-permute-start.6) | collective-permute-done | bytes 655392 | tf_op jit(solution)/shard_map/ppermute | solution.py:466
  93.8 1.6 %final_kernel.1 = (f32[192,2592]{1,0:T(8,128)}, f32[192,192]{1,0:T(8,128)}, f32[192,192]{1,0:T(8,128)}, f32[8,192]{1,0:T(8,128)}, f32[1,192]{1,0:T(1,128)}) custom-call(bf16[2560,128]{1,0:T(8,128)(2,1)S(1)} %bitcast.22, bf16[2560,128]{1,0:T(8,128)(2,1)S(1)} %collective-permute-done.6.other_ref), custom_call_target="tpu_custom_call" | custom-call | tf_op jit(solution)/shard_map/final_kernel/pallas_call | solution.py:380
  (19 shorter events, 0.0 us)
Async XLA Ops:
  0.6 22.3 %copy-start.3 = (s32[6,8]{1,0:T(8,128)S(1)}, s32[6,8]{1,0:T(8,128)}, u32[]{:S(2)}) copy-start(s32[6,8]{1,0:T(8,128)} %near_ref.3) | copy-start | bytes 580
  0.6 22.3 %copy-start.4 = (f32[8,192]{1,0:T(8,128)S(1)}, f32[8,192]{1,0:T(8,128)}, u32[]{:S(2)}) copy-start(f32[8,192]{1,0:T(8,128)} %query_ref.3) | copy-start | bytes 18436
  0.7 22.3 %copy-start.1 = (f32[192,192]{1,0:T(8,128)S(1)}, f32[192,192]{1,0:T(8,128)}, u32[]{:S(2)}) copy-start(f32[192,192]{1,0:T(8,128)} %val_ref.3) | copy-start | bytes 442372
  0.7 22.3 %copy-start = (f32[192,192]{1,0:T(8,128)S(1)}, f32[192,192]{1,0:T(8,128)}, u32[]{:S(2)}) copy-start(f32[192,192]{1,0:T(8,128)} %key_ref.3) | copy-start | bytes 442372
  0.7 22.3 %copy-start.6 = (f32[192]{0:T(256)S(1)}, f32[192]{0:T(256)}, u32[]{:S(2)}) copy-start(f32[192]{0:T(256)} %param.16) | copy-start | bytes 2308
  0.7 22.3 %copy-start.5 = (s32[1,512,1]{1,2,0:T(1,128)S(1)}, s32[1,512,1]{1,2,0:T(1,128)}, u32[]{:S(2)}) copy-start(s32[1,512,1]{1,2,0:T(1,128)} %param.13) | copy-start | bytes 6148
  3.2 19.7 %all-to-all-start = ((bf16[32,16,384]{2,1,0:T(8,128)(2,1)}), bf16[32,16,384]{2,1,0:T(8,128)(2,1)S(1)}, u32[]{:S(2)}, u32[]{:S(2)}) async-start(bf16[32,16,384]{2,1,0:T(8,128)(2,1)} %get-tuple-element.42), calls=%async_computation | async-start | bytes 786432 | tf_op jit(solution)/shard_map/all_to_all | solution.py:419
  12.6 6.7 %collective-permute-start = (bf16[256,128]{1,0:T(8,128)(2,1)S(1)}, bf16[256,128]{1,0:T(8,128)(2,1)S(1)}, u32[]{:S(2)}, u32[]{:S(2)}) collective-permute-start(bf16[256,128]{1,0:T(8,128)(2,1)S(1)} %get-tuple-element.40), channel_id=1, source_target_pairs={{0,1},{1,2},{2,3},{3,4},{4,5},{5,6},{6,7},{8,9},{9,10},{10,11},{11... | collective-permute-start | bytes 196616 | tf_op jit(solution)/shard_map/ppermute | solution.py:397
  16.2 4.9 %collective-permute-start.1 = (bf16[256,128]{1,0:T(8,128)(2,1)S(1)}, bf16[256,128]{1,0:T(8,128)(2,1)S(1)}, u32[]{:S(2)}, u32[]{:S(2)}) collective-permute-start(bf16[256,128]{1,0:T(8,128)(2,1)S(1)} %get-tuple-element.41), channel_id=1, source_target_pairs={{0,8},{1,9},{2,10},{3,11},{4,12},{5,13},{6,14},{7,15},{8,16},{9,17... | collective-permute-start | bytes 196616 | tf_op jit(solution)/shard_map/ppermute | solution.py:397
  45.9 2.2 %collective-permute-start.5 = (bf16[2560,128]{1,0:T(8,128)(2,1)S(1)}, bf16[2560,128]{1,0:T(8,128)(2,1)S(1)}, u32[]{:S(2)}, u32[]{:S(2)}) collective-permute-start(bf16[2560,128]{1,0:T(8,128)(2,1)S(1)} %get-tuple-element.57), channel_id=1, source_target_pairs={{0,1},{1,0},{2,3},{3,2},{4,5},{5,4},{6,7},{7,6},{8,9},{9,8},{10,11... | collective-permute-start | bytes 1966088 | tf_op jit(solution)/shard_map/ppermute | solution.py:448
  49.0 20.6 %all-to-all-start.2 = ((bf16[64,40,128]{2,1,0:T(8,128)(2,1)}), bf16[64,40,128]{2,1,0:T(8,128)(2,1)S(1)}, u32[]{:S(2)}, u32[]{:S(2)}) async-start(bf16[64,40,128]{2,1,0:T(8,128)(2,1)} %bitcast.11), calls=%async_computation.2 | async-start | bytes 1310720 | tf_op jit(solution)/shard_map/all_to_all | solution.py:450
  55.7 20.6 %copy-start.2 = (s32[1,8,512]{2,1,0:T(8,128)S(1)}, s32[1,8,512]{2,1,0:T(8,128)}, u32[]{:S(2)}) copy-start(s32[1,8,512]{2,1,0:T(8,128)} %param.11) | copy-start | bytes 49156
  55.7 14.9 %collective-permute-start.2 = (bf16[64,192]{1,0:T(8,128)(2,1)S(1)}, bf16[64,192]{1,0:T(8,128)(2,1)S(1)}, u32[]{:S(2)}, u32[]{:S(2)}) collective-permute-start(bf16[64,192]{1,0:T(8,128)(2,1)S(1)} %get-tuple-element.54), channel_id=1, source_target_pairs={{1,0},{2,1},{3,2},{4,3},{5,4},{6,5},{7,6},{9,8},{10,9},{11,10},{12... | collective-permute-start | bytes 73736 | tf_op jit(solution)/shard_map/ppermute | solution.py:397
  58.2 12.4 %collective-permute-start.3 = (bf16[64,192]{1,0:T(8,128)(2,1)S(1)}, bf16[64,192]{1,0:T(8,128)(2,1)S(1)}, u32[]{:S(2)}, u32[]{:S(2)}) collective-permute-start(bf16[64,192]{1,0:T(8,128)(2,1)S(1)} %get-tuple-element.55), channel_id=1, source_target_pairs={{8,0},{9,1},{10,2},{11,3},{12,4},{13,5},{14,6},{15,7},{16,8},{17,9... | collective-permute-start | bytes 73736 | tf_op jit(solution)/shard_map/ppermute | solution.py:397
  59.5 11.1 %collective-permute-start.4 = (bf16[16,192]{1,0:T(8,128)(2,1)S(1)}, bf16[16,192]{1,0:T(8,128)(2,1)S(1)}, u32[]{:S(2)}, u32[]{:S(2)}) collective-permute-start(bf16[16,192]{1,0:T(8,128)(2,1)S(1)} %slice.3), channel_id=1, source_target_pairs={{9,0},{10,1},{11,2},{12,3},{13,4},{14,5},{15,6},{17,8},{18,9},{19,... | collective-permute-start | bytes 18440 | tf_op jit(solution)/shard_map/ppermute | solution.py:397
  70.6 19.6 %all-to-all-start.3 = ((bf16[64,40,128]{2,1,0:T(8,128)(2,1)}), bf16[64,40,128]{2,1,0:T(8,128)(2,1)S(1)}, u32[]{:S(2)}, u32[]{:S(2)}) async-start(bf16[64,40,128]{2,1,0:T(8,128)(2,1)} %total_kernel.1), calls=%async_computation.3 | async-start | bytes 1310720 | tf_op jit(solution)/shard_map/all_to_all | solution.py:456
  90.2 3.6 %collective-permute-start.6 = (bf16[2560,128]{1,0:T(8,128)(2,1)S(1)}, bf16[2560,128]{1,0:T(8,128)(2,1)S(1)}, u32[]{:S(2)}, u32[]{:S(2)}) collective-permute-start(bf16[2560,128]{1,0:T(8,128)(2,1)S(1)} %bitcast.21), channel_id=1, source_target_pairs={{0,1},{1,0},{2,3},{3,2},{4,5},{5,4},{6,7},{7,6},{8,9},{9,8},{10,11... | collective-permute-start | bytes 1966088 | tf_op jit(solution)/shard_map/ppermute | solution.py:466

commit v4 on v3

--- a/solution.py
+++ b/solution.py
@@ -20,6 +20,7 @@
 F32, BF16 = jnp.float32, jnp.bfloat16
 SPACE = ("chip", "core")
 CHIPS = ("section", "chip")
+ROOT, CUBIC = 0.7978845608028654, 0.044715
 VMEM_LIMIT = 44 * 1024 * 1024
 
 
@@ -105,16 +106,55 @@
     early_ref[...] = jnp.broadcast_to(early[None], early_ref.shape)
 
 
-def forward_kernel(
-    near_ref, w_hbm, v_ref, xr_ref, yr_ref, bias_ref, key_ref, val_ref, query_ref,
-    routes_ref, early_ref,
-    podd_ref, peven_ref, wp_ref, slope_ref, hid_ref, ku_ref, kn_ref, wt_ref, tt_ref, rr_ref,
-    send_ref, slot_ref, routes8_ref, w_ref, sem,
+def prepare_kernel(
+    near_ref, w_hbm, routes_ref,
+    wp_ref, group_ref,
+    slot_ref, routes8_ref, w_ref, sem,
 ):
     fetch = pltpu.make_async_copy(w_hbm, w_ref, sem)
     fetch.start()
     find_slots(near_ref, slot_ref)
     wp_ref[...] = jnp.zeros_like(wp_ref)
+    for slot in range(8):
+        routes8_ref[slot : slot + 1, :] = routes_ref[:, 64 * slot : 64 * slot + 64]
+    routes = jnp.concatenate(
+        [routes8_ref[pl.ds(slot_ref[p], 1), :] for p in range(8)], axis=0
+    ).astype(BF16)
+    row = lax.broadcasted_iota(jnp.int32, (64, 512), 1)
+    inside = ((row >> 6) & 3) * 16 + ((row >> 3) & 3) * 4 + (row & 3)
+    pick = (inside == lax.broadcasted_iota(jnp.int32, (64, 512), 0)).astype(F32).astype(BF16)
+    spread = nn(routes, pick)
+    row = lax.broadcasted_iota(jnp.int32, (8, 512), 1)
+    place = (row >> 8) + ((row >> 5) & 1) * 2 + ((row >> 2) & 1) * 4
+    mine = place == lax.broadcasted_iota(jnp.int32, (8, 512), 0)
+    group = jnp.sum(jnp.where(mine, spread, 0.0), axis=0, keepdims=True)
+    group_ref[...] = jnp.broadcast_to(group, (8, 512))
+
+    fetch.wait()
+    for tap in range(27):
+        wp_ref[:, pl.ds(tap * LANES, CIN)] = w_ref[:, pl.ds(tap * CIN, CIN)]
+
+
+def shared_out(group, amounts):
+    return jnp.concatenate(
+        [jnp.where(group == float(g), amounts, 0.0) for g in range(GROUPS)], axis=0
+    ).astype(BF16)
+
+
+def forward_kernel(
+    key_hbm, val_hbm, query_hbm, v_ref, xr_ref, yr_ref, bias_ref, wp_ref, group_ref, early_ref,
+    podd_ref, peven_ref, slope_ref, hidt_ref, cott_ref, kut_ref, knt_ref, wt_ref, tt_ref, kt_ref,
+    vw_ref, send_ref,
+    key_ref, val_ref, query_ref, sems,
+):
+    copies = [
+        pltpu.make_async_copy(source, target, sems.at[i])
+        for i, (source, target) in enumerate(
+            ((key_hbm, key_ref), (val_hbm, val_ref), (query_hbm, query_ref))
+        )
+    ]
+    for copy in copies:
+        copy.start()
     here = lax.axis_index("chip") * 2 + lax.axis_index("core")
     inner = jnp.logical_and(here >= 8, lax.rem(here, 8) > 0)
     corner = early_ref[pl.ds(pl.multiple_of(16 * jnp.maximum(here - 9, 0), 16), 16), 256:384]
@@ -122,11 +162,9 @@
     first = lax.broadcasted_iota(jnp.int32, (64, LANES), 0) % 8 == 0
     for x in range(-1, 16):
         if x < 0:
-            planes = xr_ref[...].astype(F32).reshape(4, 64, LANES)
-            edge = corner
+            planes, edge = xr_ref[...].astype(F32).reshape(4, 64, LANES), corner
         else:
-            planes = v_ref[x].astype(F32)
-            edge = yr_ref[pl.ds(16 * x, 16), :].astype(F32)
+            planes, edge = v_ref[x].astype(F32), yr_ref[pl.ds(16 * x, 16), :].astype(F32)
         if x % 2 == 0:
             out_ref, row = peven_ref, 32 * x
         else:
@@ -141,61 +179,52 @@
                     piece = jnp.where(first, 0.0, pltpu.roll(piece, 1, 0))
                 column = (3 * b + c) * LANES
                 out_ref[pl.ds(row, 64), pl.ds(column, LANES)] = piece.astype(BF16)
-    fetch.wait()
-    for tap in range(27):
-        wp_ref[:, pl.ds(tap * LANES, CIN)] = w_ref[:, pl.ds(tap * CIN, CIN)]
     before = (
         nt(podd_ref[0:512, :], wp_ref[:, 0:SLOTS9])
         + nt(peven_ref[...], wp_ref[:, SLOTS9 : 2 * SLOTS9])
         + nt(podd_ref[64:576, :], wp_ref[:, 2 * SLOTS9 : 3 * SLOTS9])
         + bias_ref[...]
     )
-    root = 0.7978845608028654
     square = before * before
-    tanh = jnp.tanh(root * before * (1.0 + 0.044715 * square))
+    tanh = jnp.tanh(ROOT * before * (1.0 + CUBIC * square))
     hidden = (0.5 * before * (1.0 + tanh)).astype(BF16)
-    slope_ref[...] = 0.5 * (1.0 + tanh) + 0.5 * before * (1.0 - tanh * tanh) * root * (
-        1.0 + 3.0 * 0.044715 * square
-    )
-    hid_ref[...] = hidden
-
-    kh, kl = split(key_ref[...])
+    slope = 0.5 * (1.0 + tanh) + 0.5 * before * (1.0 - tanh * tanh) * ROOT * (
+        1.0 + 3.0 * CUBIC * square
+    )
+    slope_ref[...] = slope.T
+    hidt_ref[...] = hidden.astype(F32).T.astype(BF16)
+
+    for copy in copies:
+        copy.wait()
+    kh, kl = split(key_ref[...].T)
     vh, vl = split(val_ref[...])
-    keys = nn(hidden, kh) + nn(hidden, kl)
+    kt_ref[0:COUT, :] = kh
+    kt_ref[COUT : 2 * COUT, :] = kl
+    vw_ref[0:COUT, :] = vh
+    vw_ref[COUT : 2 * COUT, :] = vl
+    keys = nt(kh, hidden) + nt(kl, hidden)
     values = nn(hidden, vh) + nn(hidden, vl)
-    key_norm = lax.rsqrt(jnp.sum(keys * keys, axis=-1, keepdims=True) + EPS)
-    ku = keys * key_norm
-    ku_ref[...] = ku
-    kn_ref[...] = key_norm
     queries = query_ref[...]
     qu = queries * lax.rsqrt(jnp.sum(queries * queries, axis=-1, keepdims=True) + EPS)
-    uh, ul = split(ku)
+    key_norm = lax.rsqrt(jnp.sum(keys * keys, axis=0, keepdims=True) + EPS)
+    kut = keys * key_norm
+    kut_ref[...] = kut
+    knt_ref[...] = jnp.broadcast_to(key_norm, (8, 512))
+    uh, ul = split(kut)
     qh, ql = split(qu)
-    weights = jnp.exp(TEMPER * (nt(qh, uh) + nt(ql, uh) + nt(qh, ul)))
+    weights = jnp.exp(TEMPER * (nn(qh, uh) + nn(ql, uh) + nn(qh, ul)))
     wt_ref[...] = weights
-
-    for slot in range(8):
-        routes8_ref[slot : slot + 1, :] = routes_ref[:, 64 * slot : 64 * slot + 64]
-    routes = jnp.concatenate(
-        [routes8_ref[pl.ds(slot_ref[p], 1), :] for p in range(8)], axis=0
-    ).astype(BF16)
-    row = lax.broadcasted_iota(jnp.int32, (64, 512), 1)
-    inside = ((row >> 6) & 3) * 16 + ((row >> 3) & 3) * 4 + (row & 3)
-    pick = (inside == lax.broadcasted_iota(jnp.int32, (64, 512), 0)).astype(F32).astype(BF16)
-    spread = nn(routes, pick)
-    row = lax.broadcasted_iota(jnp.int32, (8, 512), 1)
-    place = (row >> 8) + ((row >> 5) & 1) * 2 + ((row >> 2) & 1) * 4
-    here = place == lax.broadcasted_iota(jnp.int32, (8, 512), 0)
-    group = jnp.sum(jnp.where(here, spread, 0.0), axis=0, keepdims=True)
-    group = jnp.broadcast_to(group, (8, 512))
-    rr_ref[...] = group
-
-    shares = jnp.concatenate(
-        [jnp.where(group == float(g), weights, 0.0) for g in range(GROUPS)], axis=0
-    ).astype(BF16)
+    group = group_ref[...]
+    shares = shared_out(group, weights)
     vb = values.astype(BF16)
     sums = nn(shares, jnp.concatenate([vb, jnp.ones((512, 64), BF16)], axis=1))
     cot = early_ref[:, 0:COUT]
+    cott_ref[...] = cot.astype(F32).T.astype(BF16)
+    meets = nt(cot, vb)
+    total = jnp.zeros((8, 512), F32)
+    for g in range(GROUPS):
+        total = total + jnp.where(group == float(g), meets[8 * g : 8 * g + 8], 0.0)
+    tt_ref[...] = total
     inner = jnp.sum(sums[:, 0:COUT] * cot.astype(F32), axis=-1, keepdims=True)
     lane = lax.broadcasted_iota(jnp.int32, (8, 64), 1)
     mass = jnp.zeros((8, 64), F32)
@@ -207,16 +236,10 @@
     send_ref[:, 0:COUT] = sums[:, 0:COUT].astype(BF16)
     send_ref[:, COUT:256] = jnp.concatenate([table.astype(BF16)] * 32, axis=0)
 
-    meets = nt(cot, vb)
-    total = jnp.zeros((8, 512), F32)
-    for g in range(GROUPS):
-        total = total + jnp.where(group == float(g), meets[8 * g : 8 * g + 8], 0.0)
-    tt_ref[...] = total
-
 
 def backward_kernel(
-    recv_ref, podd_ref, peven_ref, slope_ref, hid_ref, ku_ref, kn_ref, wt_ref, tt_ref, rr_ref,
-    early_ref, key_ref, val_ref, query_ref,
+    recv_ref, podd_ref, peven_ref, slope_ref, hidt_ref, kut_ref, knt_ref, wt_ref, tt_ref,
+    group_ref, cott_ref, kt_ref, vw_ref, query_ref,
     pooled_ref, db_ref, xs_ref, ys_ref, keep_ref, give_ref, sum_ref,
 ):
     got = jnp.sum(recv_ref[...].reshape(32, 16, 256).astype(F32), axis=0)
@@ -234,49 +257,48 @@
     d_mass = -dots * inverse * inverse
     ih, il = split(inverse)
     mh, ml = split(d_mass)
-    group = rr_ref[...]
-    member = (
-        lax.broadcasted_iota(jnp.int32, (64, 512), 0).astype(F32)
-        == jnp.broadcast_to(group[0:1], (64, 512))
-    ).astype(F32).astype(BF16)
+    group = group_ref[...]
+    rows = lax.broadcasted_iota(jnp.int32, (64, 512), 0).astype(F32)
+    member = (rows == jnp.broadcast_to(group[0:1], (64, 512))).astype(F32).astype(BF16)
     inv_row = nn(ih, member) + nn(il, member)
     dm_row = nn(mh, member) + nn(ml, member)
     weights = wt_ref[...]
     d_cos = TEMPER * weights * (tt_ref[...] * inv_row + dm_row)
-    scaled = weights * inv_row
-    shares = jnp.concatenate(
-        [jnp.where(group == float(g), scaled, 0.0) for g in range(GROUPS)], axis=0
-    ).astype(BF16)
-    d_value = tn(shares, early_ref[:, 0:COUT]).astype(BF16)
-
+    d_value = nn(cott_ref[...], shared_out(group, weights * inv_row))
+
+    kut = kut_ref[...]
     queries = query_ref[...]
     qn = lax.rsqrt(jnp.sum(queries * queries, axis=-1, keepdims=True) + EPS)
     qu = queries * qn
-    ku = ku_ref[...]
-    dc = d_cos.astype(BF16)
-    d_ku = tn(dc, qu.astype(BF16))
-    d_key = kn_ref[...] * (d_ku - ku * jnp.sum(ku * d_ku, axis=-1, keepdims=True))
-    d_key = d_key.astype(BF16)
-    d_qu = nn(dc, ku.astype(BF16))
+    ch, cl = split(d_cos)
+    qh, ql = split(qu.T)
+    d_ku = nn(qh, ch) + nn(ql, ch) + nn(qh, cl)
+    d_key = knt_ref[0:1, :] * (d_ku - kut * jnp.sum(kut * d_ku, axis=0, keepdims=True))
+    d_qu = nt(ch, kut.astype(BF16))
     d_query = qn * (d_qu - qu * jnp.sum(qu * d_qu, axis=-1, keepdims=True))
 
-    d_hidden = nt(d_key, key_ref[...].astype(BF16)) + nt(d_value, val_ref[...].astype(BF16))
+    kh, kl = split(d_key)
+    vh, vl = split(d_value)
+    d_hidden = tn(kt_ref[0:COUT, :], kh) + tn(kt_ref[COUT : 2 * COUT, :], kh)
+    d_hidden = d_hidden + tn(kt_ref[0:COUT, :], kl) + nn(vw_ref[0:COUT, :], vl)
+    d_hidden = d_hidden + nn(vw_ref[0:COUT, :], vh) + nn(vw_ref[COUT : 2 * COUT, :], vh)
     d_before = d_hidden * slope_ref[...]
-    db = d_before.astype(BF16)
+    dbt = d_before.astype(BF16)
+    d_rows = d_before.T
+    db = d_rows.astype(BF16)
     db_ref[...] = db
     xs_ref[...] = db[0:64]
-    ys_ref[...] = d_before.reshape(8, 64, COUT)[:, 0:8].reshape(64, COUT).astype(BF16)
-
-    hid = hid_ref[...]
+    ys_ref[...] = d_rows.reshape(8, 64, COUT)[:, 0:8].reshape(64, COUT).astype(BF16)
+
     parts = (podd_ref[0:512, :], peven_ref[...], podd_ref[64:576, :])
     for a in range(3):
-        grad = tn(db, parts[a])
+        grad = nn(dbt, parts[a])
         for tap in range(9):
             piece = grad[:, tap * LANES : tap * LANES + CIN]
             sum_ref[:, pl.ds((9 * a + tap) * CIN, CIN)] = piece
-    sum_ref[:, KDIM : KDIM + COUT] = tn(hid, d_key)
-    sum_ref[:, KDIM + COUT : KDIM + 2 * COUT] = tn(hid, d_value)
-    bias = jnp.broadcast_to(jnp.sum(d_before, axis=0, keepdims=True), (8, COUT))
+    sum_ref[:, KDIM : KDIM + COUT] = nt(hidt_ref[...], kh)
+    sum_ref[:, KDIM + COUT : KDIM + 2 * COUT] = nt(hidt_ref[...], vh)
+    bias = jnp.broadcast_to(jnp.sum(d_rows, axis=0, keepdims=True), (8, COUT))
     small = [d_query[:, 0:CIN], d_query[:, CIN:COUT], bias[:, 0:CIN], bias[:, CIN:COUT]]
     small = jnp.concatenate(small + [jnp.zeros((COUT - 32, CIN), F32)], axis=0)
     sum_ref[:, KDIM + 2 * COUT : WIDE] = small
@@ -316,9 +338,12 @@
 
 
 def spread_kernel(
-    near_ref, db_ref, xr_ref, yr_ref, xyr_ref, wp_ref, occ_ref, out_ref,
-    ext_ref, even_ref, odd_ref, rows_ref, slot_ref,
+    near_ref, w_hbm, db_ref, xr_ref, yr_ref, xyr_ref, occ_ref, out_ref,
+    ext_ref, even_ref, odd_ref, rows_ref, slot_ref, w_ref, wp_ref, sem,
 ):
+    fetch = pltpu.make_async_copy(w_hbm, w_ref, sem)
+    fetch.start()
+    wp_ref[...] = jnp.zeros_like(wp_ref)
     find_slots(near_ref, slot_ref)
     edge = yr_ref[...].astype(F32)
     for jx in range(8):
@@ -328,6 +353,9 @@
     ext_ref[pl.ds(640, 8), :] = xyr_ref[...].astype(F32)[0:8]
     low = ext_ref[0:576, :].astype(BF16)
     high = ext_ref[72:648, :].astype(BF16)
+    fetch.wait()
+    for number in range(27):
+        wp_ref[:, pl.ds(number * LANES, CIN)] = w_ref[:, pl.ds(number * CIN, CIN)]
     even_ref[...] = nn(low, wp_ref[:, SLOTS9 : 2 * SLOTS9])
     odd_ref[...] = nn(low, wp_ref[:, 2 * SLOTS9 : 3 * SLOTS9]) + nn(high, wp_ref[:, 0:SLOTS9])
     last = lax.broadcasted_iota(jnp.int32, (32, LANES), 0) % 8 == 7
@@ -419,19 +447,30 @@
     early = lax.all_to_all(early, SPACE, 0, 0, tiled=True).reshape(512, 3 * LANES)
     xr = shift(xs, 1, 0)
     yr = shift(ys, 0, 1)
-    podd, peven, wp, slope, hid, ku, kn, wt, tt, rr, send = call(
-        forward_kernel, "sh",
-        [
-            like((576, SLOTS9), BF16), like((512, SLOTS9), BF16), like((COUT, 27 * LANES), BF16),
-            like((512, COUT)), like((512, COUT), BF16), like((512, COUT)), like((512, 1)),
-            like((8, 512)), like((8, 512)), like((8, 512)), like((512, 256), BF16),
+    wp, group = call(
+        prepare_kernel, "sh",
+        [
+            like((COUT, 27 * LANES), BF16), like((8, 512)),
         ],
         [
             slots, pltpu.VMEM((8, 64), jnp.int32), pltpu.VMEM((COUT, KDIM), BF16),
             pltpu.SemaphoreType.DMA,
         ],
-        neighbors, conv_weight.T, v, xr, yr, conv_bias.reshape(1, COUT), key_weight,
-        value_weight, queries, routes.reshape(1, 512), early,
+        neighbors, conv_weight.T, routes.reshape(1, 512),
+    )
+    podd, peven, slope, hidt, cott, kut, knt, wt, tt, kt, vw, send = call(
+        forward_kernel, "hhh",
+        [
+            like((576, SLOTS9), BF16), like((512, SLOTS9), BF16), like((COUT, 512)),
+            like((COUT, 512), BF16), like((COUT, 512), BF16), like((COUT, 512)), like((8, 512)),
+            like((8, 512)), like((8, 512)), like((2 * COUT, COUT), BF16),
+            like((2 * COUT, COUT), BF16), like((512, 256), BF16),
+        ],
+        [
+            pltpu.VMEM((COUT, COUT), F32), pltpu.VMEM((COUT, COUT), F32),
+            pltpu.VMEM((NQ, COUT), F32), pltpu.SemaphoreType.DMA((3,)),
+        ],
+        key_weight, value_weight, queries, v, xr, yr, conv_bias.reshape(1, COUT), wp, group, early,
     )
     recv = lax.all_to_all(send.reshape(32, 16, 256), SPACE, 0, 0, tiled=True).reshape(512, 256)
     pooled, db, bxs, bys, keep, give = call(
@@ -441,8 +480,7 @@
             like((64, COUT), BF16), like((HALF, LANES)), like((HALF, LANES), BF16),
         ],
         [pltpu.VMEM((COUT, WIDE), F32)],
-        recv, podd, peven, slope, hid, ku, kn, wt, tt, rr, early, key_weight, value_weight,
-        queries,
+        recv, podd, peven, slope, hidt, kut, knt, wt, tt, group, cott, kt, vw, queries,
     )
     swap = [(0, 1), (1, 0)]
     taken = lax.ppermute(give, "core", swap)
@@ -455,12 +493,14 @@
     bxr, byr, bxyr, copies = lax.optimization_barrier((bxr, byr, bxyr, copies))
     mine = lax.all_to_all(copies, CHIPS, 0, 0, tiled=True).reshape(HALF, LANES)
     d_features = call(
-        spread_kernel, "s", like((8, CIN, 512), BF16),
+        spread_kernel, "sh", like((8, CIN, 512), BF16),
         [
             pltpu.VMEM((648, COUT), F32), pltpu.VMEM((576, SLOTS9), F32),
             pltpu.VMEM((576, SLOTS9), F32), pltpu.VMEM((1024, LANES), F32), slots,
-        ],
-        neighbors, db, bxr, byr, bxyr, wp, occupancy,
+            pltpu.VMEM((COUT, KDIM), BF16), pltpu.VMEM((COUT, 27 * LANES), BF16),
+            pltpu.SemaphoreType.DMA,
+        ],
+        neighbors, conv_weight.T, db, bxr, byr, bxyr, occupancy,
     )
     mine, d_features = lax.optimization_barrier((mine, d_features))
     other = lax.ppermute(mine, "core", swap)

time: 96 us -> 95 us (0.990)
  waiting for transfers between devices: 26.7 us -> 22.7 us
  Pallas kernels: 17.5 us -> 20.5 us
    pallas_call x7 -> x8, Pallas kernels: 17.5 us -> 20.5 us  [call(): pl.pallas_call(kernel, out_shape=outs, in_specs=in_specs, out_specs=jax.t...]
    ppermute x5, waiting for transfers between devices: 1.82 us -> 0.01 us  [shift(): return lax.ppermute(shard, SPACE, pairs)]
    all_to_all x1, waiting for transfers between devices: 10.7 us -> 9.3 us  [on_device(): mine = lax.all_to_all(copies, CHIPS, 0, 0, tiled=True).reshape(HALF, LANES)]
  transfers between devices with their start and end apart: 10 -> 10, of which waited for: 6 -> 5; matrix products, arithmetic and copies ran while one was open for 0% -> 0% of each run, Pallas kernels for 4% -> 9%
where the time goes in v4:
time: 95 us; the launch traced here: 94.3 us
  starting transfers between devices  35.7 us (38%)
  waiting for transfers between devices  22.7 us (24%)
  Pallas kernels  20.5 us (22%)
  blocking collectives  14.6 us (15%)
    pallas_call x8, Pallas kernels, call(): pl.pallas_call(kernel, out_shape=outs, in_specs=in_specs, out_specs=jax.t...  20.5 us
    all_to_all x1, blocking collectives, on_device(): lax.all_to_all(send.reshape(32, 16, 256), SPACE, 0, 0, tiled=True)  14.6 us
    ppermute x5, starting transfers between devices, shift(): return lax.ppermute(shard, SPACE, pairs)  11.7 us
    all_to_all x1, starting transfers between devices, on_device(): lax.all_to_all(early, SPACE, 0, 0, tiled=True).reshape(512, 3 * LANES)  9.44 us
    all_to_all x1, waiting for transfers between devices, on_device(): mine = lax.all_to_all(copies, CHIPS, 0, 0, tiled=True).reshape(HALF, LANES)  9.3 us
    all_to_all x1, waiting for transfers between devices, on_device(): lax.all_to_all(half.reshape(64, SHARD, LANES), CHIPS, 0, 0, tiled=True)  8.79 us
    all_to_all x1, starting transfers between devices, on_device(): lax.all_to_all(half.reshape(64, SHARD, LANES), CHIPS, 0, 0, tiled=True)  6.66 us
    all_to_all x1, starting transfers between devices, on_device(): mine = lax.all_to_all(copies, CHIPS, 0, 0, tiled=True).reshape(HALF, LANES)  5.73 us
  transfers between devices with their start and end apart: 10, of which 5 were waited for; matrix products, arithmetic and copies ran while one was open for 0% of the time, Pallas kernels for 9%

profile of v4, /device:TPU:1, one launch (start us, length us, event | category | flops | bytes accessed | tf_op | source)
XLA Modules:
  0.0 94.3 jit_solution(37510262384255988)
XLA Ops:
  0.7 2.4 %place_kernel.1 = (bf16[16,4,64,128]{3,2,1,0:T(8,128)(2,1)S(1)}, bf16[256,128]{1,0:T(8,128)(2,1)S(1)}, bf16[256,128]{1,0:T(8,128)(2,1)S(1)}, bf16[32,16,384]{2,1,0:T(8,128)(2,1)}) custom-call(s32[6,8]{1,0:T(8,128)} %near_ref.3, bf16[8,96,512]{2,1,0:T(8,128)(2,1)} %bitcast.30, s32[8,512]{1,0:T(8,128)} %bitcast.24, f32[16,192]{1,0:T(8,128)} %bitcast.32), custom_call_target="tpu_custom_call" | custom-call | tf_op jit(solution)/shard_map/place_kernel/pallas_call | solution.py:408
  3.1 9.4 %all-to-all-start = ((bf16[32,16,384]{2,1,0:T(8,128)(2,1)}), bf16[32,16,384]{2,1,0:T(8,128)(2,1)S(1)}, u32[]{:S(2)}, u32[]{:S(2)}) async-start(bf16[32,16,384]{2,1,0:T(8,128)(2,1)} %get-tuple-element.47), calls=%async_computation | async-start | bytes 786432 | tf_op jit(solution)/shard_map/all_to_all | solution.py:447
  12.6 3.5 %collective-permute-start = (bf16[256,128]{1,0:T(8,128)(2,1)S(1)}, bf16[256,128]{1,0:T(8,128)(2,1)S(1)}, u32[]{:S(2)}, u32[]{:S(2)}) collective-permute-start(bf16[256,128]{1,0:T(8,128)(2,1)S(1)} %get-tuple-element.43), channel_id=1, source_target_pairs={{0,1},{1,2},{2,3},{3,4},{4,5},{5,6},{6,7},{8,9},{9,10},{10,11},{11... | collective-permute-start | bytes 196616 | tf_op jit(solution)/shard_map/ppermute | solution.py:425
  16.1 3.1 %collective-permute-start.1 = (bf16[256,128]{1,0:T(8,128)(2,1)S(1)}, bf16[256,128]{1,0:T(8,128)(2,1)S(1)}, u32[]{:S(2)}, u32[]{:S(2)}) collective-permute-start(bf16[256,128]{1,0:T(8,128)(2,1)S(1)} %get-tuple-element.44), channel_id=1, source_target_pairs={{0,8},{1,9},{2,10},{3,11},{4,12},{5,13},{6,14},{7,15},{8,16},{9,17... | collective-permute-start | bytes 196616 | tf_op jit(solution)/shard_map/ppermute | solution.py:425
  19.2 2.5 %prepare_kernel.1 = (bf16[192,3456]{1,0:T(8,128)(2,1)S(1)}, f32[8,512]{1,0:T(8,128)S(1)}) custom-call(s32[6,8]{1,0:T(8,128)S(1)} %copy-done.1, bf16[192,2592]{1,0:T(8,128)(2,1)} %bitcast.28, s32[1,512]{1,0:T(1,128)S(1)} %bitcast.26), custom_call_target="tpu_custom_call" | custom-call | tf_op jit(solution)/shard_map/prepare_kernel/pallas_call | solution.py:408
  21.8 1.0 %all-to-all-done = bf16[32,16,384]{2,1,0:T(8,128)(2,1)S(1)} async-done(((bf16[32,16,384]{2,1,0:T(8,128)(2,1)}), bf16[32,16,384]{2,1,0:T(8,128)(2,1)S(1)}, u32[]{:S(2)}, u32[]{:S(2)}) %all-to-all-start) | async-done | bytes 393248 | tf_op jit(solution)/shard_map/all_to_all | solution.py:447
  22.8 4.2 %forward_kernel.1 = (bf16[576,1152]{1,0:T(8,128)(2,1)S(1)}, bf16[512,1152]{1,0:T(8,128)(2,1)S(1)}, f32[192,512]{1,0:T(8,128)S(1)}, bf16[192,512]{1,0:T(8,128)(2,...) custom-call(f32[192,192]{1,0:T(8,128)} %key_hbm.1, ...), custom_call_target="tpu_custom_call" | custom-call | tf_op jit(solution)/shard_map/forward_kernel/pallas_call | solution.py:408
  27.1 14.6 %all_to_all.20 = bf16[32,16,256]{2,1,0:T(8,128)(2,1)S(1)} all-to-all(bf16[32,16,256]{2,1,0:T(8,128)(2,1)S(1)} %bitcast.23), channel_id=1, replica_groups=mesh['section'=4,'chip'=16,'core'=2] {'chip','core'}, dimensions={0} | all-to-all | bytes 524288 | tf_op jit(solution)/shard_map/all_to_all | solution.py:475
  41.6 3.3 %backward_kernel.1 = (f32[16,192]{1,0:T(8,128)}, bf16[512,192]{1,0:T(8,128)(2,1)S(1)}, bf16[64,192]{1,0:T(8,128)(2,1)S(1)}, bf16[64,192]{1,0:T(8,128)(2,1)S(1)},...) custom-call(bf16[512,256]{1,0:T(8,128)(2,1)S(1)} %bitcast.22, bf16[576,1152]{1,0:T(8,128)(2,1)S(1)} %get-tuple-element.49.podd_ref, ...), custom_call_target="tpu_custom_call" | custom-call | tf_op jit(solution)/shard_map/backward_kernel/pallas_call | solution.py:408
  44.9 0.2 collective-permute-start.5
  45.1 1.9 %collective-permute-done.5.b_ref = bf16[2560,128]{1,0:T(8,128)(2,1)S(1)} collective-permute-done((bf16[2560,128]{1,0:T(8,128)(2,1)S(1)}, bf16[2560,128]{1,0:T(8,128)(2,1)S(1)}, u32[]{:S(2)}, u32[]{:S(2)}) %collective-permute-start.5) | collective-permute-done | bytes 655392 | tf_op jit(solution)/shard_map/ppermute | solution.py:486
  47.0 1.0 %add_kernel.1 = bf16[2560,128]{1,0:T(8,128)(2,1)} custom-call(f32[2560,128]{1,0:T(8,128)S(1)} %get-tuple-element.63.a_ref, bf16[2560,128]{1,0:T(8,128)(2,1)S(1)} %collective-permute-done.5.b_ref), custom_call_target="tpu_custom_call" | custom-call | tf_op jit(solution)/shard_map/add_kernel/pallas_call | solution.py:408
  48.0 6.7 %all-to-all-start.2 = ((bf16[64,40,128]{2,1,0:T(8,128)(2,1)}), bf16[64,40,128]{2,1,0:T(8,128)(2,1)S(1)}, u32[]{:S(2)}, u32[]{:S(2)}) async-start(bf16[64,40,128]{2,1,0:T(8,128)(2,1)} %bitcast.11), calls=%async_computation.2 | async-start | bytes 1310720 | tf_op jit(solution)/shard_map/all_to_all | solution.py:488
  54.7 2.5 %collective-permute-start.2 = (bf16[64,192]{1,0:T(8,128)(2,1)S(1)}, bf16[64,192]{1,0:T(8,128)(2,1)S(1)}, u32[]{:S(2)}, u32[]{:S(2)}) collective-permute-start(bf16[64,192]{1,0:T(8,128)(2,1)S(1)} %get-tuple-element.61), channel_id=1, source_target_pairs={{1,0},{2,1},{3,2},{4,3},{5,4},{6,5},{7,6},{9,8},{10,9},{11,10},{12... | collective-permute-start | bytes 73736 | tf_op jit(solution)/shard_map/ppermute | solution.py:425
  57.2 1.3 %collective-permute-start.3 = (bf16[64,192]{1,0:T(8,128)(2,1)S(1)}, bf16[64,192]{1,0:T(8,128)(2,1)S(1)}, u32[]{:S(2)}, u32[]{:S(2)}) collective-permute-start(bf16[64,192]{1,0:T(8,128)(2,1)S(1)} %get-tuple-element.62), channel_id=1, source_target_pairs={{8,0},{9,1},{10,2},{11,3},{12,4},{13,5},{14,6},{15,7},{16,8},{17,9... | collective-permute-start | bytes 73736 | tf_op jit(solution)/shard_map/ppermute | solution.py:425
  58.5 1.3 %collective-permute-start.4 = (bf16[16,192]{1,0:T(8,128)(2,1)S(1)}, bf16[16,192]{1,0:T(8,128)(2,1)S(1)}, u32[]{:S(2)}, u32[]{:S(2)}) collective-permute-start(bf16[16,192]{1,0:T(8,128)(2,1)S(1)} %slice.3), channel_id=1, source_target_pairs={{9,0},{10,1},{11,2},{12,3},{13,4},{14,5},{15,6},{17,8},{18,9},{19,... | collective-permute-start | bytes 18440 | tf_op jit(solution)/shard_map/ppermute | solution.py:425
  59.8 8.8 %all-to-all-done.2.recv_ref = bf16[64,40,128]{2,1,0:T(8,128)(2,1)S(1)} async-done(((bf16[64,40,128]{2,1,0:T(8,128)(2,1)}), bf16[64,40,128]{2,1,0:T(8,128)(2,1)S(1)}, u32[]{:S(2)}, u32[]{:S(2)}) %all-to-all-start.2) | async-done | bytes 655392 | tf_op jit(solution)/shard_map/all_to_all | solution.py:488
  68.6 1.0 %total_kernel.1 = bf16[64,40,128]{2,1,0:T(8,128)(2,1)} custom-call(bf16[64,40,128]{2,1,0:T(8,128)(2,1)S(1)} %all-to-all-done.2.recv_ref), custom_call_target="tpu_custom_call" | custom-call | tf_op jit(solution)/shard_map/total_kernel/pallas_call | solution.py:408
  69.6 5.7 %all-to-all-start.3 = ((bf16[64,40,128]{2,1,0:T(8,128)(2,1)}), bf16[64,40,128]{2,1,0:T(8,128)(2,1)S(1)}, u32[]{:S(2)}, u32[]{:S(2)}) async-start(bf16[64,40,128]{2,1,0:T(8,128)(2,1)} %total_kernel.1), calls=%async_computation.3 | async-start | bytes 1310720 | tf_op jit(solution)/shard_map/all_to_all | solution.py:494
  75.3 4.5 %spread_kernel.1 = bf16[8,96,512]{2,1,0:T(8,128)(2,1)} custom-call(s32[6,8]{1,0:T(8,128)S(1)} %copy-done.1, bf16[192,2592]{1,0:T(8,128)(2,1)} %bitcast.29, bf16[512,192]{1,0:T(8,128)(2,1)S(1)} %get-tuple-element.66.db_ref, bf16[64,192]{1,0:T(8,128)(2,1)S(1)} %collective-permute-done.2.xr_ref, bf16[64,192]{1,0:T(8,128)(2,1)S(1)} %collective-permute-done.3.yr_ref, ...), custom_call_target="tpu_custom_call" | custom-call | tf_op jit(solution)/shard_map/spread_kernel/pallas_call | solution.py:408
  79.9 9.3 %all-to-all-done.3 = bf16[64,40,128]{2,1,0:T(8,128)(2,1)S(1)} async-done(((bf16[64,40,128]{2,1,0:T(8,128)(2,1)}), bf16[64,40,128]{2,1,0:T(8,128)(2,1)S(1)}, u32[]{:S(2)}, u32[]{:S(2)}) %all-to-all-start.3) | async-done | bytes 655392 | tf_op jit(solution)/shard_map/all_to_all | solution.py:494
  89.2 1.9 %collective-permute-start.6 = (bf16[2560,128]{1,0:T(8,128)(2,1)S(1)}, bf16[2560,128]{1,0:T(8,128)(2,1)S(1)}, u32[]{:S(2)}, u32[]{:S(2)}) collective-permute-start(bf16[2560,128]{1,0:T(8,128)(2,1)S(1)} %bitcast.19), channel_id=1, source_target_pairs={{0,1},{1,0},{2,3},{3,2},{4,5},{5,4},{6,7},{7,6},{8,9},{9,8},{10,11... | collective-permute-start | bytes 1966088 | tf_op jit(solution)/shard_map/ppermute | solution.py:506
  91.1 1.7 %collective-permute-done.6.other_ref = bf16[2560,128]{1,0:T(8,128)(2,1)S(1)} collective-permute-done((bf16[2560,128]{1,0:T(8,128)(2,1)S(1)}, bf16[2560,128]{1,0:T(8,128)(2,1)S(1)}, u32[]{:S(2)}, u32[]{:S(2)}) %collective-permute-start.6) | collective-permute-done | bytes 655392 | tf_op jit(solution)/shard_map/ppermute | solution.py:506
  92.8 1.6 %final_kernel.1 = (f32[192,2592]{1,0:T(8,128)}, f32[192,192]{1,0:T(8,128)}, f32[192,192]{1,0:T(8,128)}, f32[8,192]{1,0:T(8,128)}, f32[1,192]{1,0:T(1,128)}) custom-call(bf16[2560,128]{1,0:T(8,128)(2,1)S(1)} %bitcast.20, bf16[2560,128]{1,0:T(8,128)(2,1)S(1)} %collective-permute-done.6.other_ref), custom_call_target="tpu_custom_call" | custom-call | tf_op jit(solution)/shard_map/final_kernel/pallas_call | solution.py:408
  (16 shorter events, 0.0 us)
Async XLA Ops:
  0.6 18.6 %copy-start.1 = (s32[6,8]{1,0:T(8,128)S(1)}, s32[6,8]{1,0:T(8,128)}, u32[]{:S(2)}) copy-start(s32[6,8]{1,0:T(8,128)} %near_ref.3) | copy-start | bytes 580
  0.6 18.6 %copy-start.3 = (s32[1,512,1]{1,2,0:T(1,128)S(1)}, s32[1,512,1]{1,2,0:T(1,128)}, u32[]{:S(2)}) copy-start(s32[1,512,1]{1,2,0:T(1,128)} %param.13) | copy-start | bytes 6148
  0.7 22.2 %copy-start.4 = (f32[192]{0:T(256)S(1)}, f32[192]{0:T(256)}, u32[]{:S(2)}) copy-start(f32[192]{0:T(256)} %param.16) | copy-start | bytes 2308
  3.1 19.7 %all-to-all-start = ((bf16[32,16,384]{2,1,0:T(8,128)(2,1)}), bf16[32,16,384]{2,1,0:T(8,128)(2,1)S(1)}, u32[]{:S(2)}, u32[]{:S(2)}) async-start(bf16[32,16,384]{2,1,0:T(8,128)(2,1)} %get-tuple-element.47), calls=%async_computation | async-start | bytes 786432 | tf_op jit(solution)/shard_map/all_to_all | solution.py:447
  12.6 9.2 %collective-permute-start = (bf16[256,128]{1,0:T(8,128)(2,1)S(1)}, bf16[256,128]{1,0:T(8,128)(2,1)S(1)}, u32[]{:S(2)}, u32[]{:S(2)}) collective-permute-start(bf16[256,128]{1,0:T(8,128)(2,1)S(1)} %get-tuple-element.43), channel_id=1, source_target_pairs={{0,1},{1,2},{2,3},{3,4},{4,5},{5,6},{6,7},{8,9},{9,10},{10,11},{11... | collective-permute-start | bytes 196616 | tf_op jit(solution)/shard_map/ppermute | solution.py:425
  16.1 5.7 %collective-permute-start.1 = (bf16[256,128]{1,0:T(8,128)(2,1)S(1)}, bf16[256,128]{1,0:T(8,128)(2,1)S(1)}, u32[]{:S(2)}, u32[]{:S(2)}) collective-permute-start(bf16[256,128]{1,0:T(8,128)(2,1)S(1)} %get-tuple-element.44), channel_id=1, source_target_pairs={{0,8},{1,9},{2,10},{3,11},{4,12},{5,13},{6,14},{7,15},{8,16},{9,17... | collective-permute-start | bytes 196616 | tf_op jit(solution)/shard_map/ppermute | solution.py:425
  22.8 18.8 %copy-start.2 = (f32[8,192]{1,0:T(8,128)S(1)}, f32[8,192]{1,0:T(8,128)}, u32[]{:S(2)}) copy-start(f32[8,192]{1,0:T(8,128)} %query_ref.1) | copy-start | bytes 18436
  44.9 2.1 %collective-permute-start.5 = (bf16[2560,128]{1,0:T(8,128)(2,1)S(1)}, bf16[2560,128]{1,0:T(8,128)(2,1)S(1)}, u32[]{:S(2)}, u32[]{:S(2)}) collective-permute-start(bf16[2560,128]{1,0:T(8,128)(2,1)S(1)} %get-tuple-element.64), channel_id=1, source_target_pairs={{0,1},{1,0},{2,3},{3,2},{4,5},{5,4},{6,7},{7,6},{8,9},{9,8},{10,11... | collective-permute-start | bytes 1966088 | tf_op jit(solution)/shard_map/ppermute | solution.py:486
  48.0 20.6 %all-to-all-start.2 = ((bf16[64,40,128]{2,1,0:T(8,128)(2,1)}), bf16[64,40,128]{2,1,0:T(8,128)(2,1)S(1)}, u32[]{:S(2)}, u32[]{:S(2)}) async-start(bf16[64,40,128]{2,1,0:T(8,128)(2,1)} %bitcast.11), calls=%async_computation.2 | async-start | bytes 1310720 | tf_op jit(solution)/shard_map/all_to_all | solution.py:488
  54.7 20.6 %copy-start = (s32[1,8,512]{2,1,0:T(8,128)S(1)}, s32[1,8,512]{2,1,0:T(8,128)}, u32[]{:S(2)}) copy-start(s32[1,8,512]{2,1,0:T(8,128)} %param.11) | copy-start | bytes 49156
  54.7 14.9 %collective-permute-start.2 = (bf16[64,192]{1,0:T(8,128)(2,1)S(1)}, bf16[64,192]{1,0:T(8,128)(2,1)S(1)}, u32[]{:S(2)}, u32[]{:S(2)}) collective-permute-start(bf16[64,192]{1,0:T(8,128)(2,1)S(1)} %get-tuple-element.61), channel_id=1, source_target_pairs={{1,0},{2,1},{3,2},{4,3},{5,4},{6,5},{7,6},{9,8},{10,9},{11,10},{12... | collective-permute-start | bytes 73736 | tf_op jit(solution)/shard_map/ppermute | solution.py:425
  57.2 12.4 %collective-permute-start.3 = (bf16[64,192]{1,0:T(8,128)(2,1)S(1)}, bf16[64,192]{1,0:T(8,128)(2,1)S(1)}, u32[]{:S(2)}, u32[]{:S(2)}) collective-permute-start(bf16[64,192]{1,0:T(8,128)(2,1)S(1)} %get-tuple-element.62), channel_id=1, source_target_pairs={{8,0},{9,1},{10,2},{11,3},{12,4},{13,5},{14,6},{15,7},{16,8},{17,9... | collective-permute-start | bytes 73736 | tf_op jit(solution)/shard_map/ppermute | solution.py:425
  58.5 11.1 %collective-permute-start.4 = (bf16[16,192]{1,0:T(8,128)(2,1)S(1)}, bf16[16,192]{1,0:T(8,128)(2,1)S(1)}, u32[]{:S(2)}, u32[]{:S(2)}) collective-permute-start(bf16[16,192]{1,0:T(8,128)(2,1)S(1)} %slice.3), channel_id=1, source_target_pairs={{9,0},{10,1},{11,2},{12,3},{13,4},{14,5},{15,6},{17,8},{18,9},{19,... | collective-permute-start | bytes 18440 | tf_op jit(solution)/shard_map/ppermute | solution.py:425
  69.6 19.6 %all-to-all-start.3 = ((bf16[64,40,128]{2,1,0:T(8,128)(2,1)}), bf16[64,40,128]{2,1,0:T(8,128)(2,1)S(1)}, u32[]{:S(2)}, u32[]{:S(2)}) async-start(bf16[64,40,128]{2,1,0:T(8,128)(2,1)} %total_kernel.1), calls=%async_computation.3 | async-start | bytes 1310720 | tf_op jit(solution)/shard_map/all_to_all | solution.py:494
  89.2 3.6 %collective-permute-start.6 = (bf16[2560,128]{1,0:T(8,128)(2,1)S(1)}, bf16[2560,128]{1,0:T(8,128)(2,1)S(1)}, u32[]{:S(2)}, u32[]{:S(2)}) collective-permute-start(bf16[2560,128]{1,0:T(8,128)(2,1)S(1)} %bitcast.19), channel_id=1, source_target_pairs={{0,1},{1,0},{2,3},{3,2},{4,5},{5,4},{6,7},{7,6},{8,9},{9,8},{10,11... | collective-permute-start | bytes 1966088 | tf_op jit(solution)/shard_map/ppermute | solution.py:506

commit v5 on v4

--- a/solution.py
+++ b/solution.py
@@ -16,6 +16,7 @@
 KDIM = 27 * CIN
 SHARD = 40
 HALF = 64 * SHARD
+USED = 12 * COUT
 WIDE = 24 * LANES
 F32, BF16 = jnp.float32, jnp.bfloat16
 SPACE = ("chip", "core")
@@ -62,13 +63,11 @@
     near_hbm, feat_hbm, occ_hbm, cot_hbm, v_ref, xs_ref, ys_ref, early_ref,
     near_ref, feat_ref, occ_ref, cot_ref, rows_ref, slot_ref, sems,
 ):
+    pairs = [(near_hbm, near_ref), (occ_hbm, occ_ref), (cot_hbm, cot_ref)]
+    pairs += [(feat_hbm.at[slot], feat_ref.at[slot]) for slot in range(8)]
     copies = [
         pltpu.make_async_copy(source, target, sems.at[i])
-        for i, (source, target) in enumerate(
-            (
-                (near_hbm, near_ref), (feat_hbm, feat_ref), (occ_hbm, occ_ref), (cot_hbm, cot_ref),
-            )
-        )
+        for i, (source, target) in enumerate(pairs)
     ]
     for copy in copies:
         copy.start()
@@ -109,10 +108,14 @@
 def prepare_kernel(
     near_ref, w_hbm, routes_ref,
     wp_ref, group_ref,
-    slot_ref, routes8_ref, w_ref, sem,
-):
-    fetch = pltpu.make_async_copy(w_hbm, w_ref, sem)
-    fetch.start()
+    slot_ref, routes8_ref, w_ref, sems,
+):
+    fetches = [
+        pltpu.make_async_copy(w_hbm.at[pl.ds(48 * i, 48)], w_ref.at[pl.ds(48 * i, 48)], sems.at[i])
+        for i in range(4)
+    ]
+    for fetch in fetches:
+        fetch.start()
     find_slots(near_ref, slot_ref)
     wp_ref[...] = jnp.zeros_like(wp_ref)
     for slot in range(8):
@@ -130,9 +133,11 @@
     group = jnp.sum(jnp.where(mine, spread, 0.0), axis=0, keepdims=True)
     group_ref[...] = jnp.broadcast_to(group, (8, 512))
 
-    fetch.wait()
-    for tap in range(27):
-        wp_ref[:, pl.ds(tap * LANES, CIN)] = w_ref[:, pl.ds(tap * CIN, CIN)]
+    for i, fetch in enumerate(fetches):
+        fetch.wait()
+        for tap in range(27):
+            piece = w_ref[48 * i : 48 * i + 48, tap * CIN : tap * CIN + CIN]
+            wp_ref[48 * i : 48 * i + 48, tap * LANES : tap * LANES + CIN] = piece
 
 
 def shared_out(group, amounts):
@@ -198,10 +203,8 @@
         copy.wait()
     kh, kl = split(key_ref[...].T)
     vh, vl = split(val_ref[...])
-    kt_ref[0:COUT, :] = kh
-    kt_ref[COUT : 2 * COUT, :] = kl
-    vw_ref[0:COUT, :] = vh
-    vw_ref[COUT : 2 * COUT, :] = vl
+    kt_ref[...] = kh
+    vw_ref[...] = vh
     keys = nt(kh, hidden) + nt(kl, hidden)
     values = nn(hidden, vh) + nn(hidden, vl)
     queries = query_ref[...]
@@ -210,9 +213,7 @@
     kut = keys * key_norm
     kut_ref[...] = kut
     knt_ref[...] = jnp.broadcast_to(key_norm, (8, 512))
-    uh, ul = split(kut)
-    qh, ql = split(qu)
-    weights = jnp.exp(TEMPER * (nn(qh, uh) + nn(ql, uh) + nn(qh, ul)))
+    weights = jnp.exp(TEMPER * nn(qu.astype(BF16), kut.astype(BF16)))
     wt_ref[...] = weights
     group = group_ref[...]
     shares = shared_out(group, weights)
@@ -270,18 +271,14 @@
     queries = query_ref[...]
     qn = lax.rsqrt(jnp.sum(queries * queries, axis=-1, keepdims=True) + EPS)
     qu = queries * qn
-    ch, cl = split(d_cos)
-    qh, ql = split(qu.T)
-    d_ku = nn(qh, ch) + nn(ql, ch) + nn(qh, cl)
+    ch = d_cos.astype(BF16)
+    d_ku = nn(qu.T.astype(BF16), ch)
     d_key = knt_ref[0:1, :] * (d_ku - kut * jnp.sum(kut * d_ku, axis=0, keepdims=True))
     d_qu = nt(ch, kut.astype(BF16))
     d_query = qn * (d_qu - qu * jnp.sum(qu * d_qu, axis=-1, keepdims=True))
 
-    kh, kl = split(d_key)
-    vh, vl = split(d_value)
-    d_hidden = tn(kt_ref[0:COUT, :], kh) + tn(kt_ref[COUT : 2 * COUT, :], kh)
-    d_hidden = d_hidden + tn(kt_ref[0:COUT, :], kl) + nn(vw_ref[0:COUT, :], vl)
-    d_hidden = d_hidden + nn(vw_ref[0:COUT, :], vh) + nn(vw_ref[COUT : 2 * COUT, :], vh)
+    kh, vh = d_key.astype(BF16), d_value.astype(BF16)
+    d_hidden = tn(kt_ref[...], kh) + nn(vw_ref[...], vh)
     d_before = d_hidden * slope_ref[...]
     dbt = d_before.astype(BF16)
     d_rows = d_before.T
@@ -308,13 +305,11 @@
         right = sum_ref[:, LANES * (t + 12) : LANES * (t + 13)]
         keep_ref[COUT * t : COUT * (t + 1), :] = jnp.where(low, left, right)
         give_ref[COUT * t : COUT * (t + 1), :] = jnp.where(low, right, left).astype(BF16)
-    rest = HALF - 12 * COUT
-    keep_ref[12 * COUT : HALF, :] = jnp.zeros((rest, LANES), F32)
-    give_ref[12 * COUT : HALF, :] = jnp.zeros((rest, LANES), BF16)
 
 
 def add_kernel(a_ref, b_ref, out_ref):
-    out_ref[...] = (a_ref[...] + b_ref[...].astype(F32)).astype(BF16)
+    out_ref[0:USED, :] = (a_ref[...] + b_ref[...].astype(F32)).astype(BF16)
+    out_ref[USED:HALF, :] = jnp.zeros((HALF - USED, LANES), BF16)
 
 
 def total_kernel(recv_ref, out_ref):
@@ -322,19 +317,40 @@
     out_ref[...] = jnp.broadcast_to(total[None], out_ref.shape)
 
 
-def final_kernel(mine_ref, other_ref, dw_ref, dk_ref, dv_ref, dq_ref, dbias_ref, all_ref):
+def final_kernel(
+    mine_ref, other_ref, dw_hbm, dk_ref, dv_ref, dq_ref, dbias_ref, dw_ref, tail_ref, sems
+):
     low = lax.axis_index("core") == 0
-    for t in range(12):
-        mine = mine_ref[COUT * t : COUT * (t + 1), :].astype(F32)
-        other = other_ref[COUT * t : COUT * (t + 1), :].astype(F32)
-        all_ref[:, LANES * t : LANES * (t + 1)] = jnp.where(low, mine, other)
-        all_ref[:, LANES * (t + 12) : LANES * (t + 13)] = jnp.where(low, other, mine)
-    dw_ref[...] = all_ref[:, 0:KDIM]
-    dk_ref[...] = all_ref[:, KDIM : KDIM + COUT]
-    dv_ref[...] = all_ref[:, KDIM + COUT : KDIM + 2 * COUT]
-    small = all_ref[0:32, KDIM + 2 * COUT : WIDE]
+
+    def tile(t, start, rows):
+        place = COUT * (t % 12) + start
+        mine = mine_ref[place : place + rows, :].astype(F32)
+        other = other_ref[place : place + rows, :].astype(F32)
+        return jnp.where(low, mine, other) if t < 12 else jnp.where(low, other, mine)
+
+    copies = []
+    for i in range(4):
+        start = 48 * i
+        for t in range(20):
+            dw_ref[start : start + 48, LANES * t : LANES * (t + 1)] = tile(t, start, 48)
+        for t in range(20, 24):
+            tail_ref[start : start + 48, LANES * (t - 20) : LANES * (t - 19)] = tile(t, start, 48)
+        dw_ref[start : start + 48, 20 * LANES : KDIM] = tail_ref[
+            start : start + 48, 0 : KDIM - 20 * LANES
+        ]
+        copy = pltpu.make_async_copy(
+            dw_ref.at[pl.ds(start, 48)], dw_hbm.at[pl.ds(start, 48)], sems.at[i]
+        )
+        copy.start()
+        copies.append(copy)
+    base = KDIM - 20 * LANES
+    dk_ref[...] = tail_ref[:, base : base + COUT]
+    dv_ref[...] = tail_ref[:, base + COUT : base + 2 * COUT]
+    small = tail_ref[0:32, base + 2 * COUT : 4 * LANES]
     dq_ref[...] = jnp.concatenate([small[0:8], small[8:16]], axis=1)
     dbias_ref[...] = jnp.concatenate([small[16:17], small[24:25]], axis=1)
+    for copy in copies:
+        copy.wait()
 
 
 def spread_kernel(
@@ -397,7 +413,7 @@
     return jax.ShapeDtypeStruct(shape, dtype)
 
 
-def call(kernel, kinds, outs, scratch, *args):
+def call(kernel, kinds, outs, scratch, *args, first_out=None):
     spaces = {"s": pltpu.SMEM, "h": pltpu.HBM, "v": pltpu.VMEM}
     kinds = kinds + "v" * (len(args) - len(kinds))
     in_specs = [pl.BlockSpec(memory_space=spaces[kind]) for kind in kinds]
@@ -405,11 +421,14 @@
         pltpu.with_memory_space_constraint(arg, pltpu.HBM) if kind == "h" else arg
         for arg, kind in zip(args, kinds, strict=True)
     ]
+    out_specs = jax.tree.map(lambda _: vm(), outs)
+    if first_out is not None:
+        out_specs[0] = pl.BlockSpec(memory_space=first_out)
     return pl.pallas_call(
         kernel,
         out_shape=outs,
         in_specs=in_specs,
-        out_specs=jax.tree.map(lambda _: vm(), outs),
+        out_specs=out_specs,
         scratch_shapes=scratch,
         compiler_params=params(),
         name=kernel.__name__,
@@ -440,7 +459,7 @@
         [
             pltpu.SMEM((6, 8), jnp.int32), pltpu.VMEM((8, CIN, 512), BF16),
             pltpu.VMEM((8, 512), jnp.int32), pltpu.VMEM((16, COUT), F32),
-            pltpu.VMEM((1024, LANES), F32), slots, pltpu.SemaphoreType.DMA((4,)),
+            pltpu.VMEM((1024, LANES), F32), slots, pltpu.SemaphoreType.DMA((11,)),
         ],
         neighbors, features, occupancy, cotangent.reshape(16, COUT),
     )
@@ -454,7 +473,7 @@
         ],
         [
             slots, pltpu.VMEM((8, 64), jnp.int32), pltpu.VMEM((COUT, KDIM), BF16),
-            pltpu.SemaphoreType.DMA,
+            pltpu.SemaphoreType.DMA((4,)),
         ],
         neighbors, conv_weight.T, routes.reshape(1, 512),
     )
@@ -463,8 +482,8 @@
         [
             like((576, SLOTS9), BF16), like((512, SLOTS9), BF16), like((COUT, 512)),
             like((COUT, 512), BF16), like((COUT, 512), BF16), like((COUT, 512)), like((8, 512)),
-            like((8, 512)), like((8, 512)), like((2 * COUT, COUT), BF16),
-            like((2 * COUT, COUT), BF16), like((512, 256), BF16),
+            like((8, 512)), like((8, 512)), like((COUT, COUT), BF16),
+            like((COUT, COUT), BF16), like((512, 256), BF16),
         ],
         [
             pltpu.VMEM((COUT, COUT), F32), pltpu.VMEM((COUT, COUT), F32),
@@ -477,7 +496,7 @@
         backward_kernel, "",
         [
             like((16, COUT)), like((512, COUT), BF16), like((64, COUT), BF16),
-            like((64, COUT), BF16), like((HALF, LANES)), like((HALF, LANES), BF16),
+            like((64, COUT), BF16), like((USED, LANES)), like((USED, LANES), BF16),
         ],
         [pltpu.VMEM((COUT, WIDE), F32)],
         recv, podd, peven, slope, hidt, kut, knt, wt, tt, group, cott, kt, vw, queries,
@@ -510,8 +529,11 @@
             like((COUT, KDIM)), like((COUT, COUT)), like((COUT, COUT)), like((NQ, COUT)),
             like((1, COUT)),
         ],
-        [pltpu.VMEM((COUT, WIDE), F32)],
-        mine, other,
+        [
+            pltpu.VMEM((COUT, KDIM), F32), pltpu.VMEM((COUT, 4 * LANES), F32),
+            pltpu.SemaphoreType.DMA((4,)),
+        ],
+        mine, other, first_out=pltpu.HBM,
     )
     return (
         pooled.reshape(1, 2, NQ, COUT), jnp.swapaxes(d_features, 1, 2)[None], d_weight.T,

time: 95 us -> 94.1 us (level)
  no operation moved by 1% of the time
where the time goes in v5:
time: 94.1 us; the launch traced here: 93.5 us
  starting transfers between devices  35.7 us (38%)
  waiting for transfers between devices  22.7 us (24%)
  Pallas kernels  19.7 us (21%)
  blocking collectives  14.6 us (16%)
    pallas_call x8, Pallas kernels, call(): pl.pallas_call(kernel, out_shape=outs, in_specs=in_specs, out_specs=out_s...  19.7 us
    all_to_all x1, blocking collectives, on_device(): lax.all_to_all(send.reshape(32, 16, 256), SPACE, 0, 0, tiled=True)  14.6 us
    ppermute x5, starting transfers between devices, shift(): return lax.ppermute(shard, SPACE, pairs)  11.7 us
    all_to_all x1, starting transfers between devices, on_device(): lax.all_to_all(early, SPACE, 0, 0, tiled=True).reshape(512, 3 * LANES)  9.44 us
    all_to_all x1, waiting for transfers between devices, on_device(): mine = lax.all_to_all(copies, CHIPS, 0, 0, tiled=True).reshape(HALF, LANES)  9.3 us
    all_to_all x1, waiting for transfers between devices, on_device(): lax.all_to_all(half.reshape(64, SHARD, LANES), CHIPS, 0, 0, tiled=True)  8.79 us
    all_to_all x1, starting transfers between devices, on_device(): lax.all_to_all(half.reshape(64, SHARD, LANES), CHIPS, 0, 0, tiled=True)  6.66 us
    all_to_all x1, starting transfers between devices, on_device(): mine = lax.all_to_all(copies, CHIPS, 0, 0, tiled=True).reshape(HALF, LANES)  5.73 us
  transfers between devices with their start and end apart: 10, of which 5 were waited for; matrix products, arithmetic and copies ran while one was open for 0% of the time, Pallas kernels for 9%

profile of v5, /device:TPU:1, one launch (start us, length us, event | category | flops | bytes accessed | tf_op | source)
XLA Modules:
  0.0 93.5 jit_solution(391622773330728022)
XLA Ops:
  0.7 2.6 %place_kernel.1 = (bf16[16,4,64,128]{3,2,1,0:T(8,128)(2,1)S(1)}, bf16[256,128]{1,0:T(8,128)(2,1)S(1)}, bf16[256,128]{1,0:T(8,128)(2,1)S(1)}, bf16[32,16,384]{2,1,0:T(8,128)(2,1)}) custom-call(s32[6,8]{1,0:T(8,128)} %near_ref.3, bf16[8,96,512]{2,1,0:T(8,128)(2,1)} %bitcast.30, s32[8,512]{1,0:T(8,128)} %bitcast.24, f32[16,192]{1,0:T(8,128)} %bitcast.32), custom_call_target="tpu_custom_call" | custom-call | tf_op jit(solution)/shard_map/place_kernel/pallas_call | solution.py:427
  3.3 9.4 %all-to-all-start = ((bf16[32,16,384]{2,1,0:T(8,128)(2,1)}), bf16[32,16,384]{2,1,0:T(8,128)(2,1)S(1)}, u32[]{:S(2)}, u32[]{:S(2)}) async-start(bf16[32,16,384]{2,1,0:T(8,128)(2,1)} %get-tuple-element.47), calls=%async_computation | async-start | bytes 786432 | tf_op jit(solution)/shard_map/all_to_all | solution.py:466
  12.7 3.5 %collective-permute-start = (bf16[256,128]{1,0:T(8,128)(2,1)S(1)}, bf16[256,128]{1,0:T(8,128)(2,1)S(1)}, u32[]{:S(2)}, u32[]{:S(2)}) collective-permute-start(bf16[256,128]{1,0:T(8,128)(2,1)S(1)} %get-tuple-element.43), channel_id=1, source_target_pairs={{0,1},{1,2},{2,3},{3,4},{4,5},{5,6},{6,7},{8,9},{9,10},{10,11},{11... | collective-permute-start | bytes 196616 | tf_op jit(solution)/shard_map/ppermute | solution.py:444
  16.3 3.1 %collective-permute-start.1 = (bf16[256,128]{1,0:T(8,128)(2,1)S(1)}, bf16[256,128]{1,0:T(8,128)(2,1)S(1)}, u32[]{:S(2)}, u32[]{:S(2)}) collective-permute-start(bf16[256,128]{1,0:T(8,128)(2,1)S(1)} %get-tuple-element.44), channel_id=1, source_target_pairs={{0,8},{1,9},{2,10},{3,11},{4,12},{5,13},{6,14},{7,15},{8,16},{9,17... | collective-permute-start | bytes 196616 | tf_op jit(solution)/shard_map/ppermute | solution.py:444
  19.4 2.5 %prepare_kernel.1 = (bf16[192,3456]{1,0:T(8,128)(2,1)S(1)}, f32[8,512]{1,0:T(8,128)S(1)}) custom-call(s32[6,8]{1,0:T(8,128)S(1)} %copy-done.1, bf16[192,2592]{1,0:T(8,128)(2,1)} %bitcast.28, s32[1,512]{1,0:T(1,128)S(1)} %bitcast.26), custom_call_target="tpu_custom_call" | custom-call | tf_op jit(solution)/shard_map/prepare_kernel/pallas_call | solution.py:427
  21.9 1.1 %all-to-all-done = bf16[32,16,384]{2,1,0:T(8,128)(2,1)S(1)} async-done(((bf16[32,16,384]{2,1,0:T(8,128)(2,1)}), bf16[32,16,384]{2,1,0:T(8,128)(2,1)S(1)}, u32[]{:S(2)}, u32[]{:S(2)}) %all-to-all-start) | async-done | bytes 393248 | tf_op jit(solution)/shard_map/all_to_all | solution.py:466
  23.0 3.8 %forward_kernel.1 = (bf16[576,1152]{1,0:T(8,128)(2,1)S(1)}, bf16[512,1152]{1,0:T(8,128)(2,1)S(1)}, f32[192,512]{1,0:T(8,128)S(1)}, bf16[192,512]{1,0:T(8,128)(2,...) custom-call(f32[192,192]{1,0:T(8,128)} %key_hbm.1, ...), custom_call_target="tpu_custom_call" | custom-call | tf_op jit(solution)/shard_map/forward_kernel/pallas_call | solution.py:427
  26.8 14.6 %all_to_all.20 = bf16[32,16,256]{2,1,0:T(8,128)(2,1)S(1)} all-to-all(bf16[32,16,256]{2,1,0:T(8,128)(2,1)S(1)} %bitcast.23), channel_id=1, replica_groups=mesh['section'=4,'chip'=16,'core'=2] {'chip','core'}, dimensions={0} | all-to-all | bytes 524288 | tf_op jit(solution)/shard_map/all_to_all | solution.py:494
  41.4 2.1 %backward_kernel.1 = (f32[16,192]{1,0:T(8,128)}, bf16[512,192]{1,0:T(8,128)(2,1)S(1)}, bf16[64,192]{1,0:T(8,128)(2,1)S(1)}, bf16[64,192]{1,0:T(8,128)(2,1)S(1)},...) custom-call(bf16[512,256]{1,0:T(8,128)(2,1)S(1)} %bitcast.22, bf16[576,1152]{1,0:T(8,128)(2,1)S(1)} %get-tuple-element.49.podd_ref, ...), custom_call_target="tpu_custom_call" | custom-call | tf_op jit(solution)/shard_map/backward_kernel/pallas_call | solution.py:427
  43.5 0.3 collective-permute-start.5
  43.7 1.8 %collective-permute-done.5.b_ref = bf16[2304,128]{1,0:T(8,128)(2,1)S(1)} collective-permute-done((bf16[2304,128]{1,0:T(8,128)(2,1)S(1)}, bf16[2304,128]{1,0:T(8,128)(2,1)S(1)}, u32[]{:S(2)}, u32[]{:S(2)}) %collective-permute-start.5) | collective-permute-done | bytes 589856 | tf_op jit(solution)/shard_map/ppermute | solution.py:505
  45.5 1.0 %add_kernel.1 = bf16[2560,128]{1,0:T(8,128)(2,1)} custom-call(f32[2304,128]{1,0:T(8,128)S(1)} %get-tuple-element.63.a_ref, bf16[2304,128]{1,0:T(8,128)(2,1)S(1)} %collective-permute-done.5.b_ref), custom_call_target="tpu_custom_call" | custom-call | tf_op jit(solution)/shard_map/add_kernel/pallas_call | solution.py:427
  46.5 6.7 %all-to-all-start.2 = ((bf16[64,40,128]{2,1,0:T(8,128)(2,1)}), bf16[64,40,128]{2,1,0:T(8,128)(2,1)S(1)}, u32[]{:S(2)}, u32[]{:S(2)}) async-start(bf16[64,40,128]{2,1,0:T(8,128)(2,1)} %bitcast.11), calls=%async_computation.2 | async-start | bytes 1310720 | tf_op jit(solution)/shard_map/all_to_all | solution.py:507
  53.2 2.5 %collective-permute-start.2 = (bf16[64,192]{1,0:T(8,128)(2,1)S(1)}, bf16[64,192]{1,0:T(8,128)(2,1)S(1)}, u32[]{:S(2)}, u32[]{:S(2)}) collective-permute-start(bf16[64,192]{1,0:T(8,128)(2,1)S(1)} %get-tuple-element.61), channel_id=1, source_target_pairs={{1,0},{2,1},{3,2},{4,3},{5,4},{6,5},{7,6},{9,8},{10,9},{11,10},{12... | collective-permute-start | bytes 73736 | tf_op jit(solution)/shard_map/ppermute | solution.py:444
  55.7 1.3 %collective-permute-start.3 = (bf16[64,192]{1,0:T(8,128)(2,1)S(1)}, bf16[64,192]{1,0:T(8,128)(2,1)S(1)}, u32[]{:S(2)}, u32[]{:S(2)}) collective-permute-start(bf16[64,192]{1,0:T(8,128)(2,1)S(1)} %get-tuple-element.62), channel_id=1, source_target_pairs={{8,0},{9,1},{10,2},{11,3},{12,4},{13,5},{14,6},{15,7},{16,8},{17,9... | collective-permute-start | bytes 73736 | tf_op jit(solution)/shard_map/ppermute | solution.py:444
  57.0 1.3 %collective-permute-start.4 = (bf16[16,192]{1,0:T(8,128)(2,1)S(1)}, bf16[16,192]{1,0:T(8,128)(2,1)S(1)}, u32[]{:S(2)}, u32[]{:S(2)}) collective-permute-start(bf16[16,192]{1,0:T(8,128)(2,1)S(1)} %slice.3), channel_id=1, source_target_pairs={{9,0},{10,1},{11,2},{12,3},{13,4},{14,5},{15,6},{17,8},{18,9},{19,... | collective-permute-start | bytes 18440 | tf_op jit(solution)/shard_map/ppermute | solution.py:444
  58.3 8.8 %all-to-all-done.2.recv_ref = bf16[64,40,128]{2,1,0:T(8,128)(2,1)S(1)} async-done(((bf16[64,40,128]{2,1,0:T(8,128)(2,1)}), bf16[64,40,128]{2,1,0:T(8,128)(2,1)S(1)}, u32[]{:S(2)}, u32[]{:S(2)}) %all-to-all-start.2) | async-done | bytes 655392 | tf_op jit(solution)/shard_map/all_to_all | solution.py:507
  67.1 1.0 %total_kernel.1 = bf16[64,40,128]{2,1,0:T(8,128)(2,1)} custom-call(bf16[64,40,128]{2,1,0:T(8,128)(2,1)S(1)} %all-to-all-done.2.recv_ref), custom_call_target="tpu_custom_call" | custom-call | tf_op jit(solution)/shard_map/total_kernel/pallas_call | solution.py:427
  68.1 5.7 %all-to-all-start.3 = ((bf16[64,40,128]{2,1,0:T(8,128)(2,1)}), bf16[64,40,128]{2,1,0:T(8,128)(2,1)S(1)}, u32[]{:S(2)}, u32[]{:S(2)}) async-start(bf16[64,40,128]{2,1,0:T(8,128)(2,1)} %total_kernel.1), calls=%async_computation.3 | async-start | bytes 1310720 | tf_op jit(solution)/shard_map/all_to_all | solution.py:513
  73.8 4.5 %spread_kernel.1 = bf16[8,96,512]{2,1,0:T(8,128)(2,1)} custom-call(s32[6,8]{1,0:T(8,128)S(1)} %copy-done.1, bf16[192,2592]{1,0:T(8,128)(2,1)} %bitcast.29, bf16[512,192]{1,0:T(8,128)(2,1)S(1)} %get-tuple-element.66.db_ref, bf16[64,192]{1,0:T(8,128)(2,1)S(1)} %collective-permute-done.2.xr_ref, bf16[64,192]{1,0:T(8,128)(2,1)S(1)} %collective-permute-done.3.yr_ref, ...), custom_call_target="tpu_custom_call" | custom-call | tf_op jit(solution)/shard_map/spread_kernel/pallas_call | solution.py:427
  78.4 9.3 %all-to-all-done.3 = bf16[64,40,128]{2,1,0:T(8,128)(2,1)S(1)} async-done(((bf16[64,40,128]{2,1,0:T(8,128)(2,1)}), bf16[64,40,128]{2,1,0:T(8,128)(2,1)S(1)}, u32[]{:S(2)}, u32[]{:S(2)}) %all-to-all-start.3) | async-done | bytes 655392 | tf_op jit(solution)/shard_map/all_to_all | solution.py:513
  87.7 1.9 %collective-permute-start.6 = (bf16[2560,128]{1,0:T(8,128)(2,1)S(1)}, bf16[2560,128]{1,0:T(8,128)(2,1)S(1)}, u32[]{:S(2)}, u32[]{:S(2)}) collective-permute-start(bf16[2560,128]{1,0:T(8,128)(2,1)S(1)} %bitcast.19), channel_id=1, source_target_pairs={{0,1},{1,0},{2,3},{3,2},{4,5},{5,4},{6,7},{7,6},{8,9},{9,8},{10,11... | collective-permute-start | bytes 1966088 | tf_op jit(solution)/shard_map/ppermute | solution.py:525
  89.6 1.7 %collective-permute-done.6.other_ref = bf16[2560,128]{1,0:T(8,128)(2,1)S(1)} collective-permute-done((bf16[2560,128]{1,0:T(8,128)(2,1)S(1)}, bf16[2560,128]{1,0:T(8,128)(2,1)S(1)}, u32[]{:S(2)}, u32[]{:S(2)}) %collective-permute-start.6) | collective-permute-done | bytes 655392 | tf_op jit(solution)/shard_map/ppermute | solution.py:525
  91.3 2.2 %final_kernel.1 = (f32[192,2592]{1,0:T(8,128)}, f32[192,192]{1,0:T(8,128)}, f32[192,192]{1,0:T(8,128)}, f32[8,192]{1,0:T(8,128)}, f32[1,192]{1,0:T(1,128)}) custom-call(bf16[2560,128]{1,0:T(8,128)(2,1)S(1)} %bitcast.20, bf16[2560,128]{1,0:T(8,128)(2,1)S(1)} %collective-permute-done.6.other_ref), custom_call_target="tpu_custom_call" | custom-call | tf_op jit(solution)/shard_map/final_kernel/pallas_call | solution.py:427
  (16 shorter events, 0.0 us)
Async XLA Ops:
  0.6 18.7 %copy-start.1 = (s32[6,8]{1,0:T(8,128)S(1)}, s32[6,8]{1,0:T(8,128)}, u32[]{:S(2)}) copy-start(s32[6,8]{1,0:T(8,128)} %near_ref.3) | copy-start | bytes 580
  0.6 18.7 %copy-start.3 = (s32[1,512,1]{1,2,0:T(1,128)S(1)}, s32[1,512,1]{1,2,0:T(1,128)}, u32[]{:S(2)}) copy-start(s32[1,512,1]{1,2,0:T(1,128)} %param.13) | copy-start | bytes 6148
  0.7 22.3 %copy-start.4 = (f32[192]{0:T(256)S(1)}, f32[192]{0:T(256)}, u32[]{:S(2)}) copy-start(f32[192]{0:T(256)} %param.16) | copy-start | bytes 2308
  3.3 19.7 %all-to-all-start = ((bf16[32,16,384]{2,1,0:T(8,128)(2,1)}), bf16[32,16,384]{2,1,0:T(8,128)(2,1)S(1)}, u32[]{:S(2)}, u32[]{:S(2)}) async-start(bf16[32,16,384]{2,1,0:T(8,128)(2,1)} %get-tuple-element.47), calls=%async_computation | async-start | bytes 786432 | tf_op jit(solution)/shard_map/all_to_all | solution.py:466
  12.7 9.2 %collective-permute-start = (bf16[256,128]{1,0:T(8,128)(2,1)S(1)}, bf16[256,128]{1,0:T(8,128)(2,1)S(1)}, u32[]{:S(2)}, u32[]{:S(2)}) collective-permute-start(bf16[256,128]{1,0:T(8,128)(2,1)S(1)} %get-tuple-element.43), channel_id=1, source_target_pairs={{0,1},{1,2},{2,3},{3,4},{4,5},{5,6},{6,7},{8,9},{9,10},{10,11},{11... | collective-permute-start | bytes 196616 | tf_op jit(solution)/shard_map/ppermute | solution.py:444
  16.3 5.6 %collective-permute-start.1 = (bf16[256,128]{1,0:T(8,128)(2,1)S(1)}, bf16[256,128]{1,0:T(8,128)(2,1)S(1)}, u32[]{:S(2)}, u32[]{:S(2)}) collective-permute-start(bf16[256,128]{1,0:T(8,128)(2,1)S(1)} %get-tuple-element.44), channel_id=1, source_target_pairs={{0,8},{1,9},{2,10},{3,11},{4,12},{5,13},{6,14},{7,15},{8,16},{9,17... | collective-permute-start | bytes 196616 | tf_op jit(solution)/shard_map/ppermute | solution.py:444
  23.0 18.4 %copy-start.2 = (f32[8,192]{1,0:T(8,128)S(1)}, f32[8,192]{1,0:T(8,128)}, u32[]{:S(2)}) copy-start(f32[8,192]{1,0:T(8,128)} %query_ref.1) | copy-start | bytes 18436
  43.5 2.0 %collective-permute-start.5 = (bf16[2304,128]{1,0:T(8,128)(2,1)S(1)}, bf16[2304,128]{1,0:T(8,128)(2,1)S(1)}, u32[]{:S(2)}, u32[]{:S(2)}) collective-permute-start(bf16[2304,128]{1,0:T(8,128)(2,1)S(1)} %get-tuple-element.64), channel_id=1, source_target_pairs={{0,1},{1,0},{2,3},{3,2},{4,5},{5,4},{6,7},{7,6},{8,9},{9,8},{10,11... | collective-permute-start | bytes 1769480 | tf_op jit(solution)/shard_map/ppermute | solution.py:505
  46.5 20.6 %all-to-all-start.2 = ((bf16[64,40,128]{2,1,0:T(8,128)(2,1)}), bf16[64,40,128]{2,1,0:T(8,128)(2,1)S(1)}, u32[]{:S(2)}, u32[]{:S(2)}) async-start(bf16[64,40,128]{2,1,0:T(8,128)(2,1)} %bitcast.11), calls=%async_computation.2 | async-start | bytes 1310720 | tf_op jit(solution)/shard_map/all_to_all | solution.py:507
  53.1 20.6 %copy-start = (s32[1,8,512]{2,1,0:T(8,128)S(1)}, s32[1,8,512]{2,1,0:T(8,128)}, u32[]{:S(2)}) copy-start(s32[1,8,512]{2,1,0:T(8,128)} %param.11) | copy-start | bytes 49156
  53.2 14.9 %collective-permute-start.2 = (bf16[64,192]{1,0:T(8,128)(2,1)S(1)}, bf16[64,192]{1,0:T(8,128)(2,1)S(1)}, u32[]{:S(2)}, u32[]{:S(2)}) collective-permute-start(bf16[64,192]{1,0:T(8,128)(2,1)S(1)} %get-tuple-element.61), channel_id=1, source_target_pairs={{1,0},{2,1},{3,2},{4,3},{5,4},{6,5},{7,6},{9,8},{10,9},{11,10},{12... | collective-permute-start | bytes 73736 | tf_op jit(solution)/shard_map/ppermute | solution.py:444
  55.7 12.4 %collective-permute-start.3 = (bf16[64,192]{1,0:T(8,128)(2,1)S(1)}, bf16[64,192]{1,0:T(8,128)(2,1)S(1)}, u32[]{:S(2)}, u32[]{:S(2)}) collective-permute-start(bf16[64,192]{1,0:T(8,128)(2,1)S(1)} %get-tuple-element.62), channel_id=1, source_target_pairs={{8,0},{9,1},{10,2},{11,3},{12,4},{13,5},{14,6},{15,7},{16,8},{17,9... | collective-permute-start | bytes 73736 | tf_op jit(solution)/shard_map/ppermute | solution.py:444
  57.0 11.1 %collective-permute-start.4 = (bf16[16,192]{1,0:T(8,128)(2,1)S(1)}, bf16[16,192]{1,0:T(8,128)(2,1)S(1)}, u32[]{:S(2)}, u32[]{:S(2)}) collective-permute-start(bf16[16,192]{1,0:T(8,128)(2,1)S(1)} %slice.3), channel_id=1, source_target_pairs={{9,0},{10,1},{11,2},{12,3},{13,4},{14,5},{15,6},{17,8},{18,9},{19,... | collective-permute-start | bytes 18440 | tf_op jit(solution)/shard_map/ppermute | solution.py:444
  68.1 19.6 %all-to-all-start.3 = ((bf16[64,40,128]{2,1,0:T(8,128)(2,1)}), bf16[64,40,128]{2,1,0:T(8,128)(2,1)S(1)}, u32[]{:S(2)}, u32[]{:S(2)}) async-start(bf16[64,40,128]{2,1,0:T(8,128)(2,1)} %total_kernel.1), calls=%async_computation.3 | async-start | bytes 1310720 | tf_op jit(solution)/shard_map/all_to_all | solution.py:513
  87.7 3.6 %collective-permute-start.6 = (bf16[2560,128]{1,0:T(8,128)(2,1)S(1)}, bf16[2560,128]{1,0:T(8,128)(2,1)S(1)}, u32[]{:S(2)}, u32[]{:S(2)}) collective-permute-start(bf16[2560,128]{1,0:T(8,128)(2,1)S(1)} %bitcast.19), channel_id=1, source_target_pairs={{0,1},{1,0},{2,3},{3,2},{4,5},{5,4},{6,7},{7,6},{8,9},{9,8},{10,11... | collective-permute-start | bytes 1966088 | tf_op jit(solution)/shard_map/ppermute | solution.py:525

commit v6 on v4

--- a/solution.py
+++ b/solution.py
@@ -15,7 +15,9 @@
 GROUPS, NQ = 64, 8
 KDIM = 27 * CIN
 SHARD = 40
+PACKED, PACKS = 9 * CIN, 7 * LANES
 HALF = 64 * SHARD
+USED = 12 * COUT
 WIDE = 24 * LANES
 F32, BF16 = jnp.float32, jnp.bfloat16
 SPACE = ("chip", "core")
@@ -62,13 +64,12 @@
     near_hbm, feat_hbm, occ_hbm, cot_hbm, v_ref, xs_ref, ys_ref, early_ref,
     near_ref, feat_ref, occ_ref, cot_ref, rows_ref, slot_ref, sems,
 ):
+    pairs = [
+        (near_hbm, near_ref), (feat_hbm, feat_ref), (occ_hbm, occ_ref), (cot_hbm, cot_ref),
+    ]
     copies = [
         pltpu.make_async_copy(source, target, sems.at[i])
-        for i, (source, target) in enumerate(
-            (
-                (near_hbm, near_ref), (feat_hbm, feat_ref), (occ_hbm, occ_ref), (cot_hbm, cot_ref),
-            )
-        )
+        for i, (source, target) in enumerate(pairs)
     ]
     for copy in copies:
         copy.start()
@@ -106,15 +107,7 @@
     early_ref[...] = jnp.broadcast_to(early[None], early_ref.shape)
 
 
-def prepare_kernel(
-    near_ref, w_hbm, routes_ref,
-    wp_ref, group_ref,
-    slot_ref, routes8_ref, w_ref, sem,
-):
-    fetch = pltpu.make_async_copy(w_hbm, w_ref, sem)
-    fetch.start()
-    find_slots(near_ref, slot_ref)
-    wp_ref[...] = jnp.zeros_like(wp_ref)
+def row_groups(routes_ref, routes8_ref, slot_ref):
     for slot in range(8):
         routes8_ref[slot : slot + 1, :] = routes_ref[:, 64 * slot : 64 * slot + 64]
     routes = jnp.concatenate(
@@ -128,11 +121,13 @@
     place = (row >> 8) + ((row >> 5) & 1) * 2 + ((row >> 2) & 1) * 4
     mine = place == lax.broadcasted_iota(jnp.int32, (8, 512), 0)
     group = jnp.sum(jnp.where(mine, spread, 0.0), axis=0, keepdims=True)
-    group_ref[...] = jnp.broadcast_to(group, (8, 512))
-
-    fetch.wait()
-    for tap in range(27):
-        wp_ref[:, pl.ds(tap * LANES, CIN)] = w_ref[:, pl.ds(tap * CIN, CIN)]
+    return jnp.broadcast_to(group, (8, 512))
+
+
+def pad_weights(w_ref, wp_ref):
+    for a in range(3):
+        wp_ref[:, PACKS * a : PACKS * a + PACKED] = w_ref[:, PACKED * a : PACKED * (a + 1)]
+        wp_ref[:, PACKS * a + PACKED : PACKS * (a + 1)] = jnp.zeros((COUT, PACKS - PACKED), BF16)
 
 
 def shared_out(group, amounts):
@@ -142,19 +137,24 @@
 
 
 def forward_kernel(
-    key_hbm, val_hbm, query_hbm, v_ref, xr_ref, yr_ref, bias_ref, wp_ref, group_ref, early_ref,
+    near_hbm, key_hbm, val_hbm, query_hbm, bias_hbm, routes_hbm, v_ref, xr_ref, yr_ref, w_ref,
+    early_ref,
     podd_ref, peven_ref, slope_ref, hidt_ref, cott_ref, kut_ref, knt_ref, wt_ref, tt_ref, kt_ref,
-    vw_ref, send_ref,
-    key_ref, val_ref, query_ref, sems,
+    vw_ref, group_ref, send_ref,
+    near_ref, key_ref, val_ref, query_ref, bias_ref, routes_ref, sems, slot_ref, routes8_ref, wp_ref,
 ):
     copies = [
         pltpu.make_async_copy(source, target, sems.at[i])
         for i, (source, target) in enumerate(
-            ((key_hbm, key_ref), (val_hbm, val_ref), (query_hbm, query_ref))
+            (
+                (near_hbm, near_ref), (key_hbm, key_ref), (val_hbm, val_ref),
+                (query_hbm, query_ref), (bias_hbm, bias_ref), (routes_hbm, routes_ref),
+            )
         )
     ]
     for copy in copies:
         copy.start()
+    pad_weights(w_ref, wp_ref)
     here = lax.axis_index("chip") * 2 + lax.axis_index("core")
     inner = jnp.logical_and(here >= 8, lax.rem(here, 8) > 0)
     corner = early_ref[pl.ds(pl.multiple_of(16 * jnp.maximum(here - 9, 0), 16), 16), 256:384]
@@ -177,12 +177,18 @@
                     piece = jnp.concatenate([edge[8 * pz : 8 * pz + 8], piece[0:56]], axis=0)
                 if c == 0:
                     piece = jnp.where(first, 0.0, pltpu.roll(piece, 1, 0))
-                column = (3 * b + c) * LANES
-                out_ref[pl.ds(row, 64), pl.ds(column, LANES)] = piece.astype(BF16)
+                column = (3 * b + c) * CIN
+                out_ref[pl.ds(row, 64), pl.ds(column, CIN)] = piece[:, 0:CIN].astype(BF16)
+        out_ref[pl.ds(row, 64), PACKED:PACKS] = jnp.zeros((64, PACKS - PACKED), BF16)
+    for copy in copies:
+        copy.wait()
+    find_slots(near_ref, slot_ref)
+    group = row_groups(routes_ref, routes8_ref, slot_ref)
+    group_ref[...] = group
     before = (
-        nt(podd_ref[0:512, :], wp_ref[:, 0:SLOTS9])
-        + nt(peven_ref[...], wp_ref[:, SLOTS9 : 2 * SLOTS9])
-        + nt(podd_ref[64:576, :], wp_ref[:, 2 * SLOTS9 : 3 * SLOTS9])
+        nt(podd_ref[0:512, :], wp_ref[:, 0:PACKS])
+        + nt(peven_ref[...], wp_ref[:, PACKS : 2 * PACKS])
+        + nt(podd_ref[64:576, :], wp_ref[:, 2 * PACKS : 3 * PACKS])
         + bias_ref[...]
     )
     square = before * before
@@ -194,14 +200,10 @@
     slope_ref[...] = slope.T
     hidt_ref[...] = hidden.astype(F32).T.astype(BF16)
 
-    for copy in copies:
-        copy.wait()
     kh, kl = split(key_ref[...].T)
     vh, vl = split(val_ref[...])
-    kt_ref[0:COUT, :] = kh
-    kt_ref[COUT : 2 * COUT, :] = kl
-    vw_ref[0:COUT, :] = vh
-    vw_ref[COUT : 2 * COUT, :] = vl
+    kt_ref[...] = kh
+    vw_ref[...] = vh
     keys = nt(kh, hidden) + nt(kl, hidden)
     values = nn(hidden, vh) + nn(hidden, vl)
     queries = query_ref[...]
@@ -210,11 +212,8 @@
     kut = keys * key_norm
     kut_ref[...] = kut
     knt_ref[...] = jnp.broadcast_to(key_norm, (8, 512))
-    uh, ul = split(kut)
-    qh, ql = split(qu)
-    weights = jnp.exp(TEMPER * (nn(qh, uh) + nn(ql, uh) + nn(qh, ul)))
+    weights = jnp.exp(TEMPER * nn(qu.astype(BF16), kut.astype(BF16)))
     wt_ref[...] = weights
-    group = group_ref[...]
     shares = shared_out(group, weights)
     vb = values.astype(BF16)
     sums = nn(shares, jnp.concatenate([vb, jnp.ones((512, 64), BF16)], axis=1))
@@ -270,18 +269,14 @@
     queries = query_ref[...]
     qn = lax.rsqrt(jnp.sum(queries * queries, axis=-1, keepdims=True) + EPS)
     qu = queries * qn
-    ch, cl = split(d_cos)
-    qh, ql = split(qu.T)
-    d_ku = nn(qh, ch) + nn(ql, ch) + nn(qh, cl)
+    ch = d_cos.astype(BF16)
+    d_ku = nn(qu.T.astype(BF16), ch)
     d_key = knt_ref[0:1, :] * (d_ku - kut * jnp.sum(kut * d_ku, axis=0, keepdims=True))
     d_qu = nt(ch, kut.astype(BF16))
     d_query = qn * (d_qu - qu * jnp.sum(qu * d_qu, axis=-1, keepdims=True))
 
-    kh, kl = split(d_key)
-    vh, vl = split(d_value)
-    d_hidden = tn(kt_ref[0:COUT, :], kh) + tn(kt_ref[COUT : 2 * COUT, :], kh)
-    d_hidden = d_hidden + tn(kt_ref[0:COUT, :], kl) + nn(vw_ref[0:COUT, :], vl)
-    d_hidden = d_hidden + nn(vw_ref[0:COUT, :], vh) + nn(vw_ref[COUT : 2 * COUT, :], vh)
+    kh, vh = d_key.astype(BF16), d_value.astype(BF16)
+    d_hidden = tn(kt_ref[...], kh) + nn(vw_ref[...], vh)
     d_before = d_hidden * slope_ref[...]
     dbt = d_before.astype(BF16)
     d_rows = d_before.T
@@ -292,10 +287,7 @@
 
     parts = (podd_ref[0:512, :], peven_ref[...], podd_ref[64:576, :])
     for a in range(3):
-        grad = nn(dbt, parts[a])
-        for tap in range(9):
-            piece = grad[:, tap * LANES : tap * LANES + CIN]
-            sum_ref[:, pl.ds((9 * a + tap) * CIN, CIN)] = piece
+        sum_ref[:, PACKED * a : PACKED * (a + 1)] = nn(dbt, parts[a])[:, 0:PACKED]
     sum_ref[:, KDIM : KDIM + COUT] = nt(hidt_ref[...], kh)
     sum_ref[:, KDIM + COUT : KDIM + 2 * COUT] = nt(hidt_ref[...], vh)
     bias = jnp.broadcast_to(jnp.sum(d_rows, axis=0, keepdims=True), (8, COUT))
@@ -308,13 +300,11 @@
         right = sum_ref[:, LANES * (t + 12) : LANES * (t + 13)]
         keep_ref[COUT * t : COUT * (t + 1), :] = jnp.where(low, left, right)
         give_ref[COUT * t : COUT * (t + 1), :] = jnp.where(low, right, left).astype(BF16)
-    rest = HALF - 12 * COUT
-    keep_ref[12 * COUT : HALF, :] = jnp.zeros((rest, LANES), F32)
-    give_ref[12 * COUT : HALF, :] = jnp.zeros((rest, LANES), BF16)
 
 
 def add_kernel(a_ref, b_ref, out_ref):
-    out_ref[...] = (a_ref[...] + b_ref[...].astype(F32)).astype(BF16)
+    out_ref[0:USED, :] = (a_ref[...] + b_ref[...].astype(F32)).astype(BF16)
+    out_ref[USED:HALF, :] = jnp.zeros((HALF - USED, LANES), BF16)
 
 
 def total_kernel(recv_ref, out_ref):
@@ -447,37 +437,29 @@
     early = lax.all_to_all(early, SPACE, 0, 0, tiled=True).reshape(512, 3 * LANES)
     xr = shift(xs, 1, 0)
     yr = shift(ys, 0, 1)
-    wp, group = call(
-        prepare_kernel, "sh",
-        [
-            like((COUT, 27 * LANES), BF16), like((8, 512)),
-        ],
-        [
-            slots, pltpu.VMEM((8, 64), jnp.int32), pltpu.VMEM((COUT, KDIM), BF16),
-            pltpu.SemaphoreType.DMA,
-        ],
-        neighbors, conv_weight.T, routes.reshape(1, 512),
-    )
-    podd, peven, slope, hidt, cott, kut, knt, wt, tt, kt, vw, send = call(
-        forward_kernel, "hhh",
-        [
-            like((576, SLOTS9), BF16), like((512, SLOTS9), BF16), like((COUT, 512)),
+    podd, peven, slope, hidt, cott, kut, knt, wt, tt, kt, vw, group, send = call(
+        forward_kernel, "hhhhhh",
+        [
+            like((576, PACKS), BF16), like((512, PACKS), BF16), like((COUT, 512)),
             like((COUT, 512), BF16), like((COUT, 512), BF16), like((COUT, 512)), like((8, 512)),
-            like((8, 512)), like((8, 512)), like((2 * COUT, COUT), BF16),
-            like((2 * COUT, COUT), BF16), like((512, 256), BF16),
-        ],
-        [
-            pltpu.VMEM((COUT, COUT), F32), pltpu.VMEM((COUT, COUT), F32),
-            pltpu.VMEM((NQ, COUT), F32), pltpu.SemaphoreType.DMA((3,)),
-        ],
-        key_weight, value_weight, queries, v, xr, yr, conv_bias.reshape(1, COUT), wp, group, early,
+            like((8, 512)), like((8, 512)), like((COUT, COUT), BF16),
+            like((COUT, COUT), BF16), like((8, 512)), like((512, 256), BF16),
+        ],
+        [
+            pltpu.SMEM((6, 8), jnp.int32), pltpu.VMEM((COUT, COUT), F32),
+            pltpu.VMEM((COUT, COUT), F32), pltpu.VMEM((NQ, COUT), F32), pltpu.VMEM((1, COUT), F32),
+            pltpu.VMEM((1, 512), jnp.int32), pltpu.SemaphoreType.DMA((6,)), slots,
+            pltpu.VMEM((8, 64), jnp.int32), pltpu.VMEM((COUT, 3 * PACKS), BF16),
+        ],
+        neighbors, key_weight, value_weight, queries, conv_bias.reshape(1, COUT),
+        routes.reshape(1, 512), v, xr, yr, conv_weight.T, early,
     )
     recv = lax.all_to_all(send.reshape(32, 16, 256), SPACE, 0, 0, tiled=True).reshape(512, 256)
     pooled, db, bxs, bys, keep, give = call(
         backward_kernel, "",
         [
             like((16, COUT)), like((512, COUT), BF16), like((64, COUT), BF16),
-            like((64, COUT), BF16), like((HALF, LANES)), like((HALF, LANES), BF16),
+            like((64, COUT), BF16), like((USED, LANES)), like((USED, LANES), BF16),
         ],
         [pltpu.VMEM((COUT, WIDE), F32)],
         recv, podd, peven, slope, hidt, kut, knt, wt, tt, group, cott, kt, vw, queries,

time: 95 us -> 95.4 us (level)
  waiting for transfers between devices: 22.7 us -> 25.2 us
  Pallas kernels: 20.5 us -> 18.4 us
    pallas_call x8 -> x7, Pallas kernels: 20.5 us -> 18.4 us  [call(): pl.pallas_call(kernel, out_shape=outs, in_specs=in_specs, out_specs=jax.t...]
    ppermute x5, waiting for transfers between devices: 0.01 us -> 1.82 us  [shift(): return lax.ppermute(shard, SPACE, pairs)]
  transfers between devices with their start and end apart: 10 -> 10, of which waited for: 5 -> 6; matrix products, arithmetic and copies ran while one was open for 0% -> 0% of each run, Pallas kernels for 9% -> 6%
where the time goes in v6:
time: 95.4 us; the launch traced here: 94.7 us
  starting transfers between devices  35.8 us (38%)
  waiting for transfers between devices  25.2 us (26%)
  Pallas kernels  18.4 us (19%)
  blocking collectives  14.6 us (15%)
    pallas_call x7, Pallas kernels, call(): pl.pallas_call(kernel, out_shape=outs, in_specs=in_specs, out_specs=jax.t...  18.4 us
    all_to_all x1, blocking collectives, on_device(): lax.all_to_all(send.reshape(32, 16, 256), SPACE, 0, 0, tiled=True)  14.6 us
    ppermute x5, starting transfers between devices, shift(): return lax.ppermute(shard, SPACE, pairs)  11.7 us
    all_to_all x1, starting transfers between devices, on_device(): lax.all_to_all(early, SPACE, 0, 0, tiled=True).reshape(512, 3 * LANES)  9.45 us
    all_to_all x1, waiting for transfers between devices, on_device(): mine = lax.all_to_all(copies, CHIPS, 0, 0, tiled=True).reshape(HALF, LANES)  9.27 us
    all_to_all x1, waiting for transfers between devices, on_device(): lax.all_to_all(half.reshape(64, SHARD, LANES), CHIPS, 0, 0, tiled=True)  8.8 us
    all_to_all x1, starting transfers between devices, on_device(): lax.all_to_all(half.reshape(64, SHARD, LANES), CHIPS, 0, 0, tiled=True)  6.79 us
    all_to_all x1, starting transfers between devices, on_device(): mine = lax.all_to_all(copies, CHIPS, 0, 0, tiled=True).reshape(HALF, LANES)  5.72 us
  transfers between devices with their start and end apart: 10, of which 6 were waited for; matrix products, arithmetic and copies ran while one was open for 0% of the time, Pallas kernels for 6%

profile of v6, /device:TPU:1, one launch (start us, length us, event | category | flops | bytes accessed | tf_op | source)
XLA Modules:
  0.0 94.7 jit_solution(5216755980997212293)
XLA Ops:
  0.6 2.5 %place_kernel.1 = (bf16[16,4,64,128]{3,2,1,0:T(8,128)(2,1)S(1)}, bf16[256,128]{1,0:T(8,128)(2,1)S(1)}, bf16[256,128]{1,0:T(8,128)(2,1)S(1)}, bf16[32,16,384]{2,1,0:T(8,128)(2,1)}) custom-call(s32[6,8]{1,0:T(8,128)} %near_ref.1, bf16[8,96,512]{2,1,0:T(8,128)(2,1)} %bitcast.28, s32[8,512]{1,0:T(8,128)} %bitcast.26, f32[16,192]{1,0:T(8,128)} %bitcast.30), custom_call_target="tpu_custom_call" | custom-call | tf_op jit(solution)/shard_map/place_kernel/pallas_call | solution.py:398
  3.2 9.4 %all-to-all-start = ((bf16[32,16,384]{2,1,0:T(8,128)(2,1)}), bf16[32,16,384]{2,1,0:T(8,128)(2,1)S(1)}, u32[]{:S(2)}, u32[]{:S(2)}) async-start(bf16[32,16,384]{2,1,0:T(8,128)(2,1)} %get-tuple-element.44), calls=%async_computation | async-start | bytes 786432 | tf_op jit(solution)/shard_map/all_to_all | solution.py:437
  12.6 3.5 %collective-permute-start = (bf16[256,128]{1,0:T(8,128)(2,1)S(1)}, bf16[256,128]{1,0:T(8,128)(2,1)S(1)}, u32[]{:S(2)}, u32[]{:S(2)}) collective-permute-start(bf16[256,128]{1,0:T(8,128)(2,1)S(1)} %get-tuple-element.42), channel_id=1, source_target_pairs={{0,1},{1,2},{2,3},{3,4},{4,5},{5,6},{6,7},{8,9},{9,10},{10,11},{11... | collective-permute-start | bytes 196616 | tf_op jit(solution)/shard_map/ppermute | solution.py:415
  16.2 3.1 %collective-permute-start.1 = (bf16[256,128]{1,0:T(8,128)(2,1)S(1)}, bf16[256,128]{1,0:T(8,128)(2,1)S(1)}, u32[]{:S(2)}, u32[]{:S(2)}) collective-permute-start(bf16[256,128]{1,0:T(8,128)(2,1)S(1)} %get-tuple-element.43), channel_id=1, source_target_pairs={{0,8},{1,9},{2,10},{3,11},{4,12},{5,13},{6,14},{7,15},{8,16},{9,17... | collective-permute-start | bytes 196616 | tf_op jit(solution)/shard_map/ppermute | solution.py:415
  19.3 1.8 %collective-permute-done.1.yr_ref = bf16[256,128]{1,0:T(8,128)(2,1)S(1)} collective-permute-done((bf16[256,128]{1,0:T(8,128)(2,1)S(1)}, bf16[256,128]{1,0:T(8,128)(2,1)S(1)}, u32[]{:S(2)}, u32[]{:S(2)}) %collective-permute-start.1) | collective-permute-done | bytes 65568 | tf_op jit(solution)/shard_map/ppermute | solution.py:415
  21.1 1.8 %all-to-all-done = bf16[32,16,384]{2,1,0:T(8,128)(2,1)S(1)} async-done(((bf16[32,16,384]{2,1,0:T(8,128)(2,1)}), bf16[32,16,384]{2,1,0:T(8,128)(2,1)S(1)}, u32[]{:S(2)}, u32[]{:S(2)}) %all-to-all-start) | async-done | bytes 393248 | tf_op jit(solution)/shard_map/all_to_all | solution.py:437
  22.9 5.5 %forward_kernel.1 = (bf16[576,896]{1,0:T(8,128)(2,1)S(1)}, bf16[512,896]{1,0:T(8,128)(2,1)S(1)}, f32[192,512]{1,0:T(8,128)S(1)}, bf16[192,512]{1,0:T(8,128)(2,1)...) custom-call(s32[6,8]{1,0:T(8,128)} %near_ref.1, ...), custom_call_target="tpu_custom_call" | custom-call | tf_op jit(solution)/shard_map/forward_kernel/pallas_call | solution.py:398
  28.4 14.6 %all_to_all.20 = bf16[32,16,256]{2,1,0:T(8,128)(2,1)S(1)} all-to-all(bf16[32,16,256]{2,1,0:T(8,128)(2,1)S(1)} %bitcast.25), channel_id=1, replica_groups=mesh['section'=4,'chip'=16,'core'=2] {'chip','core'}, dimensions={0} | all-to-all | bytes 524288 | tf_op jit(solution)/shard_map/all_to_all | solution.py:457
  42.9 2.3 %backward_kernel.1 = (f32[16,192]{1,0:T(8,128)}, bf16[512,192]{1,0:T(8,128)(2,1)S(1)}, bf16[64,192]{1,0:T(8,128)(2,1)S(1)}, bf16[64,192]{1,0:T(8,128)(2,1)S(1)},...) custom-call(bf16[512,256]{1,0:T(8,128)(2,1)S(1)} %bitcast.24, bf16[576,896]{1,0:T(8,128)(2,1)S(1)} %get-tuple-element.46.podd_ref, ...), custom_call_target="tpu_custom_call" | custom-call | tf_op jit(solution)/shard_map/backward_kernel/pallas_call | solution.py:398
  45.3 0.2 collective-permute-start.5
  45.5 1.8 %collective-permute-done.5.b_ref = bf16[2304,128]{1,0:T(8,128)(2,1)S(1)} collective-permute-done((bf16[2304,128]{1,0:T(8,128)(2,1)S(1)}, bf16[2304,128]{1,0:T(8,128)(2,1)S(1)}, u32[]{:S(2)}, u32[]{:S(2)}) %collective-permute-start.5) | collective-permute-done | bytes 589856 | tf_op jit(solution)/shard_map/ppermute | solution.py:468
  47.3 1.0 %add_kernel.1 = bf16[2560,128]{1,0:T(8,128)(2,1)} custom-call(f32[2304,128]{1,0:T(8,128)S(1)} %get-tuple-element.61.a_ref, bf16[2304,128]{1,0:T(8,128)(2,1)S(1)} %collective-permute-done.5.b_ref), custom_call_target="tpu_custom_call" | custom-call | tf_op jit(solution)/shard_map/add_kernel/pallas_call | solution.py:398
  48.3 6.8 %all-to-all-start.2 = ((bf16[64,40,128]{2,1,0:T(8,128)(2,1)}), bf16[64,40,128]{2,1,0:T(8,128)(2,1)S(1)}, u32[]{:S(2)}, u32[]{:S(2)}) async-start(bf16[64,40,128]{2,1,0:T(8,128)(2,1)} %bitcast.11), calls=%async_computation.2 | async-start | bytes 1310720 | tf_op jit(solution)/shard_map/all_to_all | solution.py:470
  55.1 2.5 %collective-permute-start.2 = (bf16[64,192]{1,0:T(8,128)(2,1)S(1)}, bf16[64,192]{1,0:T(8,128)(2,1)S(1)}, u32[]{:S(2)}, u32[]{:S(2)}) collective-permute-start(bf16[64,192]{1,0:T(8,128)(2,1)S(1)} %get-tuple-element.59), channel_id=1, source_target_pairs={{1,0},{2,1},{3,2},{4,3},{5,4},{6,5},{7,6},{9,8},{10,9},{11,10},{12... | collective-permute-start | bytes 73736 | tf_op jit(solution)/shard_map/ppermute | solution.py:415
  57.6 1.3 %collective-permute-start.3 = (bf16[64,192]{1,0:T(8,128)(2,1)S(1)}, bf16[64,192]{1,0:T(8,128)(2,1)S(1)}, u32[]{:S(2)}, u32[]{:S(2)}) collective-permute-start(bf16[64,192]{1,0:T(8,128)(2,1)S(1)} %get-tuple-element.60), channel_id=1, source_target_pairs={{8,0},{9,1},{10,2},{11,3},{12,4},{13,5},{14,6},{15,7},{16,8},{17,9... | collective-permute-start | bytes 73736 | tf_op jit(solution)/shard_map/ppermute | solution.py:415
  58.9 1.3 %collective-permute-start.4 = (bf16[16,192]{1,0:T(8,128)(2,1)S(1)}, bf16[16,192]{1,0:T(8,128)(2,1)S(1)}, u32[]{:S(2)}, u32[]{:S(2)}) collective-permute-start(bf16[16,192]{1,0:T(8,128)(2,1)S(1)} %slice.3), channel_id=1, source_target_pairs={{9,0},{10,1},{11,2},{12,3},{13,4},{14,5},{15,6},{17,8},{18,9},{19,... | collective-permute-start | bytes 18440 | tf_op jit(solution)/shard_map/ppermute | solution.py:415
  60.2 8.8 %all-to-all-done.2.recv_ref = bf16[64,40,128]{2,1,0:T(8,128)(2,1)S(1)} async-done(((bf16[64,40,128]{2,1,0:T(8,128)(2,1)}), bf16[64,40,128]{2,1,0:T(8,128)(2,1)S(1)}, u32[]{:S(2)}, u32[]{:S(2)}) %all-to-all-start.2) | async-done | bytes 655392 | tf_op jit(solution)/shard_map/all_to_all | solution.py:470
  69.0 1.0 %total_kernel.1 = bf16[64,40,128]{2,1,0:T(8,128)(2,1)} custom-call(bf16[64,40,128]{2,1,0:T(8,128)(2,1)S(1)} %all-to-all-done.2.recv_ref), custom_call_target="tpu_custom_call" | custom-call | tf_op jit(solution)/shard_map/total_kernel/pallas_call | solution.py:398
  70.0 5.7 %all-to-all-start.3 = ((bf16[64,40,128]{2,1,0:T(8,128)(2,1)}), bf16[64,40,128]{2,1,0:T(8,128)(2,1)S(1)}, u32[]{:S(2)}, u32[]{:S(2)}) async-start(bf16[64,40,128]{2,1,0:T(8,128)(2,1)} %total_kernel.1), calls=%async_computation.3 | async-start | bytes 1310720 | tf_op jit(solution)/shard_map/all_to_all | solution.py:476
  75.7 4.5 %spread_kernel.1 = bf16[8,96,512]{2,1,0:T(8,128)(2,1)} custom-call(s32[6,8]{1,0:T(8,128)S(1)} %copy-done.2, bf16[192,2592]{1,0:T(8,128)(2,1)} %bitcast.19, bf16[512,192]{1,0:T(8,128)(2,1)S(1)} %get-tuple-element.64.db_ref, bf16[64,192]{1,0:T(8,128)(2,1)S(1)} %collective-permute-done.2.xr_ref, bf16[64,192]{1,0:T(8,128)(2,1)S(1)} %collective-permute-done.3.yr_ref, ...), custom_call_target="tpu_custom_call" | custom-call | tf_op jit(solution)/shard_map/spread_kernel/pallas_call | solution.py:398
  80.3 9.3 %all-to-all-done.3 = bf16[64,40,128]{2,1,0:T(8,128)(2,1)S(1)} async-done(((bf16[64,40,128]{2,1,0:T(8,128)(2,1)}), bf16[64,40,128]{2,1,0:T(8,128)(2,1)S(1)}, u32[]{:S(2)}, u32[]{:S(2)}) %all-to-all-start.3) | async-done | bytes 655392 | tf_op jit(solution)/shard_map/all_to_all | solution.py:476
  89.5 1.9 %collective-permute-start.6 = (bf16[2560,128]{1,0:T(8,128)(2,1)S(1)}, bf16[2560,128]{1,0:T(8,128)(2,1)S(1)}, u32[]{:S(2)}, u32[]{:S(2)}) collective-permute-start(bf16[2560,128]{1,0:T(8,128)(2,1)S(1)} %bitcast.21), channel_id=1, source_target_pairs={{0,1},{1,0},{2,3},{3,2},{4,5},{5,4},{6,7},{7,6},{8,9},{9,8},{10,11... | collective-permute-start | bytes 1966088 | tf_op jit(solution)/shard_map/ppermute | solution.py:488
  91.5 1.7 %collective-permute-done.6.other_ref = bf16[2560,128]{1,0:T(8,128)(2,1)S(1)} collective-permute-done((bf16[2560,128]{1,0:T(8,128)(2,1)S(1)}, bf16[2560,128]{1,0:T(8,128)(2,1)S(1)}, u32[]{:S(2)}, u32[]{:S(2)}) %collective-permute-start.6) | collective-permute-done | bytes 655392 | tf_op jit(solution)/shard_map/ppermute | solution.py:488
  93.2 1.6 %final_kernel.1 = (f32[192,2592]{1,0:T(8,128)}, f32[192,192]{1,0:T(8,128)}, f32[192,192]{1,0:T(8,128)}, f32[8,192]{1,0:T(8,128)}, f32[1,192]{1,0:T(1,128)}) custom-call(bf16[2560,128]{1,0:T(8,128)(2,1)S(1)} %bitcast.22, bf16[2560,128]{1,0:T(8,128)(2,1)S(1)} %collective-permute-done.6.other_ref), custom_call_target="tpu_custom_call" | custom-call | tf_op jit(solution)/shard_map/final_kernel/pallas_call | solution.py:398
  (13 shorter events, 0.0 us)
Async XLA Ops:
  0.6 22.3 %copy-start = (bf16[2592,192]{0,1:T(8,128)(2,1)S(1)}, bf16[2592,192]{0,1:T(8,128)(2,1)}, u32[]{:S(2)}) copy-start(bf16[2592,192]{0,1:T(8,128)(2,1)} %param.15) | copy-start | bytes 2985988
  3.2 39.8 %copy-start.3 = (f32[8,192]{1,0:T(8,128)S(1)}, f32[8,192]{1,0:T(8,128)}, u32[]{:S(2)}) copy-start(f32[8,192]{1,0:T(8,128)} %query_ref.1) | copy-start | bytes 18436
  3.2 19.7 %all-to-all-start = ((bf16[32,16,384]{2,1,0:T(8,128)(2,1)}), bf16[32,16,384]{2,1,0:T(8,128)(2,1)S(1)}, u32[]{:S(2)}, u32[]{:S(2)}) async-start(bf16[32,16,384]{2,1,0:T(8,128)(2,1)} %get-tuple-element.44), calls=%async_computation | async-start | bytes 786432 | tf_op jit(solution)/shard_map/all_to_all | solution.py:437
  12.6 6.7 %collective-permute-start = (bf16[256,128]{1,0:T(8,128)(2,1)S(1)}, bf16[256,128]{1,0:T(8,128)(2,1)S(1)}, u32[]{:S(2)}, u32[]{:S(2)}) collective-permute-start(bf16[256,128]{1,0:T(8,128)(2,1)S(1)} %get-tuple-element.42), channel_id=1, source_target_pairs={{0,1},{1,2},{2,3},{3,4},{4,5},{5,6},{6,7},{8,9},{9,10},{10,11},{11... | collective-permute-start | bytes 196616 | tf_op jit(solution)/shard_map/ppermute | solution.py:415
  16.2 4.9 %collective-permute-start.1 = (bf16[256,128]{1,0:T(8,128)(2,1)S(1)}, bf16[256,128]{1,0:T(8,128)(2,1)S(1)}, u32[]{:S(2)}, u32[]{:S(2)}) collective-permute-start(bf16[256,128]{1,0:T(8,128)(2,1)S(1)} %get-tuple-element.43), channel_id=1, source_target_pairs={{0,8},{1,9},{2,10},{3,11},{4,12},{5,13},{6,14},{7,15},{8,16},{9,17... | collective-permute-start | bytes 196616 | tf_op jit(solution)/shard_map/ppermute | solution.py:415
  45.3 2.0 %collective-permute-start.5 = (bf16[2304,128]{1,0:T(8,128)(2,1)S(1)}, bf16[2304,128]{1,0:T(8,128)(2,1)S(1)}, u32[]{:S(2)}, u32[]{:S(2)}) collective-permute-start(bf16[2304,128]{1,0:T(8,128)(2,1)S(1)} %get-tuple-element.62), channel_id=1, source_target_pairs={{0,1},{1,0},{2,3},{3,2},{4,5},{5,4},{6,7},{7,6},{8,9},{9,8},{10,11... | collective-permute-start | bytes 1769480 | tf_op jit(solution)/shard_map/ppermute | solution.py:468
  48.3 27.4 %copy-start.1 = (s32[1,8,512]{2,1,0:T(8,128)S(1)}, s32[1,8,512]{2,1,0:T(8,128)}, u32[]{:S(2)}) copy-start(s32[1,8,512]{2,1,0:T(8,128)} %param.11) | copy-start | bytes 49156
  48.3 27.4 %copy-start.2 = (s32[6,8]{1,0:T(8,128)S(1)}, s32[6,8]{1,0:T(8,128)}, u32[]{:S(2)}) copy-start(s32[6,8]{1,0:T(8,128)} %near_ref.1) | copy-start | bytes 580
  48.3 20.7 %all-to-all-start.2 = ((bf16[64,40,128]{2,1,0:T(8,128)(2,1)}), bf16[64,40,128]{2,1,0:T(8,128)(2,1)S(1)}, u32[]{:S(2)}, u32[]{:S(2)}) async-start(bf16[64,40,128]{2,1,0:T(8,128)(2,1)} %bitcast.11), calls=%async_computation.2 | async-start | bytes 1310720 | tf_op jit(solution)/shard_map/all_to_all | solution.py:470
  55.1 14.9 %collective-permute-start.2 = (bf16[64,192]{1,0:T(8,128)(2,1)S(1)}, bf16[64,192]{1,0:T(8,128)(2,1)S(1)}, u32[]{:S(2)}, u32[]{:S(2)}) collective-permute-start(bf16[64,192]{1,0:T(8,128)(2,1)S(1)} %get-tuple-element.59), channel_id=1, source_target_pairs={{1,0},{2,1},{3,2},{4,3},{5,4},{6,5},{7,6},{9,8},{10,9},{11,10},{12... | collective-permute-start | bytes 73736 | tf_op jit(solution)/shard_map/ppermute | solution.py:415
  57.6 12.4 %collective-permute-start.3 = (bf16[64,192]{1,0:T(8,128)(2,1)S(1)}, bf16[64,192]{1,0:T(8,128)(2,1)S(1)}, u32[]{:S(2)}, u32[]{:S(2)}) collective-permute-start(bf16[64,192]{1,0:T(8,128)(2,1)S(1)} %get-tuple-element.60), channel_id=1, source_target_pairs={{8,0},{9,1},{10,2},{11,3},{12,4},{13,5},{14,6},{15,7},{16,8},{17,9... | collective-permute-start | bytes 73736 | tf_op jit(solution)/shard_map/ppermute | solution.py:415
  58.9 11.1 %collective-permute-start.4 = (bf16[16,192]{1,0:T(8,128)(2,1)S(1)}, bf16[16,192]{1,0:T(8,128)(2,1)S(1)}, u32[]{:S(2)}, u32[]{:S(2)}) collective-permute-start(bf16[16,192]{1,0:T(8,128)(2,1)S(1)} %slice.3), channel_id=1, source_target_pairs={{9,0},{10,1},{11,2},{12,3},{13,4},{14,5},{15,6},{17,8},{18,9},{19,... | collective-permute-start | bytes 18440 | tf_op jit(solution)/shard_map/ppermute | solution.py:415
  70.0 19.6 %all-to-all-start.3 = ((bf16[64,40,128]{2,1,0:T(8,128)(2,1)}), bf16[64,40,128]{2,1,0:T(8,128)(2,1)S(1)}, u32[]{:S(2)}, u32[]{:S(2)}) async-start(bf16[64,40,128]{2,1,0:T(8,128)(2,1)} %total_kernel.1), calls=%async_computation.3 | async-start | bytes 1310720 | tf_op jit(solution)/shard_map/all_to_all | solution.py:476
  89.5 3.7 %collective-permute-start.6 = (bf16[2560,128]{1,0:T(8,128)(2,1)S(1)}, bf16[2560,128]{1,0:T(8,128)(2,1)S(1)}, u32[]{:S(2)}, u32[]{:S(2)}) collective-permute-start(bf16[2560,128]{1,0:T(8,128)(2,1)S(1)} %bitcast.21), channel_id=1, source_target_pairs={{0,1},{1,0},{2,3},{3,2},{4,5},{5,4},{6,7},{7,6},{8,9},{9,8},{10,11... | collective-permute-start | bytes 1966088 | tf_op jit(solution)/shard_map/ppermute | solution.py:488

commit v7 on v4

--- a/solution.py
+++ b/solution.py
@@ -16,6 +16,7 @@
 KDIM = 27 * CIN
 SHARD = 40
 HALF = 64 * SHARD
+USED = 12 * COUT
 WIDE = 24 * LANES
 F32, BF16 = jnp.float32, jnp.bfloat16
 SPACE = ("chip", "core")
@@ -109,10 +110,14 @@
 def prepare_kernel(
     near_ref, w_hbm, routes_ref,
     wp_ref, group_ref,
-    slot_ref, routes8_ref, w_ref, sem,
+    slot_ref, routes8_ref, w_ref, sems,
 ):
-    fetch = pltpu.make_async_copy(w_hbm, w_ref, sem)
-    fetch.start()
+    fetches = [
+        pltpu.make_async_copy(w_hbm.at[pl.ds(48 * i, 48)], w_ref.at[pl.ds(48 * i, 48)], sems.at[i])
+        for i in range(4)
+    ]
+    for fetch in fetches:
+        fetch.start()
     find_slots(near_ref, slot_ref)
     wp_ref[...] = jnp.zeros_like(wp_ref)
     for slot in range(8):
@@ -130,9 +135,11 @@
     group = jnp.sum(jnp.where(mine, spread, 0.0), axis=0, keepdims=True)
     group_ref[...] = jnp.broadcast_to(group, (8, 512))
 
-    fetch.wait()
-    for tap in range(27):
-        wp_ref[:, pl.ds(tap * LANES, CIN)] = w_ref[:, pl.ds(tap * CIN, CIN)]
+    for i, fetch in enumerate(fetches):
+        fetch.wait()
+        for tap in range(27):
+            piece = w_ref[48 * i : 48 * i + 48, tap * CIN : tap * CIN + CIN]
+            wp_ref[48 * i : 48 * i + 48, tap * LANES : tap * LANES + CIN] = piece
 
 
 def shared_out(group, amounts):
@@ -198,10 +205,8 @@
         copy.wait()
     kh, kl = split(key_ref[...].T)
     vh, vl = split(val_ref[...])
-    kt_ref[0:COUT, :] = kh
-    kt_ref[COUT : 2 * COUT, :] = kl
-    vw_ref[0:COUT, :] = vh
-    vw_ref[COUT : 2 * COUT, :] = vl
+    kt_ref[...] = kh
+    vw_ref[...] = vh
     keys = nt(kh, hidden) + nt(kl, hidden)
     values = nn(hidden, vh) + nn(hidden, vl)
     queries = query_ref[...]
@@ -210,9 +215,7 @@
     kut = keys * key_norm
     kut_ref[...] = kut
     knt_ref[...] = jnp.broadcast_to(key_norm, (8, 512))
-    uh, ul = split(kut)
-    qh, ql = split(qu)
-    weights = jnp.exp(TEMPER * (nn(qh, uh) + nn(ql, uh) + nn(qh, ul)))
+    weights = jnp.exp(TEMPER * nn(qu.astype(BF16), kut.astype(BF16)))
     wt_ref[...] = weights
     group = group_ref[...]
     shares = shared_out(group, weights)
@@ -270,18 +273,14 @@
     queries = query_ref[...]
     qn = lax.rsqrt(jnp.sum(queries * queries, axis=-1, keepdims=True) + EPS)
     qu = queries * qn
-    ch, cl = split(d_cos)
-    qh, ql = split(qu.T)
-    d_ku = nn(qh, ch) + nn(ql, ch) + nn(qh, cl)
+    ch = d_cos.astype(BF16)
+    d_ku = nn(qu.T.astype(BF16), ch)
     d_key = knt_ref[0:1, :] * (d_ku - kut * jnp.sum(kut * d_ku, axis=0, keepdims=True))
     d_qu = nt(ch, kut.astype(BF16))
     d_query = qn * (d_qu - qu * jnp.sum(qu * d_qu, axis=-1, keepdims=True))
 
-    kh, kl = split(d_key)
-    vh, vl = split(d_value)
-    d_hidden = tn(kt_ref[0:COUT, :], kh) + tn(kt_ref[COUT : 2 * COUT, :], kh)
-    d_hidden = d_hidden + tn(kt_ref[0:COUT, :], kl) + nn(vw_ref[0:COUT, :], vl)
-    d_hidden = d_hidden + nn(vw_ref[0:COUT, :], vh) + nn(vw_ref[COUT : 2 * COUT, :], vh)
+    kh, vh = d_key.astype(BF16), d_value.astype(BF16)
+    d_hidden = tn(kt_ref[...], kh) + nn(vw_ref[...], vh)
     d_before = d_hidden * slope_ref[...]
     dbt = d_before.astype(BF16)
     d_rows = d_before.T
@@ -308,13 +307,11 @@
         right = sum_ref[:, LANES * (t + 12) : LANES * (t + 13)]
         keep_ref[COUT * t : COUT * (t + 1), :] = jnp.where(low, left, right)
         give_ref[COUT * t : COUT * (t + 1), :] = jnp.where(low, right, left).astype(BF16)
-    rest = HALF - 12 * COUT
-    keep_ref[12 * COUT : HALF, :] = jnp.zeros((rest, LANES), F32)
-    give_ref[12 * COUT : HALF, :] = jnp.zeros((rest, LANES), BF16)
 
 
 def add_kernel(a_ref, b_ref, out_ref):
-    out_ref[...] = (a_ref[...] + b_ref[...].astype(F32)).astype(BF16)
+    out_ref[0:USED, :] = (a_ref[...] + b_ref[...].astype(F32)).astype(BF16)
+    out_ref[USED:HALF, :] = jnp.zeros((HALF - USED, LANES), BF16)
 
 
 def total_kernel(recv_ref, out_ref):
@@ -454,7 +451,7 @@
         ],
         [
             slots, pltpu.VMEM((8, 64), jnp.int32), pltpu.VMEM((COUT, KDIM), BF16),
-            pltpu.SemaphoreType.DMA,
+            pltpu.SemaphoreType.DMA((4,)),
         ],
         neighbors, conv_weight.T, routes.reshape(1, 512),
     )
@@ -463,8 +460,8 @@
         [
             like((576, SLOTS9), BF16), like((512, SLOTS9), BF16), like((COUT, 512)),
             like((COUT, 512), BF16), like((COUT, 512), BF16), like((COUT, 512)), like((8, 512)),
-            like((8, 512)), like((8, 512)), like((2 * COUT, COUT), BF16),
-            like((2 * COUT, COUT), BF16), like((512, 256), BF16),
+            like((8, 512)), like((8, 512)), like((COUT, COUT), BF16),
+            like((COUT, COUT), BF16), like((512, 256), BF16),
         ],
         [
             pltpu.VMEM((COUT, COUT), F32), pltpu.VMEM((COUT, COUT), F32),
@@ -477,7 +474,7 @@
         backward_kernel, "",
         [
             like((16, COUT)), like((512, COUT), BF16), like((64, COUT), BF16),
-            like((64, COUT), BF16), like((HALF, LANES)), like((HALF, LANES), BF16),
+            like((64, COUT), BF16), like((USED, LANES)), like((USED, LANES), BF16),
         ],
         [pltpu.VMEM((COUT, WIDE), F32)],
         recv, podd, peven, slope, hidt, kut, knt, wt, tt, group, cott, kt, vw, queries,

time: 95 us -> 93.3 us (0.982)
  Pallas kernels: 20.5 us -> 18.9 us
    pallas_call x8, Pallas kernels: 20.5 us -> 18.9 us  [call(): pl.pallas_call(kernel, out_shape=outs, in_specs=in_specs, out_specs=jax.t...]
where the time goes in v7:
time: 93.3 us; the launch traced here: 92.7 us
  starting transfers between devices  35.7 us (38%)
  waiting for transfers between devices  22.7 us (24%)
  Pallas kernels  18.9 us (20%)
  blocking collectives  14.6 us (16%)
    pallas_call x8, Pallas kernels, call(): pl.pallas_call(kernel, out_shape=outs, in_specs=in_specs, out_specs=jax.t...  18.9 us
    all_to_all x1, blocking collectives, on_device(): lax.all_to_all(send.reshape(32, 16, 256), SPACE, 0, 0, tiled=True)  14.6 us
    ppermute x5, starting transfers between devices, shift(): return lax.ppermute(shard, SPACE, pairs)  11.7 us
    all_to_all x1, starting transfers between devices, on_device(): lax.all_to_all(early, SPACE, 0, 0, tiled=True).reshape(512, 3 * LANES)  9.44 us
    all_to_all x1, waiting for transfers between devices, on_device(): mine = lax.all_to_all(copies, CHIPS, 0, 0, tiled=True).reshape(HALF, LANES)  9.3 us
    all_to_all x1, waiting for transfers between devices, on_device(): lax.all_to_all(half.reshape(64, SHARD, LANES), CHIPS, 0, 0, tiled=True)  8.79 us
    all_to_all x1, starting transfers between devices, on_device(): lax.all_to_all(half.reshape(64, SHARD, LANES), CHIPS, 0, 0, tiled=True)  6.66 us
    all_to_all x1, starting transfers between devices, on_device(): mine = lax.all_to_all(copies, CHIPS, 0, 0, tiled=True).reshape(HALF, LANES)  5.73 us
  transfers between devices with their start and end apart: 10, of which 5 were waited for; matrix products, arithmetic and copies ran while one was open for 0% of the time, Pallas kernels for 9%

profile of v7, /device:TPU:1, one launch (start us, length us, event | category | flops | bytes accessed | tf_op | source)
XLA Modules:
  0.0 92.7 jit_solution(14964708201593442983)
XLA Ops:
  0.7 2.4 %place_kernel.1 = (bf16[16,4,64,128]{3,2,1,0:T(8,128)(2,1)S(1)}, bf16[256,128]{1,0:T(8,128)(2,1)S(1)}, bf16[256,128]{1,0:T(8,128)(2,1)S(1)}, bf16[32,16,384]{2,1,0:T(8,128)(2,1)}) custom-call(s32[6,8]{1,0:T(8,128)} %near_ref.3, bf16[8,96,512]{2,1,0:T(8,128)(2,1)} %bitcast.30, s32[8,512]{1,0:T(8,128)} %bitcast.24, f32[16,192]{1,0:T(8,128)} %bitcast.32), custom_call_target="tpu_custom_call" | custom-call | tf_op jit(solution)/shard_map/place_kernel/pallas_call | solution.py:405
  3.1 9.4 %all-to-all-start = ((bf16[32,16,384]{2,1,0:T(8,128)(2,1)}), bf16[32,16,384]{2,1,0:T(8,128)(2,1)S(1)}, u32[]{:S(2)}, u32[]{:S(2)}) async-start(bf16[32,16,384]{2,1,0:T(8,128)(2,1)} %get-tuple-element.47), calls=%async_computation | async-start | bytes 786432 | tf_op jit(solution)/shard_map/all_to_all | solution.py:444
  12.6 3.5 %collective-permute-start = (bf16[256,128]{1,0:T(8,128)(2,1)S(1)}, bf16[256,128]{1,0:T(8,128)(2,1)S(1)}, u32[]{:S(2)}, u32[]{:S(2)}) collective-permute-start(bf16[256,128]{1,0:T(8,128)(2,1)S(1)} %get-tuple-element.43), channel_id=1, source_target_pairs={{0,1},{1,2},{2,3},{3,4},{4,5},{5,6},{6,7},{8,9},{9,10},{10,11},{11... | collective-permute-start | bytes 196616 | tf_op jit(solution)/shard_map/ppermute | solution.py:422
  16.1 3.1 %collective-permute-start.1 = (bf16[256,128]{1,0:T(8,128)(2,1)S(1)}, bf16[256,128]{1,0:T(8,128)(2,1)S(1)}, u32[]{:S(2)}, u32[]{:S(2)}) collective-permute-start(bf16[256,128]{1,0:T(8,128)(2,1)S(1)} %get-tuple-element.44), channel_id=1, source_target_pairs={{0,8},{1,9},{2,10},{3,11},{4,12},{5,13},{6,14},{7,15},{8,16},{9,17... | collective-permute-start | bytes 196616 | tf_op jit(solution)/shard_map/ppermute | solution.py:422
  19.2 2.5 %prepare_kernel.1 = (bf16[192,3456]{1,0:T(8,128)(2,1)S(1)}, f32[8,512]{1,0:T(8,128)S(1)}) custom-call(s32[6,8]{1,0:T(8,128)S(1)} %copy-done.1, bf16[192,2592]{1,0:T(8,128)(2,1)} %bitcast.28, s32[1,512]{1,0:T(1,128)S(1)} %bitcast.26), custom_call_target="tpu_custom_call" | custom-call | tf_op jit(solution)/shard_map/prepare_kernel/pallas_call | solution.py:405
  21.7 1.1 %all-to-all-done = bf16[32,16,384]{2,1,0:T(8,128)(2,1)S(1)} async-done(((bf16[32,16,384]{2,1,0:T(8,128)(2,1)}), bf16[32,16,384]{2,1,0:T(8,128)(2,1)S(1)}, u32[]{:S(2)}, u32[]{:S(2)}) %all-to-all-start) | async-done | bytes 393248 | tf_op jit(solution)/shard_map/all_to_all | solution.py:444
  22.8 3.8 %forward_kernel.1 = (bf16[576,1152]{1,0:T(8,128)(2,1)S(1)}, bf16[512,1152]{1,0:T(8,128)(2,1)S(1)}, f32[192,512]{1,0:T(8,128)S(1)}, bf16[192,512]{1,0:T(8,128)(2,...) custom-call(f32[192,192]{1,0:T(8,128)} %key_hbm.1, ...), custom_call_target="tpu_custom_call" | custom-call | tf_op jit(solution)/shard_map/forward_kernel/pallas_call | solution.py:405
  26.6 14.6 %all_to_all.20 = bf16[32,16,256]{2,1,0:T(8,128)(2,1)S(1)} all-to-all(bf16[32,16,256]{2,1,0:T(8,128)(2,1)S(1)} %bitcast.23), channel_id=1, replica_groups=mesh['section'=4,'chip'=16,'core'=2] {'chip','core'}, dimensions={0} | all-to-all | bytes 524288 | tf_op jit(solution)/shard_map/all_to_all | solution.py:472
  41.2 2.1 %backward_kernel.1 = (f32[16,192]{1,0:T(8,128)}, bf16[512,192]{1,0:T(8,128)(2,1)S(1)}, bf16[64,192]{1,0:T(8,128)(2,1)S(1)}, bf16[64,192]{1,0:T(8,128)(2,1)S(1)},...) custom-call(bf16[512,256]{1,0:T(8,128)(2,1)S(1)} %bitcast.22, bf16[576,1152]{1,0:T(8,128)(2,1)S(1)} %get-tuple-element.49.podd_ref, ...), custom_call_target="tpu_custom_call" | custom-call | tf_op jit(solution)/shard_map/backward_kernel/pallas_call | solution.py:405
  43.3 0.3 collective-permute-start.5
  43.6 1.8 %collective-permute-done.5.b_ref = bf16[2304,128]{1,0:T(8,128)(2,1)S(1)} collective-permute-done((bf16[2304,128]{1,0:T(8,128)(2,1)S(1)}, bf16[2304,128]{1,0:T(8,128)(2,1)S(1)}, u32[]{:S(2)}, u32[]{:S(2)}) %collective-permute-start.5) | collective-permute-done | bytes 589856 | tf_op jit(solution)/shard_map/ppermute | solution.py:483
  45.4 1.0 %add_kernel.1 = bf16[2560,128]{1,0:T(8,128)(2,1)} custom-call(f32[2304,128]{1,0:T(8,128)S(1)} %get-tuple-element.63.a_ref, bf16[2304,128]{1,0:T(8,128)(2,1)S(1)} %collective-permute-done.5.b_ref), custom_call_target="tpu_custom_call" | custom-call | tf_op jit(solution)/shard_map/add_kernel/pallas_call | solution.py:405
  46.3 6.7 %all-to-all-start.2 = ((bf16[64,40,128]{2,1,0:T(8,128)(2,1)}), bf16[64,40,128]{2,1,0:T(8,128)(2,1)S(1)}, u32[]{:S(2)}, u32[]{:S(2)}) async-start(bf16[64,40,128]{2,1,0:T(8,128)(2,1)} %bitcast.11), calls=%async_computation.2 | async-start | bytes 1310720 | tf_op jit(solution)/shard_map/all_to_all | solution.py:485
  53.0 2.5 %collective-permute-start.2 = (bf16[64,192]{1,0:T(8,128)(2,1)S(1)}, bf16[64,192]{1,0:T(8,128)(2,1)S(1)}, u32[]{:S(2)}, u32[]{:S(2)}) collective-permute-start(bf16[64,192]{1,0:T(8,128)(2,1)S(1)} %get-tuple-element.61), channel_id=1, source_target_pairs={{1,0},{2,1},{3,2},{4,3},{5,4},{6,5},{7,6},{9,8},{10,9},{11,10},{12... | collective-permute-start | bytes 73736 | tf_op jit(solution)/shard_map/ppermute | solution.py:422
  55.5 1.3 %collective-permute-start.3 = (bf16[64,192]{1,0:T(8,128)(2,1)S(1)}, bf16[64,192]{1,0:T(8,128)(2,1)S(1)}, u32[]{:S(2)}, u32[]{:S(2)}) collective-permute-start(bf16[64,192]{1,0:T(8,128)(2,1)S(1)} %get-tuple-element.62), channel_id=1, source_target_pairs={{8,0},{9,1},{10,2},{11,3},{12,4},{13,5},{14,6},{15,7},{16,8},{17,9... | collective-permute-start | bytes 73736 | tf_op jit(solution)/shard_map/ppermute | solution.py:422
  56.8 1.3 %collective-permute-start.4 = (bf16[16,192]{1,0:T(8,128)(2,1)S(1)}, bf16[16,192]{1,0:T(8,128)(2,1)S(1)}, u32[]{:S(2)}, u32[]{:S(2)}) collective-permute-start(bf16[16,192]{1,0:T(8,128)(2,1)S(1)} %slice.3), channel_id=1, source_target_pairs={{9,0},{10,1},{11,2},{12,3},{13,4},{14,5},{15,6},{17,8},{18,9},{19,... | collective-permute-start | bytes 18440 | tf_op jit(solution)/shard_map/ppermute | solution.py:422
  58.1 8.8 %all-to-all-done.2.recv_ref = bf16[64,40,128]{2,1,0:T(8,128)(2,1)S(1)} async-done(((bf16[64,40,128]{2,1,0:T(8,128)(2,1)}), bf16[64,40,128]{2,1,0:T(8,128)(2,1)S(1)}, u32[]{:S(2)}, u32[]{:S(2)}) %all-to-all-start.2) | async-done | bytes 655392 | tf_op jit(solution)/shard_map/all_to_all | solution.py:485
  66.9 1.0 %total_kernel.1 = bf16[64,40,128]{2,1,0:T(8,128)(2,1)} custom-call(bf16[64,40,128]{2,1,0:T(8,128)(2,1)S(1)} %all-to-all-done.2.recv_ref), custom_call_target="tpu_custom_call" | custom-call | tf_op jit(solution)/shard_map/total_kernel/pallas_call | solution.py:405
  67.9 5.7 %all-to-all-start.3 = ((bf16[64,40,128]{2,1,0:T(8,128)(2,1)}), bf16[64,40,128]{2,1,0:T(8,128)(2,1)S(1)}, u32[]{:S(2)}, u32[]{:S(2)}) async-start(bf16[64,40,128]{2,1,0:T(8,128)(2,1)} %total_kernel.1), calls=%async_computation.3 | async-start | bytes 1310720 | tf_op jit(solution)/shard_map/all_to_all | solution.py:491
  73.7 4.5 %spread_kernel.1 = bf16[8,96,512]{2,1,0:T(8,128)(2,1)} custom-call(s32[6,8]{1,0:T(8,128)S(1)} %copy-done.1, bf16[192,2592]{1,0:T(8,128)(2,1)} %bitcast.29, bf16[512,192]{1,0:T(8,128)(2,1)S(1)} %get-tuple-element.66.db_ref, bf16[64,192]{1,0:T(8,128)(2,1)S(1)} %collective-permute-done.2.xr_ref, bf16[64,192]{1,0:T(8,128)(2,1)S(1)} %collective-permute-done.3.yr_ref, ...), custom_call_target="tpu_custom_call" | custom-call | tf_op jit(solution)/shard_map/spread_kernel/pallas_call | solution.py:405
  78.2 9.3 %all-to-all-done.3 = bf16[64,40,128]{2,1,0:T(8,128)(2,1)S(1)} async-done(((bf16[64,40,128]{2,1,0:T(8,128)(2,1)}), bf16[64,40,128]{2,1,0:T(8,128)(2,1)S(1)}, u32[]{:S(2)}, u32[]{:S(2)}) %all-to-all-start.3) | async-done | bytes 655392 | tf_op jit(solution)/shard_map/all_to_all | solution.py:491
  87.5 1.9 %collective-permute-start.6 = (bf16[2560,128]{1,0:T(8,128)(2,1)S(1)}, bf16[2560,128]{1,0:T(8,128)(2,1)S(1)}, u32[]{:S(2)}, u32[]{:S(2)}) collective-permute-start(bf16[2560,128]{1,0:T(8,128)(2,1)S(1)} %bitcast.19), channel_id=1, source_target_pairs={{0,1},{1,0},{2,3},{3,2},{4,5},{5,4},{6,7},{7,6},{8,9},{9,8},{10,11... | collective-permute-start | bytes 1966088 | tf_op jit(solution)/shard_map/ppermute | solution.py:503
  89.4 1.7 %collective-permute-done.6.other_ref = bf16[2560,128]{1,0:T(8,128)(2,1)S(1)} collective-permute-done((bf16[2560,128]{1,0:T(8,128)(2,1)S(1)}, bf16[2560,128]{1,0:T(8,128)(2,1)S(1)}, u32[]{:S(2)}, u32[]{:S(2)}) %collective-permute-start.6) | collective-permute-done | bytes 655392 | tf_op jit(solution)/shard_map/ppermute | solution.py:503
  91.1 1.6 %final_kernel.1 = (f32[192,2592]{1,0:T(8,128)}, f32[192,192]{1,0:T(8,128)}, f32[192,192]{1,0:T(8,128)}, f32[8,192]{1,0:T(8,128)}, f32[1,192]{1,0:T(1,128)}) custom-call(bf16[2560,128]{1,0:T(8,128)(2,1)S(1)} %bitcast.20, bf16[2560,128]{1,0:T(8,128)(2,1)S(1)} %collective-permute-done.6.other_ref), custom_call_target="tpu_custom_call" | custom-call | tf_op jit(solution)/shard_map/final_kernel/pallas_call | solution.py:405
  (16 shorter events, 0.0 us)
Async XLA Ops:
  0.6 18.6 %copy-start.1 = (s32[6,8]{1,0:T(8,128)S(1)}, s32[6,8]{1,0:T(8,128)}, u32[]{:S(2)}) copy-start(s32[6,8]{1,0:T(8,128)} %near_ref.3) | copy-start | bytes 580
  0.6 18.6 %copy-start.3 = (s32[1,512,1]{1,2,0:T(1,128)S(1)}, s32[1,512,1]{1,2,0:T(1,128)}, u32[]{:S(2)}) copy-start(s32[1,512,1]{1,2,0:T(1,128)} %param.13) | copy-start | bytes 6148
  0.7 22.2 %copy-start.4 = (f32[192]{0:T(256)S(1)}, f32[192]{0:T(256)}, u32[]{:S(2)}) copy-start(f32[192]{0:T(256)} %param.16) | copy-start | bytes 2308
  3.1 19.7 %all-to-all-start = ((bf16[32,16,384]{2,1,0:T(8,128)(2,1)}), bf16[32,16,384]{2,1,0:T(8,128)(2,1)S(1)}, u32[]{:S(2)}, u32[]{:S(2)}) async-start(bf16[32,16,384]{2,1,0:T(8,128)(2,1)} %get-tuple-element.47), calls=%async_computation | async-start | bytes 786432 | tf_op jit(solution)/shard_map/all_to_all | solution.py:444
  12.6 9.2 %collective-permute-start = (bf16[256,128]{1,0:T(8,128)(2,1)S(1)}, bf16[256,128]{1,0:T(8,128)(2,1)S(1)}, u32[]{:S(2)}, u32[]{:S(2)}) collective-permute-start(bf16[256,128]{1,0:T(8,128)(2,1)S(1)} %get-tuple-element.43), channel_id=1, source_target_pairs={{0,1},{1,2},{2,3},{3,4},{4,5},{5,6},{6,7},{8,9},{9,10},{10,11},{11... | collective-permute-start | bytes 196616 | tf_op jit(solution)/shard_map/ppermute | solution.py:422
  16.1 5.6 %collective-permute-start.1 = (bf16[256,128]{1,0:T(8,128)(2,1)S(1)}, bf16[256,128]{1,0:T(8,128)(2,1)S(1)}, u32[]{:S(2)}, u32[]{:S(2)}) collective-permute-start(bf16[256,128]{1,0:T(8,128)(2,1)S(1)} %get-tuple-element.44), channel_id=1, source_target_pairs={{0,8},{1,9},{2,10},{3,11},{4,12},{5,13},{6,14},{7,15},{8,16},{9,17... | collective-permute-start | bytes 196616 | tf_op jit(solution)/shard_map/ppermute | solution.py:422
  22.8 18.4 %copy-start.2 = (f32[8,192]{1,0:T(8,128)S(1)}, f32[8,192]{1,0:T(8,128)}, u32[]{:S(2)}) copy-start(f32[8,192]{1,0:T(8,128)} %query_ref.1) | copy-start | bytes 18436
  43.3 2.0 %collective-permute-start.5 = (bf16[2304,128]{1,0:T(8,128)(2,1)S(1)}, bf16[2304,128]{1,0:T(8,128)(2,1)S(1)}, u32[]{:S(2)}, u32[]{:S(2)}) collective-permute-start(bf16[2304,128]{1,0:T(8,128)(2,1)S(1)} %get-tuple-element.64), channel_id=1, source_target_pairs={{0,1},{1,0},{2,3},{3,2},{4,5},{5,4},{6,7},{7,6},{8,9},{9,8},{10,11... | collective-permute-start | bytes 1769480 | tf_op jit(solution)/shard_map/ppermute | solution.py:483
  46.3 20.6 %all-to-all-start.2 = ((bf16[64,40,128]{2,1,0:T(8,128)(2,1)}), bf16[64,40,128]{2,1,0:T(8,128)(2,1)S(1)}, u32[]{:S(2)}, u32[]{:S(2)}) async-start(bf16[64,40,128]{2,1,0:T(8,128)(2,1)} %bitcast.11), calls=%async_computation.2 | async-start | bytes 1310720 | tf_op jit(solution)/shard_map/all_to_all | solution.py:485
  53.0 20.6 %copy-start = (s32[1,8,512]{2,1,0:T(8,128)S(1)}, s32[1,8,512]{2,1,0:T(8,128)}, u32[]{:S(2)}) copy-start(s32[1,8,512]{2,1,0:T(8,128)} %param.11) | copy-start | bytes 49156
  53.0 14.9 %collective-permute-start.2 = (bf16[64,192]{1,0:T(8,128)(2,1)S(1)}, bf16[64,192]{1,0:T(8,128)(2,1)S(1)}, u32[]{:S(2)}, u32[]{:S(2)}) collective-permute-start(bf16[64,192]{1,0:T(8,128)(2,1)S(1)} %get-tuple-element.61), channel_id=1, source_target_pairs={{1,0},{2,1},{3,2},{4,3},{5,4},{6,5},{7,6},{9,8},{10,9},{11,10},{12... | collective-permute-start | bytes 73736 | tf_op jit(solution)/shard_map/ppermute | solution.py:422
  55.5 12.4 %collective-permute-start.3 = (bf16[64,192]{1,0:T(8,128)(2,1)S(1)}, bf16[64,192]{1,0:T(8,128)(2,1)S(1)}, u32[]{:S(2)}, u32[]{:S(2)}) collective-permute-start(bf16[64,192]{1,0:T(8,128)(2,1)S(1)} %get-tuple-element.62), channel_id=1, source_target_pairs={{8,0},{9,1},{10,2},{11,3},{12,4},{13,5},{14,6},{15,7},{16,8},{17,9... | collective-permute-start | bytes 73736 | tf_op jit(solution)/shard_map/ppermute | solution.py:422
  56.8 11.1 %collective-permute-start.4 = (bf16[16,192]{1,0:T(8,128)(2,1)S(1)}, bf16[16,192]{1,0:T(8,128)(2,1)S(1)}, u32[]{:S(2)}, u32[]{:S(2)}) collective-permute-start(bf16[16,192]{1,0:T(8,128)(2,1)S(1)} %slice.3), channel_id=1, source_target_pairs={{9,0},{10,1},{11,2},{12,3},{13,4},{14,5},{15,6},{17,8},{18,9},{19,... | collective-permute-start | bytes 18440 | tf_op jit(solution)/shard_map/ppermute | solution.py:422
  67.9 19.6 %all-to-all-start.3 = ((bf16[64,40,128]{2,1,0:T(8,128)(2,1)}), bf16[64,40,128]{2,1,0:T(8,128)(2,1)S(1)}, u32[]{:S(2)}, u32[]{:S(2)}) async-start(bf16[64,40,128]{2,1,0:T(8,128)(2,1)} %total_kernel.1), calls=%async_computation.3 | async-start | bytes 1310720 | tf_op jit(solution)/shard_map/all_to_all | solution.py:491
  87.5 3.6 %collective-permute-start.6 = (bf16[2560,128]{1,0:T(8,128)(2,1)S(1)}, bf16[2560,128]{1,0:T(8,128)(2,1)S(1)}, u32[]{:S(2)}, u32[]{:S(2)}) collective-permute-start(bf16[2560,128]{1,0:T(8,128)(2,1)S(1)} %bitcast.19), channel_id=1, source_target_pairs={{0,1},{1,0},{2,3},{3,2},{4,5},{5,4},{6,7},{7,6},{8,9},{9,8},{10,11... | collective-permute-start | bytes 1966088 | tf_op jit(solution)/shard_map/ppermute | solution.py:503

commit v8 on v7

--- a/solution.py
+++ b/solution.py
@@ -487,7 +487,7 @@
     byr = shift(bys, 0, -1)
     bxyr = shift(bys[0:16], -1, -1)
     copies = call(total_kernel, "", like((64, SHARD, LANES), BF16), [], pieces)
-    bxr, byr, bxyr, copies = lax.optimization_barrier((bxr, byr, bxyr, copies))
+    db, bxr, byr, copies = lax.optimization_barrier((db, bxr, byr, copies))
     mine = lax.all_to_all(copies, CHIPS, 0, 0, tiled=True).reshape(HALF, LANES)
     d_features = call(
         spread_kernel, "sh", like((8, CIN, 512), BF16),

time: 93.3 us -> 92.2 us (0.988)
  starting transfers between devices: 35.7 us -> 33.9 us
    all_to_all x1, waiting for transfers between devices: 9.3 us -> 0.01 us  [on_device(): mine = lax.all_to_all(copies, CHIPS, 0, 0, tiled=True).reshape(HALF, LANES)]
    ppermute x5, waiting for transfers between devices: 0.01 us -> 8.72 us  [shift(): return lax.ppermute(shard, SPACE, pairs)]
    all_to_all x1, waiting for transfers between devices: 8.79 us -> 10.1 us  [on_device(): lax.all_to_all(half.reshape(64, SHARD, LANES), CHIPS, 0, 0, tiled=True)]
    all_to_all x1, starting transfers between devices: 5.73 us -> 4.64 us  [on_device(): mine = lax.all_to_all(copies, CHIPS, 0, 0, tiled=True).reshape(HALF, LANES)]
where the time goes in v8:
time: 92.2 us; the launch traced here: 91.6 us
  starting transfers between devices  33.9 us (37%)
  waiting for transfers between devices  23.4 us (25%)
  Pallas kernels  18.9 us (20%)
  blocking collectives  14.6 us (16%)
    pallas_call x8, Pallas kernels, call(): pl.pallas_call(kernel, out_shape=outs, in_specs=in_specs, out_specs=jax.t...  18.9 us
    all_to_all x1, blocking collectives, on_device(): lax.all_to_all(send.reshape(32, 16, 256), SPACE, 0, 0, tiled=True)  14.6 us
    ppermute x5, starting transfers between devices, shift(): return lax.ppermute(shard, SPACE, pairs)  11.7 us
    all_to_all x1, waiting for transfers between devices, on_device(): lax.all_to_all(half.reshape(64, SHARD, LANES), CHIPS, 0, 0, tiled=True)  10.1 us
    all_to_all x1, starting transfers between devices, on_device(): lax.all_to_all(early, SPACE, 0, 0, tiled=True).reshape(512, 3 * LANES)  9.44 us
    ppermute x5, waiting for transfers between devices, shift(): return lax.ppermute(shard, SPACE, pairs)  8.72 us
    all_to_all x1, starting transfers between devices, on_device(): lax.all_to_all(half.reshape(64, SHARD, LANES), CHIPS, 0, 0, tiled=True)  6.66 us
    all_to_all x1, starting transfers between devices, on_device(): mine = lax.all_to_all(copies, CHIPS, 0, 0, tiled=True).reshape(HALF, LANES)  4.64 us
  transfers between devices with their start and end apart: 10, of which 5 were waited for; matrix products, arithmetic and copies ran while one was open for 0% of the time, Pallas kernels for 9%

profile of v8, /device:TPU:1, one launch (start us, length us, event | category | flops | bytes accessed | tf_op | source)
XLA Modules:
  0.0 91.6 jit_solution(3714724288210575657)
XLA Ops:
  0.7 2.4 %place_kernel.1 = (bf16[16,4,64,128]{3,2,1,0:T(8,128)(2,1)S(1)}, bf16[256,128]{1,0:T(8,128)(2,1)S(1)}, bf16[256,128]{1,0:T(8,128)(2,1)S(1)}, bf16[32,16,384]{2,1,0:T(8,128)(2,1)}) custom-call(s32[6,8]{1,0:T(8,128)} %near_ref.3, bf16[8,96,512]{2,1,0:T(8,128)(2,1)} %bitcast.30, s32[8,512]{1,0:T(8,128)} %bitcast.24, f32[16,192]{1,0:T(8,128)} %bitcast.32), custom_call_target="tpu_custom_call" | custom-call | tf_op jit(solution)/shard_map/place_kernel/pallas_call | solution.py:405
  3.1 9.4 %all-to-all-start = ((bf16[32,16,384]{2,1,0:T(8,128)(2,1)}), bf16[32,16,384]{2,1,0:T(8,128)(2,1)S(1)}, u32[]{:S(2)}, u32[]{:S(2)}) async-start(bf16[32,16,384]{2,1,0:T(8,128)(2,1)} %get-tuple-element.47), calls=%async_computation | async-start | bytes 786432 | tf_op jit(solution)/shard_map/all_to_all | solution.py:444
  12.6 3.5 %collective-permute-start = (bf16[256,128]{1,0:T(8,128)(2,1)S(1)}, bf16[256,128]{1,0:T(8,128)(2,1)S(1)}, u32[]{:S(2)}, u32[]{:S(2)}) collective-permute-start(bf16[256,128]{1,0:T(8,128)(2,1)S(1)} %get-tuple-element.43), channel_id=1, source_target_pairs={{0,1},{1,2},{2,3},{3,4},{4,5},{5,6},{6,7},{8,9},{9,10},{10,11},{11... | collective-permute-start | bytes 196616 | tf_op jit(solution)/shard_map/ppermute | solution.py:422
  16.1 3.1 %collective-permute-start.1 = (bf16[256,128]{1,0:T(8,128)(2,1)S(1)}, bf16[256,128]{1,0:T(8,128)(2,1)S(1)}, u32[]{:S(2)}, u32[]{:S(2)}) collective-permute-start(bf16[256,128]{1,0:T(8,128)(2,1)S(1)} %get-tuple-element.44), channel_id=1, source_target_pairs={{0,8},{1,9},{2,10},{3,11},{4,12},{5,13},{6,14},{7,15},{8,16},{9,17... | collective-permute-start | bytes 196616 | tf_op jit(solution)/shard_map/ppermute | solution.py:422
  19.2 2.5 %prepare_kernel.1 = (bf16[192,3456]{1,0:T(8,128)(2,1)S(1)}, f32[8,512]{1,0:T(8,128)S(1)}) custom-call(s32[6,8]{1,0:T(8,128)S(1)} %copy-done.1, bf16[192,2592]{1,0:T(8,128)(2,1)} %bitcast.28, s32[1,512]{1,0:T(1,128)S(1)} %bitcast.26), custom_call_target="tpu_custom_call" | custom-call | tf_op jit(solution)/shard_map/prepare_kernel/pallas_call | solution.py:405
  21.7 1.1 %all-to-all-done = bf16[32,16,384]{2,1,0:T(8,128)(2,1)S(1)} async-done(((bf16[32,16,384]{2,1,0:T(8,128)(2,1)}), bf16[32,16,384]{2,1,0:T(8,128)(2,1)S(1)}, u32[]{:S(2)}, u32[]{:S(2)}) %all-to-all-start) | async-done | bytes 393248 | tf_op jit(solution)/shard_map/all_to_all | solution.py:444
  22.8 3.8 %forward_kernel.1 = (bf16[576,1152]{1,0:T(8,128)(2,1)S(1)}, bf16[512,1152]{1,0:T(8,128)(2,1)S(1)}, f32[192,512]{1,0:T(8,128)S(1)}, bf16[192,512]{1,0:T(8,128)(2,...) custom-call(f32[192,192]{1,0:T(8,128)} %key_hbm.1, ...), custom_call_target="tpu_custom_call" | custom-call | tf_op jit(solution)/shard_map/forward_kernel/pallas_call | solution.py:405
  26.6 14.6 %all_to_all.20 = bf16[32,16,256]{2,1,0:T(8,128)(2,1)S(1)} all-to-all(bf16[32,16,256]{2,1,0:T(8,128)(2,1)S(1)} %bitcast.23), channel_id=1, replica_groups=mesh['section'=4,'chip'=16,'core'=2] {'chip','core'}, dimensions={0} | all-to-all | bytes 524288 | tf_op jit(solution)/shard_map/all_to_all | solution.py:472
  41.2 2.1 %backward_kernel.1 = (f32[16,192]{1,0:T(8,128)}, bf16[512,192]{1,0:T(8,128)(2,1)S(1)}, bf16[64,192]{1,0:T(8,128)(2,1)S(1)}, bf16[64,192]{1,0:T(8,128)(2,1)S(1)},...) custom-call(bf16[512,256]{1,0:T(8,128)(2,1)S(1)} %bitcast.22, bf16[576,1152]{1,0:T(8,128)(2,1)S(1)} %get-tuple-element.49.podd_ref, ...), custom_call_target="tpu_custom_call" | custom-call | tf_op jit(solution)/shard_map/backward_kernel/pallas_call | solution.py:405
  43.3 0.3 collective-permute-start.4
  43.6 1.8 %collective-permute-done.4.b_ref = bf16[2304,128]{1,0:T(8,128)(2,1)S(1)} collective-permute-done((bf16[2304,128]{1,0:T(8,128)(2,1)S(1)}, bf16[2304,128]{1,0:T(8,128)(2,1)S(1)}, u32[]{:S(2)}, u32[]{:S(2)}) %collective-permute-start.4) | collective-permute-done | bytes 589856 | tf_op jit(solution)/shard_map/ppermute | solution.py:483
  45.4 1.0 %add_kernel.1 = bf16[2560,128]{1,0:T(8,128)(2,1)} custom-call(f32[2304,128]{1,0:T(8,128)S(1)} %get-tuple-element.64.a_ref, bf16[2304,128]{1,0:T(8,128)(2,1)S(1)} %collective-permute-done.4.b_ref), custom_call_target="tpu_custom_call" | custom-call | tf_op jit(solution)/shard_map/add_kernel/pallas_call | solution.py:405
  46.3 6.7 %all-to-all-start.2 = ((bf16[64,40,128]{2,1,0:T(8,128)(2,1)}), bf16[64,40,128]{2,1,0:T(8,128)(2,1)S(1)}, u32[]{:S(2)}, u32[]{:S(2)}) async-start(bf16[64,40,128]{2,1,0:T(8,128)(2,1)} %bitcast.11), calls=%async_computation.2 | async-start | bytes 1310720 | tf_op jit(solution)/shard_map/all_to_all | solution.py:485
  53.0 2.5 %collective-permute-start.2 = (bf16[64,192]{1,0:T(8,128)(2,1)S(1)}, bf16[64,192]{1,0:T(8,128)(2,1)S(1)}, u32[]{:S(2)}, u32[]{:S(2)}) collective-permute-start(bf16[64,192]{1,0:T(8,128)(2,1)S(1)} %get-tuple-element.62), channel_id=1, source_target_pairs={{1,0},{2,1},{3,2},{4,3},{5,4},{6,5},{7,6},{9,8},{10,9},{11,10},{12... | collective-permute-start | bytes 73736 | tf_op jit(solution)/shard_map/ppermute | solution.py:422
  55.5 1.3 %collective-permute-start.3 = (bf16[64,192]{1,0:T(8,128)(2,1)S(1)}, bf16[64,192]{1,0:T(8,128)(2,1)S(1)}, u32[]{:S(2)}, u32[]{:S(2)}) collective-permute-start(bf16[64,192]{1,0:T(8,128)(2,1)S(1)} %get-tuple-element.63), channel_id=1, source_target_pairs={{8,0},{9,1},{10,2},{11,3},{12,4},{13,5},{14,6},{15,7},{16,8},{17,9... | collective-permute-start | bytes 73736 | tf_op jit(solution)/shard_map/ppermute | solution.py:422
  56.8 10.1 %all-to-all-done.2.recv_ref = bf16[64,40,128]{2,1,0:T(8,128)(2,1)S(1)} async-done(((bf16[64,40,128]{2,1,0:T(8,128)(2,1)}), bf16[64,40,128]{2,1,0:T(8,128)(2,1)S(1)}, u32[]{:S(2)}, u32[]{:S(2)}) %all-to-all-start.2) | async-done | bytes 655392 | tf_op jit(solution)/shard_map/all_to_all | solution.py:485
  66.9 1.0 %total_kernel.1 = bf16[64,40,128]{2,1,0:T(8,128)(2,1)} custom-call(bf16[64,40,128]{2,1,0:T(8,128)(2,1)S(1)} %all-to-all-done.2.recv_ref), custom_call_target="tpu_custom_call" | custom-call | tf_op jit(solution)/shard_map/total_kernel/pallas_call | solution.py:405
  67.9 4.6 %all-to-all-start.3 = ((bf16[64,40,128]{2,1,0:T(8,128)(2,1)}), bf16[64,40,128]{2,1,0:T(8,128)(2,1)S(1)}, u32[]{:S(2)}, u32[]{:S(2)}) async-start(bf16[64,40,128]{2,1,0:T(8,128)(2,1)} %total_kernel.1), calls=%async_computation.3 | async-start | bytes 1310720 | tf_op jit(solution)/shard_map/all_to_all | solution.py:491
  72.6 1.3 %collective-permute-start.5 = (bf16[16,192]{1,0:T(8,128)(2,1)S(1)}, bf16[16,192]{1,0:T(8,128)(2,1)S(1)}, u32[]{:S(2)}, u32[]{:S(2)}) collective-permute-start(bf16[16,192]{1,0:T(8,128)(2,1)S(1)} %slice.3), channel_id=1, source_target_pairs={{9,0},{10,1},{11,2},{12,3},{13,4},{14,5},{15,6},{17,8},{18,9},{19,... | collective-permute-start | bytes 18440 | tf_op jit(solution)/shard_map/ppermute | solution.py:422
  73.9 8.7 %collective-permute-done.5.xyr_ref = bf16[16,192]{1,0:T(8,128)(2,1)S(1)} collective-permute-done((bf16[16,192]{1,0:T(8,128)(2,1)S(1)}, bf16[16,192]{1,0:T(8,128)(2,1)S(1)}, u32[]{:S(2)}, u32[]{:S(2)}) %collective-permute-start.5) | collective-permute-done | bytes 6176 | tf_op jit(solution)/shard_map/ppermute | solution.py:422
  82.6 4.5 %spread_kernel.1 = bf16[8,96,512]{2,1,0:T(8,128)(2,1)} custom-call(s32[6,8]{1,0:T(8,128)S(1)} %copy-done.1, bf16[192,2592]{1,0:T(8,128)(2,1)} %bitcast.29, bf16[512,192]{1,0:T(8,128)(2,1)S(1)} %get-tuple-element.67.db_ref, bf16[64,192]{1,0:T(8,128)(2,1)S(1)} %collective-permute-done.2.xr_ref, bf16[64,192]{1,0:T(8,128)(2,1)S(1)} %collective-permute-done.3.yr_ref, ...), custom_call_target="tpu_custom_call" | custom-call | tf_op jit(solution)/shard_map/spread_kernel/pallas_call | solution.py:405
  87.1 1.2 %collective-permute-start.6 = (bf16[2560,128]{1,0:T(8,128)(2,1)S(1)}, bf16[2560,128]{1,0:T(8,128)(2,1)S(1)}, u32[]{:S(2)}, u32[]{:S(2)}) collective-permute-start(bf16[2560,128]{1,0:T(8,128)(2,1)S(1)} %bitcast.19), channel_id=1, source_target_pairs={{0,1},{1,0},{2,3},{3,2},{4,5},{5,4},{6,7},{7,6},{8,9},{9,8},{10,11... | collective-permute-start | bytes 1966088 | tf_op jit(solution)/shard_map/ppermute | solution.py:503
  88.3 1.7 %collective-permute-done.6.other_ref = bf16[2560,128]{1,0:T(8,128)(2,1)S(1)} collective-permute-done((bf16[2560,128]{1,0:T(8,128)(2,1)S(1)}, bf16[2560,128]{1,0:T(8,128)(2,1)S(1)}, u32[]{:S(2)}, u32[]{:S(2)}) %collective-permute-start.6) | collective-permute-done | bytes 655392 | tf_op jit(solution)/shard_map/ppermute | solution.py:503
  90.1 1.6 %final_kernel.1 = (f32[192,2592]{1,0:T(8,128)}, f32[192,192]{1,0:T(8,128)}, f32[192,192]{1,0:T(8,128)}, f32[8,192]{1,0:T(8,128)}, f32[1,192]{1,0:T(1,128)}) custom-call(bf16[2560,128]{1,0:T(8,128)(2,1)S(1)} %bitcast.20, bf16[2560,128]{1,0:T(8,128)(2,1)S(1)} %collective-permute-done.6.other_ref), custom_call_target="tpu_custom_call" | custom-call | tf_op jit(solution)/shard_map/final_kernel/pallas_call | solution.py:405
  (16 shorter events, 0.0 us)
Async XLA Ops:
  0.6 18.6 %copy-start.1 = (s32[6,8]{1,0:T(8,128)S(1)}, s32[6,8]{1,0:T(8,128)}, u32[]{:S(2)}) copy-start(s32[6,8]{1,0:T(8,128)} %near_ref.3) | copy-start | bytes 580
  0.6 18.6 %copy-start.3 = (s32[1,512,1]{1,2,0:T(1,128)S(1)}, s32[1,512,1]{1,2,0:T(1,128)}, u32[]{:S(2)}) copy-start(s32[1,512,1]{1,2,0:T(1,128)} %param.13) | copy-start | bytes 6148
  0.7 22.2 %copy-start.4 = (f32[192]{0:T(256)S(1)}, f32[192]{0:T(256)}, u32[]{:S(2)}) copy-start(f32[192]{0:T(256)} %param.16) | copy-start | bytes 2308
  3.1 19.7 %all-to-all-start = ((bf16[32,16,384]{2,1,0:T(8,128)(2,1)}), bf16[32,16,384]{2,1,0:T(8,128)(2,1)S(1)}, u32[]{:S(2)}, u32[]{:S(2)}) async-start(bf16[32,16,384]{2,1,0:T(8,128)(2,1)} %get-tuple-element.47), calls=%async_computation | async-start | bytes 786432 | tf_op jit(solution)/shard_map/all_to_all | solution.py:444
  12.6 9.2 %collective-permute-start = (bf16[256,128]{1,0:T(8,128)(2,1)S(1)}, bf16[256,128]{1,0:T(8,128)(2,1)S(1)}, u32[]{:S(2)}, u32[]{:S(2)}) collective-permute-start(bf16[256,128]{1,0:T(8,128)(2,1)S(1)} %get-tuple-element.43), channel_id=1, source_target_pairs={{0,1},{1,2},{2,3},{3,4},{4,5},{5,6},{6,7},{8,9},{9,10},{10,11},{11... | collective-permute-start | bytes 196616 | tf_op jit(solution)/shard_map/ppermute | solution.py:422
  16.1 5.6 %collective-permute-start.1 = (bf16[256,128]{1,0:T(8,128)(2,1)S(1)}, bf16[256,128]{1,0:T(8,128)(2,1)S(1)}, u32[]{:S(2)}, u32[]{:S(2)}) collective-permute-start(bf16[256,128]{1,0:T(8,128)(2,1)S(1)} %get-tuple-element.44), channel_id=1, source_target_pairs={{0,8},{1,9},{2,10},{3,11},{4,12},{5,13},{6,14},{7,15},{8,16},{9,17... | collective-permute-start | bytes 196616 | tf_op jit(solution)/shard_map/ppermute | solution.py:422
  22.8 18.4 %copy-start.2 = (f32[8,192]{1,0:T(8,128)S(1)}, f32[8,192]{1,0:T(8,128)}, u32[]{:S(2)}) copy-start(f32[8,192]{1,0:T(8,128)} %query_ref.1) | copy-start | bytes 18436
  43.3 2.0 %collective-permute-start.4 = (bf16[2304,128]{1,0:T(8,128)(2,1)S(1)}, bf16[2304,128]{1,0:T(8,128)(2,1)S(1)}, u32[]{:S(2)}, u32[]{:S(2)}) collective-permute-start(bf16[2304,128]{1,0:T(8,128)(2,1)S(1)} %get-tuple-element.65), channel_id=1, source_target_pairs={{0,1},{1,0},{2,3},{3,2},{4,5},{5,4},{6,7},{7,6},{8,9},{9,8},{10,11... | collective-permute-start | bytes 1769480 | tf_op jit(solution)/shard_map/ppermute | solution.py:483
  46.3 20.6 %all-to-all-start.2 = ((bf16[64,40,128]{2,1,0:T(8,128)(2,1)}), bf16[64,40,128]{2,1,0:T(8,128)(2,1)S(1)}, u32[]{:S(2)}, u32[]{:S(2)}) async-start(bf16[64,40,128]{2,1,0:T(8,128)(2,1)} %bitcast.11), calls=%async_computation.2 | async-start | bytes 1310720 | tf_op jit(solution)/shard_map/all_to_all | solution.py:485
  53.0 29.6 %copy-start = (s32[1,8,512]{2,1,0:T(8,128)S(1)}, s32[1,8,512]{2,1,0:T(8,128)}, u32[]{:S(2)}) copy-start(s32[1,8,512]{2,1,0:T(8,128)} %param.11) | copy-start | bytes 49156
  53.0 14.9 %collective-permute-start.2 = (bf16[64,192]{1,0:T(8,128)(2,1)S(1)}, bf16[64,192]{1,0:T(8,128)(2,1)S(1)}, u32[]{:S(2)}, u32[]{:S(2)}) collective-permute-start(bf16[64,192]{1,0:T(8,128)(2,1)S(1)} %get-tuple-element.62), channel_id=1, source_target_pairs={{1,0},{2,1},{3,2},{4,3},{5,4},{6,5},{7,6},{9,8},{10,9},{11,10},{12... | collective-permute-start | bytes 73736 | tf_op jit(solution)/shard_map/ppermute | solution.py:422
  55.5 12.4 %collective-permute-start.3 = (bf16[64,192]{1,0:T(8,128)(2,1)S(1)}, bf16[64,192]{1,0:T(8,128)(2,1)S(1)}, u32[]{:S(2)}, u32[]{:S(2)}) collective-permute-start(bf16[64,192]{1,0:T(8,128)(2,1)S(1)} %get-tuple-element.63), channel_id=1, source_target_pairs={{8,0},{9,1},{10,2},{11,3},{12,4},{13,5},{14,6},{15,7},{16,8},{17,9... | collective-permute-start | bytes 73736 | tf_op jit(solution)/shard_map/ppermute | solution.py:422
  67.9 19.2 %all-to-all-start.3 = ((bf16[64,40,128]{2,1,0:T(8,128)(2,1)}), bf16[64,40,128]{2,1,0:T(8,128)(2,1)S(1)}, u32[]{:S(2)}, u32[]{:S(2)}) async-start(bf16[64,40,128]{2,1,0:T(8,128)(2,1)} %total_kernel.1), calls=%async_computation.3 | async-start | bytes 1310720 | tf_op jit(solution)/shard_map/all_to_all | solution.py:491
  72.6 10.0 %collective-permute-start.5 = (bf16[16,192]{1,0:T(8,128)(2,1)S(1)}, bf16[16,192]{1,0:T(8,128)(2,1)S(1)}, u32[]{:S(2)}, u32[]{:S(2)}) collective-permute-start(bf16[16,192]{1,0:T(8,128)(2,1)S(1)} %slice.3), channel_id=1, source_target_pairs={{9,0},{10,1},{11,2},{12,3},{13,4},{14,5},{15,6},{17,8},{18,9},{19,... | collective-permute-start | bytes 18440 | tf_op jit(solution)/shard_map/ppermute | solution.py:422
  87.1 2.9 %collective-permute-start.6 = (bf16[2560,128]{1,0:T(8,128)(2,1)S(1)}, bf16[2560,128]{1,0:T(8,128)(2,1)S(1)}, u32[]{:S(2)}, u32[]{:S(2)}) collective-permute-start(bf16[2560,128]{1,0:T(8,128)(2,1)S(1)} %bitcast.19), channel_id=1, source_target_pairs={{0,1},{1,0},{2,3},{3,2},{4,5},{5,4},{6,7},{7,6},{8,9},{9,8},{10,11... | collective-permute-start | bytes 1966088 | tf_op jit(solution)/shard_map/ppermute | solution.py:503

commit v9 on v8

--- a/solution.py
+++ b/solution.py
@@ -335,11 +335,9 @@
 
 
 def spread_kernel(
-    near_ref, w_hbm, db_ref, xr_ref, yr_ref, xyr_ref, occ_ref, out_ref,
-    ext_ref, even_ref, odd_ref, rows_ref, slot_ref, w_ref, wp_ref, sem,
+    near_ref, w_ref, db_ref, xr_ref, yr_ref, xyr_ref, occ_ref, out_ref,
+    ext_ref, even_ref, odd_ref, rows_ref, slot_ref, wp_ref,
 ):
-    fetch = pltpu.make_async_copy(w_hbm, w_ref, sem)
-    fetch.start()
     wp_ref[...] = jnp.zeros_like(wp_ref)
     find_slots(near_ref, slot_ref)
     edge = yr_ref[...].astype(F32)
@@ -350,7 +348,6 @@
     ext_ref[pl.ds(640, 8), :] = xyr_ref[...].astype(F32)[0:8]
     low = ext_ref[0:576, :].astype(BF16)
     high = ext_ref[72:648, :].astype(BF16)
-    fetch.wait()
     for number in range(27):
         wp_ref[:, pl.ds(number * LANES, CIN)] = w_ref[:, pl.ds(number * CIN, CIN)]
     even_ref[...] = nn(low, wp_ref[:, SLOTS9 : 2 * SLOTS9])
@@ -490,12 +487,11 @@
     db, bxr, byr, copies = lax.optimization_barrier((db, bxr, byr, copies))
     mine = lax.all_to_all(copies, CHIPS, 0, 0, tiled=True).reshape(HALF, LANES)
     d_features = call(
-        spread_kernel, "sh", like((8, CIN, 512), BF16),
+        spread_kernel, "s", like((8, CIN, 512), BF16),
         [
             pltpu.VMEM((648, COUT), F32), pltpu.VMEM((576, SLOTS9), F32),
             pltpu.VMEM((576, SLOTS9), F32), pltpu.VMEM((1024, LANES), F32), slots,
-            pltpu.VMEM((COUT, KDIM), BF16), pltpu.VMEM((COUT, 27 * LANES), BF16),
-            pltpu.SemaphoreType.DMA,
+            pltpu.VMEM((COUT, 27 * LANES), BF16),
         ],
         neighbors, conv_weight.T, db, bxr, byr, bxyr, occupancy,
     )

time: 92.2 us -> 92.2 us (level)
  starting transfers between devices: 33.9 us -> 35.2 us
  Pallas kernels: 18.9 us -> 17.7 us
    ppermute x1, starting transfers between devices: 1.19 us -> 2.37 us  [on_device(): other = lax.ppermute(mine, 'core', swap)]
    pallas_call x8, Pallas kernels: 18.9 us -> 17.7 us  [call(): pl.pallas_call(kernel, out_shape=outs, in_specs=in_specs, out_specs=jax.t...]
  transfers between devices with their start and end apart: 10 -> 10, of which waited for: 5 -> 5; matrix products, arithmetic and copies ran while one was open for 0% -> 0% of each run, Pallas kernels for 9% -> 7%
where the time goes in v9:
time: 92.2 us; the launch traced here: 91.6 us
  starting transfers between devices  35.2 us (38%)
  waiting for transfers between devices  23.3 us (25%)
  Pallas kernels  17.7 us (19%)
  blocking collectives  14.6 us (16%)
    pallas_call x8, Pallas kernels, call(): pl.pallas_call(kernel, out_shape=outs, in_specs=in_specs, out_specs=jax.t...  17.7 us
    all_to_all x1, blocking collectives, on_device(): lax.all_to_all(send.reshape(32, 16, 256), SPACE, 0, 0, tiled=True)  14.6 us
    ppermute x5, starting transfers between devices, shift(): return lax.ppermute(shard, SPACE, pairs)  11.8 us
    all_to_all x1, waiting for transfers between devices, on_device(): lax.all_to_all(half.reshape(64, SHARD, LANES), CHIPS, 0, 0, tiled=True)  9.96 us
    all_to_all x1, starting transfers between devices, on_device(): lax.all_to_all(early, SPACE, 0, 0, tiled=True).reshape(512, 3 * LANES)  9.44 us
    ppermute x5, waiting for transfers between devices, shift(): return lax.ppermute(shard, SPACE, pairs)  8.72 us
    all_to_all x1, starting transfers between devices, on_device(): lax.all_to_all(half.reshape(64, SHARD, LANES), CHIPS, 0, 0, tiled=True)  6.66 us
    all_to_all x1, starting transfers between devices, on_device(): mine = lax.all_to_all(copies, CHIPS, 0, 0, tiled=True).reshape(HALF, LANES)  4.64 us
  transfers between devices with their start and end apart: 10, of which 5 were waited for; matrix products, arithmetic and copies ran while one was open for 0% of the time, Pallas kernels for 7%

profile of v9, /device:TPU:1, one launch (start us, length us, event | category | flops | bytes accessed | tf_op | source)
XLA Modules:
  0.0 91.6 jit_solution(11792646695307775213)
XLA Ops:
  0.7 2.4 %place_kernel.1 = (bf16[16,4,64,128]{3,2,1,0:T(8,128)(2,1)S(1)}, bf16[256,128]{1,0:T(8,128)(2,1)S(1)}, bf16[256,128]{1,0:T(8,128)(2,1)S(1)}, bf16[32,16,384]{2,1,0:T(8,128)(2,1)}) custom-call(s32[6,8]{1,0:T(8,128)} %near_ref.3, bf16[8,96,512]{2,1,0:T(8,128)(2,1)} %bitcast.30, s32[8,512]{1,0:T(8,128)} %bitcast.26, f32[16,192]{1,0:T(8,128)} %bitcast.32), custom_call_target="tpu_custom_call" | custom-call | tf_op jit(solution)/shard_map/place_kernel/pallas_call | solution.py:402
  3.1 9.4 %all-to-all-start = ((bf16[32,16,384]{2,1,0:T(8,128)(2,1)}), bf16[32,16,384]{2,1,0:T(8,128)(2,1)S(1)}, u32[]{:S(2)}, u32[]{:S(2)}) async-start(bf16[32,16,384]{2,1,0:T(8,128)(2,1)} %get-tuple-element.47), calls=%async_computation | async-start | bytes 786432 | tf_op jit(solution)/shard_map/all_to_all | solution.py:441
  12.6 3.5 %collective-permute-start = (bf16[256,128]{1,0:T(8,128)(2,1)S(1)}, bf16[256,128]{1,0:T(8,128)(2,1)S(1)}, u32[]{:S(2)}, u32[]{:S(2)}) collective-permute-start(bf16[256,128]{1,0:T(8,128)(2,1)S(1)} %get-tuple-element.43), channel_id=1, source_target_pairs={{0,1},{1,2},{2,3},{3,4},{4,5},{5,6},{6,7},{8,9},{9,10},{10,11},{11... | collective-permute-start | bytes 196616 | tf_op jit(solution)/shard_map/ppermute | solution.py:419
  16.1 3.1 %collective-permute-start.1 = (bf16[256,128]{1,0:T(8,128)(2,1)S(1)}, bf16[256,128]{1,0:T(8,128)(2,1)S(1)}, u32[]{:S(2)}, u32[]{:S(2)}) collective-permute-start(bf16[256,128]{1,0:T(8,128)(2,1)S(1)} %get-tuple-element.44), channel_id=1, source_target_pairs={{0,8},{1,9},{2,10},{3,11},{4,12},{5,13},{6,14},{7,15},{8,16},{9,17... | collective-permute-start | bytes 196616 | tf_op jit(solution)/shard_map/ppermute | solution.py:419
  19.2 2.5 %prepare_kernel.1 = (bf16[192,3456]{1,0:T(8,128)(2,1)S(1)}, f32[8,512]{1,0:T(8,128)S(1)}) custom-call(s32[6,8]{1,0:T(8,128)S(1)} %copy-done.2, bf16[192,2592]{1,0:T(8,128)(2,1)} %bitcast.19, s32[1,512]{1,0:T(1,128)S(1)} %bitcast.28), custom_call_target="tpu_custom_call" | custom-call | tf_op jit(solution)/shard_map/prepare_kernel/pallas_call | solution.py:402
  21.7 1.1 %all-to-all-done = bf16[32,16,384]{2,1,0:T(8,128)(2,1)S(1)} async-done(((bf16[32,16,384]{2,1,0:T(8,128)(2,1)}), bf16[32,16,384]{2,1,0:T(8,128)(2,1)S(1)}, u32[]{:S(2)}, u32[]{:S(2)}) %all-to-all-start) | async-done | bytes 393248 | tf_op jit(solution)/shard_map/all_to_all | solution.py:441
  22.8 3.8 %forward_kernel.1 = (bf16[576,1152]{1,0:T(8,128)(2,1)S(1)}, bf16[512,1152]{1,0:T(8,128)(2,1)S(1)}, f32[192,512]{1,0:T(8,128)S(1)}, bf16[192,512]{1,0:T(8,128)(2,...) custom-call(f32[192,192]{1,0:T(8,128)} %key_hbm.1, ...), custom_call_target="tpu_custom_call" | custom-call | tf_op jit(solution)/shard_map/forward_kernel/pallas_call | solution.py:402
  26.6 14.6 %all_to_all.20 = bf16[32,16,256]{2,1,0:T(8,128)(2,1)S(1)} all-to-all(bf16[32,16,256]{2,1,0:T(8,128)(2,1)S(1)} %bitcast.25), channel_id=1, replica_groups=mesh['section'=4,'chip'=16,'core'=2] {'chip','core'}, dimensions={0} | all-to-all | bytes 524288 | tf_op jit(solution)/shard_map/all_to_all | solution.py:469
  41.2 2.1 %backward_kernel.1 = (f32[16,192]{1,0:T(8,128)}, bf16[512,192]{1,0:T(8,128)(2,1)S(1)}, bf16[64,192]{1,0:T(8,128)(2,1)S(1)}, bf16[64,192]{1,0:T(8,128)(2,1)S(1)},...) custom-call(bf16[512,256]{1,0:T(8,128)(2,1)S(1)} %bitcast.24, bf16[576,1152]{1,0:T(8,128)(2,1)S(1)} %get-tuple-element.49.podd_ref, ...), custom_call_target="tpu_custom_call" | custom-call | tf_op jit(solution)/shard_map/backward_kernel/pallas_call | solution.py:402
  43.3 0.3 collective-permute-start.4
  43.6 1.8 %collective-permute-done.4.b_ref = bf16[2304,128]{1,0:T(8,128)(2,1)S(1)} collective-permute-done((bf16[2304,128]{1,0:T(8,128)(2,1)S(1)}, bf16[2304,128]{1,0:T(8,128)(2,1)S(1)}, u32[]{:S(2)}, u32[]{:S(2)}) %collective-permute-start.4) | collective-permute-done | bytes 589856 | tf_op jit(solution)/shard_map/ppermute | solution.py:480
  45.4 1.0 %add_kernel.1 = bf16[2560,128]{1,0:T(8,128)(2,1)} custom-call(f32[2304,128]{1,0:T(8,128)S(1)} %get-tuple-element.64.a_ref, bf16[2304,128]{1,0:T(8,128)(2,1)S(1)} %collective-permute-done.4.b_ref), custom_call_target="tpu_custom_call" | custom-call | tf_op jit(solution)/shard_map/add_kernel/pallas_call | solution.py:402
  46.3 6.7 %all-to-all-start.2 = ((bf16[64,40,128]{2,1,0:T(8,128)(2,1)}), bf16[64,40,128]{2,1,0:T(8,128)(2,1)S(1)}, u32[]{:S(2)}, u32[]{:S(2)}) async-start(bf16[64,40,128]{2,1,0:T(8,128)(2,1)} %bitcast.11), calls=%async_computation.2 | async-start | bytes 1310720 | tf_op jit(solution)/shard_map/all_to_all | solution.py:482
  53.0 2.6 %collective-permute-start.2 = (bf16[64,192]{1,0:T(8,128)(2,1)S(1)}, bf16[64,192]{1,0:T(8,128)(2,1)S(1)}, u32[]{:S(2)}, u32[]{:S(2)}) collective-permute-start(bf16[64,192]{1,0:T(8,128)(2,1)S(1)} %get-tuple-element.62), channel_id=1, source_target_pairs={{1,0},{2,1},{3,2},{4,3},{5,4},{6,5},{7,6},{9,8},{10,9},{11,10},{12... | collective-permute-start | bytes 73736 | tf_op jit(solution)/shard_map/ppermute | solution.py:419
  55.7 1.3 %collective-permute-start.3 = (bf16[64,192]{1,0:T(8,128)(2,1)S(1)}, bf16[64,192]{1,0:T(8,128)(2,1)S(1)}, u32[]{:S(2)}, u32[]{:S(2)}) collective-permute-start(bf16[64,192]{1,0:T(8,128)(2,1)S(1)} %get-tuple-element.63), channel_id=1, source_target_pairs={{8,0},{9,1},{10,2},{11,3},{12,4},{13,5},{14,6},{15,7},{16,8},{17,9... | collective-permute-start | bytes 73736 | tf_op jit(solution)/shard_map/ppermute | solution.py:419
  57.0 10.0 %all-to-all-done.2.recv_ref = bf16[64,40,128]{2,1,0:T(8,128)(2,1)S(1)} async-done(((bf16[64,40,128]{2,1,0:T(8,128)(2,1)}), bf16[64,40,128]{2,1,0:T(8,128)(2,1)S(1)}, u32[]{:S(2)}, u32[]{:S(2)}) %all-to-all-start.2) | async-done | bytes 655392 | tf_op jit(solution)/shard_map/all_to_all | solution.py:482
  66.9 1.0 %total_kernel.1 = bf16[64,40,128]{2,1,0:T(8,128)(2,1)} custom-call(bf16[64,40,128]{2,1,0:T(8,128)(2,1)S(1)} %all-to-all-done.2.recv_ref), custom_call_target="tpu_custom_call" | custom-call | tf_op jit(solution)/shard_map/total_kernel/pallas_call | solution.py:402
  67.9 4.6 %all-to-all-start.3 = ((bf16[64,40,128]{2,1,0:T(8,128)(2,1)}), bf16[64,40,128]{2,1,0:T(8,128)(2,1)S(1)}, u32[]{:S(2)}, u32[]{:S(2)}) async-start(bf16[64,40,128]{2,1,0:T(8,128)(2,1)} %total_kernel.1), calls=%async_computation.3 | async-start | bytes 1310720 | tf_op jit(solution)/shard_map/all_to_all | solution.py:488
  72.6 1.3 %collective-permute-start.5 = (bf16[16,192]{1,0:T(8,128)(2,1)S(1)}, bf16[16,192]{1,0:T(8,128)(2,1)S(1)}, u32[]{:S(2)}, u32[]{:S(2)}) collective-permute-start(bf16[16,192]{1,0:T(8,128)(2,1)S(1)} %slice.3), channel_id=1, source_target_pairs={{9,0},{10,1},{11,2},{12,3},{13,4},{14,5},{15,6},{17,8},{18,9},{19,... | collective-permute-start | bytes 18440 | tf_op jit(solution)/shard_map/ppermute | solution.py:419
  73.9 8.7 %collective-permute-done.5.xyr_ref = bf16[16,192]{1,0:T(8,128)(2,1)S(1)} collective-permute-done((bf16[16,192]{1,0:T(8,128)(2,1)S(1)}, bf16[16,192]{1,0:T(8,128)(2,1)S(1)}, u32[]{:S(2)}, u32[]{:S(2)}) %collective-permute-start.5) | collective-permute-done | bytes 6176 | tf_op jit(solution)/shard_map/ppermute | solution.py:419
  82.6 3.4 %spread_kernel.1 = bf16[8,96,512]{2,1,0:T(8,128)(2,1)} custom-call(s32[6,8]{1,0:T(8,128)S(1)} %copy-done.2, bf16[192,2592]{1,0:T(8,128)(2,1)S(1)} %bitcast.20, bf16[512,192]{1,0:T(8,128)(2,1)S(1)} %get-tuple-element.67.db_ref, bf16[64,192]{1,0:T(8,128)(2,1)S(1)} %collective-permute-done.2.xr_ref, bf16[64,192]{1,0:T(8,128)(2,1)S(1)} %collective-permute-done.3.yr_ref, ...), custom_call_target="tpu_custom_call" | custom-call | tf_op jit(solution)/shard_map/spread_kernel/pallas_call | solution.py:402
  86.0 2.4 %collective-permute-start.6 = (bf16[2560,128]{1,0:T(8,128)(2,1)S(1)}, bf16[2560,128]{1,0:T(8,128)(2,1)S(1)}, u32[]{:S(2)}, u32[]{:S(2)}) collective-permute-start(bf16[2560,128]{1,0:T(8,128)(2,1)S(1)} %bitcast.21), channel_id=1, source_target_pairs={{0,1},{1,0},{2,3},{3,2},{4,5},{5,4},{6,7},{7,6},{8,9},{9,8},{10,11... | collective-permute-start | bytes 1966088 | tf_op jit(solution)/shard_map/ppermute | solution.py:499
  88.3 1.7 %collective-permute-done.6.other_ref = bf16[2560,128]{1,0:T(8,128)(2,1)S(1)} collective-permute-done((bf16[2560,128]{1,0:T(8,128)(2,1)S(1)}, bf16[2560,128]{1,0:T(8,128)(2,1)S(1)}, u32[]{:S(2)}, u32[]{:S(2)}) %collective-permute-start.6) | collective-permute-done | bytes 655392 | tf_op jit(solution)/shard_map/ppermute | solution.py:499
  90.1 1.6 %final_kernel.1 = (f32[192,2592]{1,0:T(8,128)}, f32[192,192]{1,0:T(8,128)}, f32[192,192]{1,0:T(8,128)}, f32[8,192]{1,0:T(8,128)}, f32[1,192]{1,0:T(1,128)}) custom-call(bf16[2560,128]{1,0:T(8,128)(2,1)S(1)} %bitcast.22, bf16[2560,128]{1,0:T(8,128)(2,1)S(1)} %collective-permute-done.6.other_ref), custom_call_target="tpu_custom_call" | custom-call | tf_op jit(solution)/shard_map/final_kernel/pallas_call | solution.py:402
  (18 shorter events, 0.0 us)
Async XLA Ops:
  0.6 18.6 %copy-start.2 = (s32[6,8]{1,0:T(8,128)S(1)}, s32[6,8]{1,0:T(8,128)}, u32[]{:S(2)}) copy-start(s32[6,8]{1,0:T(8,128)} %near_ref.3) | copy-start | bytes 580
  0.6 18.6 %copy-start.4 = (s32[1,512,1]{1,2,0:T(1,128)S(1)}, s32[1,512,1]{1,2,0:T(1,128)}, u32[]{:S(2)}) copy-start(s32[1,512,1]{1,2,0:T(1,128)} %param.13) | copy-start | bytes 6148
  0.7 22.2 %copy-start.5 = (f32[192]{0:T(256)S(1)}, f32[192]{0:T(256)}, u32[]{:S(2)}) copy-start(f32[192]{0:T(256)} %param.16) | copy-start | bytes 2308
  3.1 19.7 %all-to-all-start = ((bf16[32,16,384]{2,1,0:T(8,128)(2,1)}), bf16[32,16,384]{2,1,0:T(8,128)(2,1)S(1)}, u32[]{:S(2)}, u32[]{:S(2)}) async-start(bf16[32,16,384]{2,1,0:T(8,128)(2,1)} %get-tuple-element.47), calls=%async_computation | async-start | bytes 786432 | tf_op jit(solution)/shard_map/all_to_all | solution.py:441
  12.6 9.2 %collective-permute-start = (bf16[256,128]{1,0:T(8,128)(2,1)S(1)}, bf16[256,128]{1,0:T(8,128)(2,1)S(1)}, u32[]{:S(2)}, u32[]{:S(2)}) collective-permute-start(bf16[256,128]{1,0:T(8,128)(2,1)S(1)} %get-tuple-element.43), channel_id=1, source_target_pairs={{0,1},{1,2},{2,3},{3,4},{4,5},{5,6},{6,7},{8,9},{9,10},{10,11},{11... | collective-permute-start | bytes 196616 | tf_op jit(solution)/shard_map/ppermute | solution.py:419
  16.1 5.6 %collective-permute-start.1 = (bf16[256,128]{1,0:T(8,128)(2,1)S(1)}, bf16[256,128]{1,0:T(8,128)(2,1)S(1)}, u32[]{:S(2)}, u32[]{:S(2)}) collective-permute-start(bf16[256,128]{1,0:T(8,128)(2,1)S(1)} %get-tuple-element.44), channel_id=1, source_target_pairs={{0,8},{1,9},{2,10},{3,11},{4,12},{5,13},{6,14},{7,15},{8,16},{9,17... | collective-permute-start | bytes 196616 | tf_op jit(solution)/shard_map/ppermute | solution.py:419
  22.8 18.4 %copy-start.3 = (f32[8,192]{1,0:T(8,128)S(1)}, f32[8,192]{1,0:T(8,128)}, u32[]{:S(2)}) copy-start(f32[8,192]{1,0:T(8,128)} %query_ref.1) | copy-start | bytes 18436
  43.3 2.0 %collective-permute-start.4 = (bf16[2304,128]{1,0:T(8,128)(2,1)S(1)}, bf16[2304,128]{1,0:T(8,128)(2,1)S(1)}, u32[]{:S(2)}, u32[]{:S(2)}) collective-permute-start(bf16[2304,128]{1,0:T(8,128)(2,1)S(1)} %get-tuple-element.65), channel_id=1, source_target_pairs={{0,1},{1,0},{2,3},{3,2},{4,5},{5,4},{6,7},{7,6},{8,9},{9,8},{10,11... | collective-permute-start | bytes 1769480 | tf_op jit(solution)/shard_map/ppermute | solution.py:480
  46.3 20.6 %all-to-all-start.2 = ((bf16[64,40,128]{2,1,0:T(8,128)(2,1)}), bf16[64,40,128]{2,1,0:T(8,128)(2,1)S(1)}, u32[]{:S(2)}, u32[]{:S(2)}) async-start(bf16[64,40,128]{2,1,0:T(8,128)(2,1)} %bitcast.11), calls=%async_computation.2 | async-start | bytes 1310720 | tf_op jit(solution)/shard_map/all_to_all | solution.py:482
  53.0 29.6 %copy-start = (bf16[2592,192]{0,1:T(8,128)(2,1)S(1)}, bf16[2592,192]{0,1:T(8,128)(2,1)}, u32[]{:S(2)}) copy-start(bf16[2592,192]{0,1:T(8,128)(2,1)} %param.15) | copy-start | bytes 2985988
  53.0 29.6 %copy-start.1 = (s32[1,8,512]{2,1,0:T(8,128)S(1)}, s32[1,8,512]{2,1,0:T(8,128)}, u32[]{:S(2)}) copy-start(s32[1,8,512]{2,1,0:T(8,128)} %param.11) | copy-start | bytes 49156
  53.0 14.9 %collective-permute-start.2 = (bf16[64,192]{1,0:T(8,128)(2,1)S(1)}, bf16[64,192]{1,0:T(8,128)(2,1)S(1)}, u32[]{:S(2)}, u32[]{:S(2)}) collective-permute-start(bf16[64,192]{1,0:T(8,128)(2,1)S(1)} %get-tuple-element.62), channel_id=1, source_target_pairs={{1,0},{2,1},{3,2},{4,3},{5,4},{6,5},{7,6},{9,8},{10,9},{11,10},{12... | collective-permute-start | bytes 73736 | tf_op jit(solution)/shard_map/ppermute | solution.py:419
  55.7 12.2 %collective-permute-start.3 = (bf16[64,192]{1,0:T(8,128)(2,1)S(1)}, bf16[64,192]{1,0:T(8,128)(2,1)S(1)}, u32[]{:S(2)}, u32[]{:S(2)}) collective-permute-start(bf16[64,192]{1,0:T(8,128)(2,1)S(1)} %get-tuple-element.63), channel_id=1, source_target_pairs={{8,0},{9,1},{10,2},{11,3},{12,4},{13,5},{14,6},{15,7},{16,8},{17,9... | collective-permute-start | bytes 73736 | tf_op jit(solution)/shard_map/ppermute | solution.py:419
  67.9 18.1 %all-to-all-start.3 = ((bf16[64,40,128]{2,1,0:T(8,128)(2,1)}), bf16[64,40,128]{2,1,0:T(8,128)(2,1)S(1)}, u32[]{:S(2)}, u32[]{:S(2)}) async-start(bf16[64,40,128]{2,1,0:T(8,128)(2,1)} %total_kernel.1), calls=%async_computation.3 | async-start | bytes 1310720 | tf_op jit(solution)/shard_map/all_to_all | solution.py:488
  72.6 10.0 %collective-permute-start.5 = (bf16[16,192]{1,0:T(8,128)(2,1)S(1)}, bf16[16,192]{1,0:T(8,128)(2,1)S(1)}, u32[]{:S(2)}, u32[]{:S(2)}) collective-permute-start(bf16[16,192]{1,0:T(8,128)(2,1)S(1)} %slice.3), channel_id=1, source_target_pairs={{9,0},{10,1},{11,2},{12,3},{13,4},{14,5},{15,6},{17,8},{18,9},{19,... | collective-permute-start | bytes 18440 | tf_op jit(solution)/shard_map/ppermute | solution.py:419
  86.0 4.1 %collective-permute-start.6 = (bf16[2560,128]{1,0:T(8,128)(2,1)S(1)}, bf16[2560,128]{1,0:T(8,128)(2,1)S(1)}, u32[]{:S(2)}, u32[]{:S(2)}) collective-permute-start(bf16[2560,128]{1,0:T(8,128)(2,1)S(1)} %bitcast.21), channel_id=1, source_target_pairs={{0,1},{1,0},{2,3},{3,2},{4,5},{5,4},{6,7},{7,6},{8,9},{9,8},{10,11... | collective-permute-start | bytes 1966088 | tf_op jit(solution)/shard_map/ppermute | solution.py:499
